TPU v7x, 512 devices: a whole 4x4x16 slice. The times are simulated.
512 devices in a mesh: seq: 32 (over z, x_hi), chan: 16 (over x_lo, y, core).
Axes of the slice: x: 4 (x_hi: 2, x_lo: 2; x = x_hi * 2 + x_lo), y: 4, z: 16, core: 2. Of those that a mesh axis runs over, the one named last changes fastest.
Arguments:
- query: bfloat16 [32, 16, 8192], P('chan', None, 'seq'), may hold values from -6 to 6
- key_in: bfloat16 [32, 16, 8192], P('chan', None, 'seq'), may hold values from -6 to 6
- value: bfloat16 [32, 16, 8192], P('chan', None, 'seq'), may hold values from -6 to 6
- grad_out: bfloat16 [32, 16, 8192], P('chan', None, 'seq'), may hold values from -6 to 6
- filters: float32 [16, 8192], P(None, 'seq'), may hold values from -2 to 2
- skip: float32 [32, 16], P('chan'), may hold values from 0.5 to 1.5
Outputs:
- query_grad: bfloat16 [32, 16, 8192], P('chan', None, 'seq')
- key_grad: bfloat16 [32, 16, 8192], P('chan', None, 'seq')
- value_grad: bfloat16 [32, 16, 8192], P('chan', None, 'seq')
- filter_grad: float32 [16, 8192], P('chan', 'seq')
All inputs are finite; a program needn't handle non-finite values.
Results may differ from a plain program's by a relative error of at most 0.0028.
Values sent between devices are 32-bit elements; how exact they have to be, the bound alone decides.
No kernel may reach another device: no remote copies, remote signals or barrier semaphores. Data moves between devices by JAX's collectives and lax.ppermute only.
A program may use at most 64 MiB of HBM per device.

v0:
```python
import math

import jax
import jax.numpy as jnp
from jax import lax
from jax.sharding import PartitionSpec as P

HIGHEST = lax.Precision.HIGHEST


def angle_table(row_count, col_count, period):
    product = (
        jnp.arange(row_count, dtype=jnp.int32)[:, None]
        * jnp.arange(col_count, dtype=jnp.int32)[None, :]
        % period
    )
    return 2.0 * math.pi / period * product.astype(jnp.float32)


def freq_order(part_count):
    first = jnp.arange(part_count, dtype=jnp.int32)
    second = jnp.where(first == 0, part_count, 2 * part_count - first)
    return jnp.stack([first, second], axis=1).reshape(-1)


def split_size(length):
    chosen = 1
    divisor = 1
    while divisor * divisor <= length:
        if length % divisor == 0:
            chosen = divisor
        divisor += 1
    return chosen


def mix_einsum(pattern, left_re, left_im, table_re, table_im):
    real_part = jnp.einsum(pattern, left_re, table_re, precision=HIGHEST) - jnp.einsum(
        pattern, left_im, table_im, precision=HIGHEST
    )
    imag_part = jnp.einsum(pattern, left_re, table_im, precision=HIGHEST) + jnp.einsum(
        pattern, left_im, table_re, precision=HIGHEST
    )
    return (real_part, imag_part)


def twist_angles(part_count, block_width, offset, full_length):
    positions = offset * block_width + jnp.arange(block_width, dtype=jnp.int32)
    product = freq_order(part_count)[:, None] * positions[None, :] % full_length
    return 2.0 * math.pi / full_length * product.astype(jnp.float32)


def across_forward(values, offset, full_length):
    part_count = values.shape[1]
    block_width = values.shape[2]
    product = (
        jnp.arange(part_count, dtype=jnp.int32)[:, None]
        * freq_order(part_count)[None, :]
        % (2 * part_count)
    )
    angles = 2.0 * math.pi / (2 * part_count) * product.astype(jnp.float32)
    spec_re = jnp.einsum("rpm,pk->rkm", values, jnp.cos(angles), precision=HIGHEST)
    spec_im = -jnp.einsum("rpm,pk->rkm", values, jnp.sin(angles), precision=HIGHEST)
    twist = twist_angles(part_count, block_width, offset, full_length)
    twist_re = jnp.cos(twist)
    twist_im = -jnp.sin(twist)
    return (spec_re * twist_re - spec_im * twist_im, spec_re * twist_im + spec_im * twist_re)


def across_inverse(spec_re, spec_im, offset, full_length):
    part_twice = spec_re.shape[1]
    part_count = part_twice // 2
    block_width = spec_re.shape[2]
    twist = twist_angles(part_count, block_width, offset, full_length)
    twist_re = jnp.cos(twist)
    twist_im = jnp.sin(twist)
    turned_re = spec_re * twist_re - spec_im * twist_im
    turned_im = spec_re * twist_im + spec_im * twist_re
    product = (
        freq_order(part_count)[:, None]
        * jnp.arange(part_count, dtype=jnp.int32)[None, :]
        % part_twice
    )
    angles = 2.0 * math.pi / part_twice * product.astype(jnp.float32)
    values = jnp.einsum("rkm,kp->rpm", turned_re, jnp.cos(angles), precision=HIGHEST)
    values = values - jnp.einsum("rkm,kp->rpm", turned_im, jnp.sin(angles), precision=HIGHEST)
    return values * (1.0 / full_length)


def local_forward(spec_re, spec_im):
    row_count, pair_count, length = spec_re.shape
    outer_size = split_size(length)
    inner_size = length // outer_size
    spec_re = spec_re.reshape(row_count, pair_count, outer_size, inner_size)
    spec_im = spec_im.reshape(row_count, pair_count, outer_size, inner_size)
    outer_angles = angle_table(outer_size, outer_size, outer_size)
    step_re, step_im = mix_einsum(
        "rtab,ac->rtcb", spec_re, spec_im, jnp.cos(outer_angles), -jnp.sin(outer_angles)
    )
    twist = angle_table(outer_size, inner_size, length)
    twist_re = jnp.cos(twist)
    twist_im = -jnp.sin(twist)
    step_re, step_im = (
        step_re * twist_re - step_im * twist_im,
        step_re * twist_im + step_im * twist_re,
    )
    inner_angles = angle_table(inner_size, inner_size, inner_size)
    final_re, final_im = mix_einsum(
        "rtcb,bd->rtdc", step_re, step_im, jnp.cos(inner_angles), -jnp.sin(inner_angles)
    )
    return (
        final_re.reshape(row_count, pair_count, length),
        final_im.reshape(row_count, pair_count, length),
    )


def local_inverse(spec_re, spec_im):
    row_count, pair_count, length = spec_re.shape
    outer_size = split_size(length)
    inner_size = length // outer_size
    spec_re = spec_re.reshape(row_count, pair_count, inner_size, outer_size)
    spec_im = spec_im.reshape(row_count, pair_count, inner_size, outer_size)
    inner_angles = angle_table(inner_size, inner_size, inner_size)
    step_re, step_im = mix_einsum(
        "rtdc,db->rtcb", spec_re, spec_im, jnp.cos(inner_angles), jnp.sin(inner_angles)
    )
    twist = angle_table(outer_size, inner_size, length)
    twist_re = jnp.cos(twist)
    twist_im = jnp.sin(twist)
    step_re, step_im = (
        step_re * twist_re - step_im * twist_im,
        step_re * twist_im + step_im * twist_re,
    )
    outer_angles = angle_table(outer_size, outer_size, outer_size)
    final_re, final_im = mix_einsum(
        "rtcb,ca->rtab", step_re, step_im, jnp.cos(outer_angles), jnp.sin(outer_angles)
    )
    return (
        final_re.reshape(row_count, pair_count, length),
        final_im.reshape(row_count, pair_count, length),
    )


def local(query, key_in, value, grad_out, filters, skip):
    seq_count = lax.axis_size("seq")
    seq_pos = lax.axis_index("seq")
    chan_count = lax.axis_size("chan")
    slot_count, groups, length = query.shape
    row_count = slot_count * groups
    full_length = 2 * seq_count * length
    query_f = query.astype(jnp.float32)
    key_f = key_in.astype(jnp.float32)
    cotangent = grad_out.astype(jnp.float32)
    gated_input = (query_f * key_f).reshape(row_count, 1, length)
    signal = (cotangent * value.astype(jnp.float32)).reshape(row_count, 1, length)
    filter_rows = filters
    filter_rows = filter_rows.reshape(filter_rows.shape[0], 1, length)
    spread_gated, spread_signal, spread_filter = (
        lax.all_to_all(gated_input, "seq", split_axis=2, concat_axis=1, tiled=True),
        lax.all_to_all(signal, "seq", split_axis=2, concat_axis=1, tiled=True),
        lax.all_to_all(filter_rows, "seq", split_axis=2, concat_axis=1, tiled=True),
    )
    gated_re, gated_im = across_forward(spread_gated, seq_pos, full_length)
    signal_re, signal_im = across_forward(spread_signal, seq_pos, full_length)
    filter_re, filter_im = across_forward(spread_filter, seq_pos, full_length)
    mixed_out = (
        lax.all_to_all(gated_re, "seq", split_axis=1, concat_axis=2, tiled=True),
        lax.all_to_all(gated_im, "seq", split_axis=1, concat_axis=2, tiled=True),
        lax.all_to_all(signal_re, "seq", split_axis=1, concat_axis=2, tiled=True),
        lax.all_to_all(signal_im, "seq", split_axis=1, concat_axis=2, tiled=True),
        lax.all_to_all(filter_re, "seq", split_axis=1, concat_axis=2, tiled=True),
        lax.all_to_all(filter_im, "seq", split_axis=1, concat_axis=2, tiled=True),
    )
    gated_re, gated_im = local_forward(mixed_out[0], mixed_out[1])
    signal_re, signal_im = local_forward(mixed_out[2], mixed_out[3])
    filter_re, filter_im = local_forward(mixed_out[4], mixed_out[5])
    pair_count = gated_re.shape[1]
    gated_re = gated_re.reshape(slot_count, groups, pair_count, length)
    gated_im = gated_im.reshape(slot_count, groups, pair_count, length)
    signal_re = signal_re.reshape(slot_count, groups, pair_count, length)
    signal_im = signal_im.reshape(slot_count, groups, pair_count, length)
    conv_re = filter_re * gated_re - filter_im * gated_im
    conv_im = filter_re * gated_im + filter_im * gated_re
    corr_re = filter_re * signal_re + filter_im * signal_im
    corr_im = filter_re * signal_im - filter_im * signal_re
    cross_re = jnp.sum(gated_re * signal_re + gated_im * signal_im, axis=0)
    cross_im = jnp.sum(gated_re * signal_im - gated_im * signal_re, axis=0)
    cross_re, cross_im = (
        lax.psum_scatter(cross_re, "chan", scatter_dimension=0, tiled=True),
        lax.psum_scatter(cross_im, "chan", scatter_dimension=0, tiled=True),
    )
    cross_re, cross_im = local_inverse(cross_re, cross_im)
    conv_re, conv_im = local_inverse(
        conv_re.reshape(row_count, pair_count, length),
        conv_im.reshape(row_count, pair_count, length),
    )
    corr_re, corr_im = local_inverse(
        corr_re.reshape(row_count, pair_count, length),
        corr_im.reshape(row_count, pair_count, length),
    )
    returned = (
        lax.all_to_all(conv_re, "seq", split_axis=2, concat_axis=1, tiled=True),
        lax.all_to_all(conv_im, "seq", split_axis=2, concat_axis=1, tiled=True),
        lax.all_to_all(corr_re, "seq", split_axis=2, concat_axis=1, tiled=True),
        lax.all_to_all(corr_im, "seq", split_axis=2, concat_axis=1, tiled=True),
        lax.all_to_all(cross_re, "seq", split_axis=2, concat_axis=1, tiled=True),
        lax.all_to_all(cross_im, "seq", split_axis=2, concat_axis=1, tiled=True),
    )
    conv = across_inverse(returned[0], returned[1], seq_pos, full_length)
    corr = across_inverse(returned[2], returned[3], seq_pos, full_length)
    lagged = across_inverse(returned[4], returned[5], seq_pos, full_length)
    skip_gain = skip.reshape(row_count, 1, 1)
    out_field = conv + skip_gain * spread_gated
    adjoint = corr + skip_gain * spread_signal
    lagged = lagged * (1.0 / math.sqrt(slot_count * chan_count * seq_count * length))
    out_field, adjoint, lagged = (
        lax.all_to_all(out_field, "seq", split_axis=1, concat_axis=2, tiled=True),
        lax.all_to_all(adjoint, "seq", split_axis=1, concat_axis=2, tiled=True),
        lax.all_to_all(lagged, "seq", split_axis=1, concat_axis=2, tiled=True),
    )
    out_field = out_field.reshape(slot_count, groups, length)
    adjoint = adjoint.reshape(slot_count, groups, length)
    lagged = lagged.reshape(lagged.shape[0], length)
    query_grad = (adjoint * key_f).astype(jnp.bfloat16)
    key_grad = (adjoint * query_f).astype(jnp.bfloat16)
    value_grad = (cotangent * out_field).astype(jnp.bfloat16)
    return (query_grad, key_grad, value_grad, lagged)


def solution(mesh):
    return jax.shard_map(
        local,
        mesh=mesh,
        in_specs=(
            P("chan", None, "seq"),
            P("chan", None, "seq"),
            P("chan", None, "seq"),
            P("chan", None, "seq"),
            P(None, "seq"),
            P("chan", None),
        ),
        out_specs=(
            P("chan", None, "seq"),
            P("chan", None, "seq"),
            P("chan", None, "seq"),
            P("chan", "seq"),
        ),
        check_vma=False,
    )
```

profile of v0, /device:TPU:24, one launch (start us, length us, event | category | flops | bytes accessed | tf_op | source)
XLA Modules:
  0.0 528.8 jit_solution(15366661442410568456)
XLA Ops:
  8.5 1.0 reduce.12
  10.2 17.9 %all-to-all-start = ((f32[32,1,128]{2,1,0:T(1,128)}), f32[32,1,128]{2,1,0:T(1,128)S(1)}, u32[]{:S(2)}, u32[]{:S(2)}) async-start(f32[32,1,128]{2,1,0:T(1,128)} %reshape.418), calls=%async_computation | async-start | bytes 32768 | tf_op jit(solution)/shard_map/all_to_all | solution.py:160
  29.3 1.0 reduce.6
  31.1 1.0 reduce.4
  33.1 1.3 dynamic-slice
  34.4 8.4 %all-to-all-done = f32[32,1,128]{2,1,0:T(1,128)S(1)} async-done(((f32[32,1,128]{2,1,0:T(1,128)}), f32[32,1,128]{2,1,0:T(1,128)S(1)}, u32[]{:S(2)}, u32[]{:S(2)}) %all-to-all-start) | async-done | bytes 16416 | tf_op jit(solution)/shard_map/all_to_all | solution.py:160
  42.8 6.2 %all-to-all-start.9 = ((f32[32,1,256]{2,1,0:T(1,128)}), f32[32,1,256]{2,1,0:T(1,128)S(1)}, u32[]{:S(2)}, u32[]{:S(2)}) async-start(f32[32,1,256]{2,1,0:T(1,128)} %reshape.436), calls=%async_computation.9 | async-start | bytes 65536 | tf_op jit(solution)/shard_map/all_to_all | solution.py:158
  52.4 11.5 %all-to-all-done.9 = f32[32,1,256]{2,1,0:T(1,128)S(1)} async-done(((f32[32,1,256]{2,1,0:T(1,128)}), f32[32,1,256]{2,1,0:T(1,128)S(1)}, u32[]{:S(2)}, u32[]{:S(2)}) %all-to-all-start.9) | async-done | bytes 32800 | tf_op jit(solution)/shard_map/all_to_all | solution.py:158
  63.9 3.9 all-to-all-start.3
  69.5 13.1 %all-to-all-done.3 = f32[32,1,256]{2,1,0:T(1,128)S(1)} async-done(((f32[32,1,256]{2,1,0:T(1,128)}), f32[32,1,256]{2,1,0:T(1,128)S(1)}, u32[]{:S(2)}, u32[]{:S(2)}) %all-to-all-start.3) | async-done | bytes 32800 | tf_op jit(solution)/shard_map/all_to_all | solution.py:159
  82.6 3.8 all-to-all-start.1
  92.0 9.3 %all-to-all-done.1 = f32[32,1,256]{2,1,0:T(1,128)S(1)} async-done(((f32[32,1,256]{2,1,0:T(1,128)}), f32[32,1,256]{2,1,0:T(1,128)S(1)}, u32[]{:S(2)}, u32[]{:S(2)}) %all-to-all-start.1) | async-done | bytes 32800 | tf_op jit(solution)/shard_map/all_to_all | solution.py:170
  101.3 5.3 all-to-all-start.2
  108.6 12.9 %all-to-all-done.2 = f32[32,1,256]{2,1,0:T(1,128)S(1)} async-done(((f32[32,1,256]{2,1,0:T(1,128)}), f32[32,1,256]{2,1,0:T(1,128)S(1)}, u32[]{:S(2)}, u32[]{:S(2)}) %all-to-all-start.2) | async-done | bytes 32800 | tf_op jit(solution)/shard_map/all_to_all | solution.py:171
  121.5 4.0 all-to-all-start.10
  127.5 2.0 fusion.28
  129.5 2.0 fusion.9
  131.4 9.2 %all-to-all-done.10 = f32[32,1,512]{2,1,0:T(1,128)S(1)} async-done(((f32[32,1,512]{2,1,0:T(1,128)}), f32[32,1,512]{2,1,0:T(1,128)S(1)}, u32[]{:S(2)}, u32[]{:S(2)}) %all-to-all-start.10) | async-done | bytes 65568 | tf_op jit(solution)/shard_map/all_to_all | solution.py:166
  140.7 5.5 %all-to-all-start.4 = ((f32[32,1,512]{2,1,0:T(1,128)}), f32[32,1,512]{2,1,0:T(1,128)S(1)}, u32[]{:S(2)}, u32[]{:S(2)}) async-start(f32[32,1,512]{2,1,0:T(1,128)} %reshape.426), calls=%async_computation.4 | async-start | bytes 131072 | tf_op jit(solution)/shard_map/all_to_all | solution.py:168
  146.1 2.0 fusion.26
  148.8 2.0 fusion.7
  152.4 9.0 %all-to-all-done.4 = f32[32,1,512]{2,1,0:T(1,128)S(1)} async-done(((f32[32,1,512]{2,1,0:T(1,128)}), f32[32,1,512]{2,1,0:T(1,128)S(1)}, u32[]{:S(2)}, u32[]{:S(2)}) %all-to-all-start.4) | async-done | bytes 65568 | tf_op jit(solution)/shard_map/all_to_all | solution.py:168
  161.4 5.6 %all-to-all-start.5 = ((f32[32,1,512]{2,1,0:T(1,128)}), f32[32,1,512]{2,1,0:T(1,128)S(1)}, u32[]{:S(2)}, u32[]{:S(2)}) async-start(f32[32,1,512]{2,1,0:T(1,128)} %reshape.428), calls=%async_computation.5 | async-start | bytes 131072 | tf_op jit(solution)/shard_map/all_to_all | solution.py:169
  168.8 13.4 %all-to-all-done.5 = f32[32,1,512]{2,1,0:T(1,128)S(1)} async-done(((f32[32,1,512]{2,1,0:T(1,128)}), f32[32,1,512]{2,1,0:T(1,128)S(1)}, u32[]{:S(2)}, u32[]{:S(2)}) %all-to-all-start.5) | async-done | bytes 65568 | tf_op jit(solution)/shard_map/all_to_all | solution.py:169
  182.2 3.8 all-to-all-start.11
  188.1 13.3 %all-to-all-done.11 = f32[32,1,512]{2,1,0:T(1,128)S(1)} async-done(((f32[32,1,512]{2,1,0:T(1,128)}), f32[32,1,512]{2,1,0:T(1,128)S(1)}, u32[]{:S(2)}, u32[]{:S(2)}) %all-to-all-start.11) | async-done | bytes 65568 | tf_op jit(solution)/shard_map/all_to_all | solution.py:167
  213.5 107.7 %all-reduce.5.cloned.1.call-done = (f32[16,2,256]{2,1,0:T(2,128)}, f32[16,2,256]{2,1,0:T(2,128)}) async-done(((f32[16,2,256]{2,1,0:T(2,128)}, f32[16,2,256]{2,1,0:T(2,128)}), (f32[16,2,256]{2,1,0:T(2,128)}, f32[16,2,256]{2,1,0:T(2,128)})) %all-reduce.5.cloned.1.call-update) | async-done | bytes 65552
  321.1 1.3 constant_dynamic-slice_fusion.1
  322.9 1.3 constant_dynamic-slice_fusion
  326.2 15.0 %all-to-all-start.15 = ((f32[1,2,256]{1,0,2:T(1,128)}), f32[1,2,256]{1,0,2:T(1,128)S(1)}, u32[]{:S(2)}, u32[]{:S(2)}) async-start(f32[1,2,256]{1,0,2:T(1,128)} %bitcast.85), calls=%async_computation.15 | async-start | bytes 262144 | tf_op jit(solution)/shard_map/all_to_all | solution.py:205
  342.2 14.9 %all-to-all-done.15 = f32[1,2,256]{1,0,2:T(1,128)S(1)} async-done(((f32[1,2,256]{1,0,2:T(1,128)}), f32[1,2,256]{1,0,2:T(1,128)S(1)}, u32[]{:S(2)}, u32[]{:S(2)}) %all-to-all-start.15) | async-done | bytes 2080 | tf_op jit(solution)/shard_map/all_to_all | solution.py:205
  357.1 6.3 %all-to-all-start.16 = ((f32[1,2,256]{1,0,2:T(1,128)}), f32[1,2,256]{1,0,2:T(1,128)S(1)}, u32[]{:S(2)}, u32[]{:S(2)}) async-start(f32[1,2,256]{1,0,2:T(1,128)} %bitcast.91), calls=%async_computation.16 | async-start | bytes 262144 | tf_op jit(solution)/shard_map/all_to_all | solution.py:206
  364.3 16.7 %all-to-all-done.16 = f32[1,2,256]{1,0,2:T(1,128)S(1)} async-done(((f32[1,2,256]{1,0,2:T(1,128)}), f32[1,2,256]{1,0,2:T(1,128)S(1)}, u32[]{:S(2)}, u32[]{:S(2)}) %all-to-all-start.16) | async-done | bytes 2080 | tf_op jit(solution)/shard_map/all_to_all | solution.py:206
  382.6 4.5 all-to-all-start.17
  387.8 0.9 reshape.432
  388.7 13.0 %all-to-all-done.17 = f32[1,32,8]{2,0,1:T(1,128)S(1)} async-done(((f32[1,32,8]{2,0,1:T(1,128)}), f32[1,32,8]{2,0,1:T(1,128)S(1)}, u32[]{:S(2)}, u32[]{:S(2)}) %all-to-all-start.17) | async-done | bytes 1056 | tf_op jit(solution)/shard_map/all_to_all | solution.py:218
  401.7 3.9 all-to-all-start.6
  407.6 13.1 %all-to-all-done.6 = f32[32,1,512]{2,1,0:T(1,128)S(1)} async-done(((f32[32,1,512]{2,1,0:T(1,128)}), f32[32,1,512]{2,1,0:T(1,128)S(1)}, u32[]{:S(2)}, u32[]{:S(2)}) %all-to-all-start.6) | async-done | bytes 65568 | tf_op jit(solution)/shard_map/all_to_all | solution.py:203
  420.8 3.8 all-to-all-start.7
  426.6 13.2 %all-to-all-done.7 = f32[32,1,512]{2,1,0:T(1,128)S(1)} async-done(((f32[32,1,512]{2,1,0:T(1,128)}), f32[32,1,512]{2,1,0:T(1,128)S(1)}, u32[]{:S(2)}, u32[]{:S(2)}) %all-to-all-start.7) | async-done | bytes 65568 | tf_op jit(solution)/shard_map/all_to_all | solution.py:204
  439.8 3.9 all-to-all-start.12
  445.7 13.1 %all-to-all-done.12 = f32[32,1,512]{2,1,0:T(1,128)S(1)} async-done(((f32[32,1,512]{2,1,0:T(1,128)}), f32[32,1,512]{2,1,0:T(1,128)S(1)}, u32[]{:S(2)}, u32[]{:S(2)}) %all-to-all-start.12) | async-done | bytes 65568 | tf_op jit(solution)/shard_map/all_to_all | solution.py:201
  458.8 3.8 all-to-all-start.13
  468.7 9.1 %all-to-all-done.13 = f32[32,1,512]{2,1,0:T(1,128)S(1)} async-done(((f32[32,1,512]{2,1,0:T(1,128)}), f32[32,1,512]{2,1,0:T(1,128)S(1)}, u32[]{:S(2)}, u32[]{:S(2)}) %all-to-all-start.13) | async-done | bytes 65568 | tf_op jit(solution)/shard_map/all_to_all | solution.py:202
  480.7 5.4 %all-to-all-start.14 = ((f32[32,1,256]{2,1,0:T(1,128)}), f32[32,1,256]{2,1,0:T(1,128)S(1)}, u32[]{:S(2)}, u32[]{:S(2)}) async-start(f32[32,1,256]{2,1,0:T(1,128)} %reshape.446), calls=%async_computation.14 | async-start | bytes 65536 | tf_op jit(solution)/shard_map/all_to_all | solution.py:216
  487.8 13.3 %all-to-all-done.14 = f32[32,1,256]{2,1,0:T(1,128)S(1)} async-done(((f32[32,1,256]{2,1,0:T(1,128)}), f32[32,1,256]{2,1,0:T(1,128)S(1)}, u32[]{:S(2)}, u32[]{:S(2)}) %all-to-all-start.14) | async-done | bytes 32800 | tf_op jit(solution)/shard_map/all_to_all | solution.py:216
  501.1 3.9 all-to-all-start.8
  506.7 13.1 %all-to-all-done.8 = f32[32,1,256]{2,1,0:T(1,128)S(1)} async-done(((f32[32,1,256]{2,1,0:T(1,128)}), f32[32,1,256]{2,1,0:T(1,128)S(1)}, u32[]{:S(2)}, u32[]{:S(2)}) %all-to-all-start.8) | async-done | bytes 32800 | tf_op jit(solution)/shard_map/all_to_all | solution.py:217
  (205 shorter events, 63.6 us)
Async XLA Ops:
  10.2 32.6 %all-to-all-start = ((f32[32,1,128]{2,1,0:T(1,128)}), f32[32,1,128]{2,1,0:T(1,128)S(1)}, u32[]{:S(2)}, u32[]{:S(2)}) async-start(f32[32,1,128]{2,1,0:T(1,128)} %reshape.418), calls=%async_computation | async-start | bytes 32768 | tf_op jit(solution)/shard_map/all_to_all | solution.py:160
  28.5 0.7 copy-start
  28.5 0.7 copy-start.3
  30.3 0.7 copy-start.1
  30.3 0.7 copy-start.2
  42.8 21.1 %all-to-all-start.9 = ((f32[32,1,256]{2,1,0:T(1,128)}), f32[32,1,256]{2,1,0:T(1,128)S(1)}, u32[]{:S(2)}, u32[]{:S(2)}) async-start(f32[32,1,256]{2,1,0:T(1,128)} %reshape.436), calls=%async_computation.9 | async-start | bytes 65536 | tf_op jit(solution)/shard_map/all_to_all | solution.py:158
  63.9 18.7 %all-to-all-start.3 = ((f32[32,1,256]{2,1,0:T(1,128)}), f32[32,1,256]{2,1,0:T(1,128)S(1)}, u32[]{:S(2)}, u32[]{:S(2)}) async-start(f32[32,1,256]{2,1,0:T(1,128)} %reshape.424), calls=%async_computation.3 | async-start | bytes 65536 | tf_op jit(solution)/shard_map/all_to_all | solution.py:159
  82.6 18.7 %all-to-all-start.1 = ((f32[32,1,256]{2,1,0:T(1,128)}), f32[32,1,256]{2,1,0:T(1,128)S(1)}, u32[]{:S(2)}, u32[]{:S(2)}) async-start(f32[32,1,256]{2,1,0:T(1,128)} %reshape.420), calls=%async_computation.1 | async-start | bytes 65536 | tf_op jit(solution)/shard_map/all_to_all | solution.py:170
  101.3 20.2 %all-to-all-start.2 = ((f32[32,1,256]{2,1,0:T(1,128)}), f32[32,1,256]{2,1,0:T(1,128)S(1)}, u32[]{:S(2)}, u32[]{:S(2)}) async-start(f32[32,1,256]{2,1,0:T(1,128)} %reshape.422), calls=%async_computation.2 | async-start | bytes 65536 | tf_op jit(solution)/shard_map/all_to_all | solution.py:171
  121.5 19.2 %all-to-all-start.10 = ((f32[32,1,512]{2,1,0:T(1,128)}), f32[32,1,512]{2,1,0:T(1,128)S(1)}, u32[]{:S(2)}, u32[]{:S(2)}) async-start(f32[32,1,512]{2,1,0:T(1,128)} %reshape.438), calls=%async_computation.10 | async-start | bytes 131072 | tf_op jit(solution)/shard_map/all_to_all | solution.py:166
  140.7 20.7 %all-to-all-start.4 = ((f32[32,1,512]{2,1,0:T(1,128)}), f32[32,1,512]{2,1,0:T(1,128)S(1)}, u32[]{:S(2)}, u32[]{:S(2)}) async-start(f32[32,1,512]{2,1,0:T(1,128)} %reshape.426), calls=%async_computation.4 | async-start | bytes 131072 | tf_op jit(solution)/shard_map/all_to_all | solution.py:168
  161.4 20.9 %all-to-all-start.5 = ((f32[32,1,512]{2,1,0:T(1,128)}), f32[32,1,512]{2,1,0:T(1,128)S(1)}, u32[]{:S(2)}, u32[]{:S(2)}) async-start(f32[32,1,512]{2,1,0:T(1,128)} %reshape.428), calls=%async_computation.5 | async-start | bytes 131072 | tf_op jit(solution)/shard_map/all_to_all | solution.py:169
  182.2 19.2 %all-to-all-start.11 = ((f32[32,1,512]{2,1,0:T(1,128)}), f32[32,1,512]{2,1,0:T(1,128)S(1)}, u32[]{:S(2)}, u32[]{:S(2)}) async-start(f32[32,1,512]{2,1,0:T(1,128)} %reshape.440), calls=%async_computation.11 | async-start | bytes 131072 | tf_op jit(solution)/shard_map/all_to_all | solution.py:167
  186.1 135.1 %all-reduce.5.cloned.1.call-start = ((), (), s32[]{:S(2)}) async-start(), calls=%async_computation.18 | async-start | bytes 131072
  326.2 30.9 %all-to-all-start.15 = ((f32[1,2,256]{1,0,2:T(1,128)}), f32[1,2,256]{1,0,2:T(1,128)S(1)}, u32[]{:S(2)}, u32[]{:S(2)}) async-start(f32[1,2,256]{1,0,2:T(1,128)} %bitcast.85), calls=%async_computation.15 | async-start | bytes 262144 | tf_op jit(solution)/shard_map/all_to_all | solution.py:205
  357.1 23.9 %all-to-all-start.16 = ((f32[1,2,256]{1,0,2:T(1,128)}), f32[1,2,256]{1,0,2:T(1,128)S(1)}, u32[]{:S(2)}, u32[]{:S(2)}) async-start(f32[1,2,256]{1,0,2:T(1,128)} %bitcast.91), calls=%async_computation.16 | async-start | bytes 262144 | tf_op jit(solution)/shard_map/all_to_all | solution.py:206
  382.6 19.1 %all-to-all-start.17 = ((f32[1,32,8]{2,0,1:T(1,128)}), f32[1,32,8]{2,0,1:T(1,128)S(1)}, u32[]{:S(2)}, u32[]{:S(2)}) async-start(f32[1,32,8]{2,0,1:T(1,128)} %copy.487), calls=%async_computation.17 | async-start | bytes 32768 | tf_op jit(solution)/shard_map/all_to_all | solution.py:218
  401.7 19.0 %all-to-all-start.6 = ((f32[32,1,512]{2,1,0:T(1,128)}), f32[32,1,512]{2,1,0:T(1,128)S(1)}, u32[]{:S(2)}, u32[]{:S(2)}) async-start(f32[32,1,512]{2,1,0:T(1,128)} %reshape.432), calls=%async_computation.6 | async-start | bytes 131072 | tf_op jit(solution)/shard_map/all_to_all | solution.py:203
  420.8 19.0 %all-to-all-start.7 = ((f32[32,1,512]{2,1,0:T(1,128)}), f32[32,1,512]{2,1,0:T(1,128)S(1)}, u32[]{:S(2)}, u32[]{:S(2)}) async-start(f32[32,1,512]{2,1,0:T(1,128)} %reshape.430), calls=%async_computation.7 | async-start | bytes 131072 | tf_op jit(solution)/shard_map/all_to_all | solution.py:204
  439.8 19.0 %all-to-all-start.12 = ((f32[32,1,512]{2,1,0:T(1,128)}), f32[32,1,512]{2,1,0:T(1,128)S(1)}, u32[]{:S(2)}, u32[]{:S(2)}) async-start(f32[32,1,512]{2,1,0:T(1,128)} %reshape.444), calls=%async_computation.12 | async-start | bytes 131072 | tf_op jit(solution)/shard_map/all_to_all | solution.py:201
  458.8 19.0 %all-to-all-start.13 = ((f32[32,1,512]{2,1,0:T(1,128)}), f32[32,1,512]{2,1,0:T(1,128)S(1)}, u32[]{:S(2)}, u32[]{:S(2)}) async-start(f32[32,1,512]{2,1,0:T(1,128)} %reshape.442), calls=%async_computation.13 | async-start | bytes 131072 | tf_op jit(solution)/shard_map/all_to_all | solution.py:202
  462.8 0.7 copy-start.4
  480.7 20.4 %all-to-all-start.14 = ((f32[32,1,256]{2,1,0:T(1,128)}), f32[32,1,256]{2,1,0:T(1,128)S(1)}, u32[]{:S(2)}, u32[]{:S(2)}) async-start(f32[32,1,256]{2,1,0:T(1,128)} %reshape.446), calls=%async_computation.14 | async-start | bytes 65536 | tf_op jit(solution)/shard_map/all_to_all | solution.py:216
  501.1 18.7 %all-to-all-start.8 = ((f32[32,1,256]{2,1,0:T(1,128)}), f32[32,1,256]{2,1,0:T(1,128)S(1)}, u32[]{:S(2)}, u32[]{:S(2)}) async-start(f32[32,1,256]{2,1,0:T(1,128)} %reshape.434), calls=%async_computation.8 | async-start | bytes 65536 | tf_op jit(solution)/shard_map/all_to_all | solution.py:217
Sparse Core Ops, SparseCore 0:
  212.7 108.4 all-reduce.4
where the time goes:
time: 537 us; the launch traced here: 529 us
  waiting for transfers between devices  327 us (61%)
  starting transfers between devices  107 us (20%)
  local copies, waits for them, and re-layouts  33.2 us (6%)
  matrix products  28.8 us (5%)
  other arithmetic  16.8 us (3%)
  between operations  15.8 us (3%)
    unnamed x2, waiting for transfers between devices  108 us
    unnamed x45, local copies, waits for them, and re-layouts  20.7 us
    all_to_all x1, starting transfers between devices, local(): lax.all_to_all(filter_rows, 'seq', split_axis=2, concat_axis=1, tiled=True)  17.9 us
    all_to_all x1, waiting for transfers between devices, local(): lax.all_to_all(cross_im, 'seq', split_axis=2, concat_axis=1, tiled=True)  16.7 us
    all_to_all x1, starting transfers between devices, local(): lax.all_to_all(cross_re, 'seq', split_axis=2, concat_axis=1, tiled=True)  15 us
    all_to_all x1, waiting for transfers between devices, local(): lax.all_to_all(cross_re, 'seq', split_axis=2, concat_axis=1, tiled=True)  14.9 us
    all_to_all x1, waiting for transfers between devices, local(): lax.all_to_all(signal_im, 'seq', split_axis=1, concat_axis=2, tiled=True)  13.4 us
    all_to_all x1, waiting for transfers between devices, local(): lax.all_to_all(out_field, 'seq', split_axis=1, concat_axis=2, tiled=True)  13.3 us
  transfers between devices with their start and end apart: 19, of which 19 were waited for; matrix products, arithmetic and copies ran while one was open for 10% of the time, Pallas kernels for 0%

commit v1 on v0

v1 whole, which is shorter than its diff:
```python
import functools
import math

import jax
import jax.numpy as jnp
import ml_dtypes
import numpy as np
from jax import lax
from jax.experimental import pallas as pl
from jax.experimental.pallas import tpu as pltpu
from jax.sharding import PartitionSpec as P

LANES = 128
VMEM = pl.BlockSpec(memory_space=pltpu.VMEM)
LIMIT = 24 * 1024 * 1024


def split_table(table):
    high = table.astype(ml_dtypes.bfloat16)
    low = (table - high.astype(np.float64)).astype(ml_dtypes.bfloat16)
    return high, low


def half_rows(side):
    return -(-(side // 2 + 1) // 8) * 8


def fourier_tables(side, parts):
    used = side // 2 + 1
    rows = half_rows(side)
    per_block = side // 2 // parts
    order = np.arange(side // 2).reshape(parts, per_block).T.reshape(-1)
    coarse = np.arange(used)
    angle = 2.0 * math.pi / side * (coarse[:, None] * order[None, :] % side)
    first = np.zeros((2, rows, side // 2))
    first[0, :used] = np.cos(angle)
    first[1, :used] = -np.sin(angle)
    first = first.reshape(2 * rows, side // 2)
    weight = np.full((used,), 2.0)
    weight[0] = weight[-1] = 1.0
    last = np.zeros((side // 2, 2, rows))
    last[:, 0, :used] = (weight[:, None] * np.cos(angle)).T / side**2
    last[:, 1, :used] = (weight[:, None] * np.sin(angle)).T / side**2
    last = last.reshape(side // 2, 2 * rows)
    turn = 2.0 * math.pi / side**2 * (coarse[:, None] * np.arange(side)[None, :])
    twist = np.zeros((2, rows, side), np.float32)
    twist[0, :used] = np.cos(turn)
    twist[1, :used] = -np.sin(turn)
    fine = 2.0 * math.pi / side * (np.arange(side)[:, None] * np.arange(side)[None, :] % side)
    fine_re, fine_im = np.cos(fine), -np.sin(fine)
    mix = np.block([[fine_re, fine_im], [-fine_im, fine_re]])
    first_high, first_low = split_table(first)
    first = np.concatenate([first_high, first_high, first_low], axis=1)
    return first, twist, *split_table(mix), *split_table(last)


def halves(values):
    high = values.astype(jnp.bfloat16)
    low = (values - high.astype(jnp.float32)).astype(jnp.bfloat16)
    return high, low


def matmul(left, right):
    return jnp.dot(left, right, preferred_element_type=jnp.float32)


def gate_kernel(query, key_in, value, grad_out, filters, sent):
    slots, groups, length = query.shape
    per_row = length // LANES
    pieces = 3 * per_row
    taps = filters[...]
    for slot in range(slots):
        gated = query[slot].astype(jnp.float32) * key_in[slot].astype(jnp.float32)
        signal = grad_out[slot].astype(jnp.float32) * value[slot].astype(jnp.float32)
        base = pieces * groups * slot
        for which, rows in enumerate((gated, signal, taps)):
            for part in range(per_row):
                place = pl.ds(base + which * per_row + part, groups, stride=pieces)
                sent[place, :] = rows[:, part * LANES : (part + 1) * LANES]


def spectral_kernel(side, parts, got, first, twist, mix_high, mix_low, last_high, last_low, sent):
    rows = half_rows(side)
    per_row = side // 2 // parts
    pieces = 3 * per_row

    def one(which):
        return jnp.concatenate(
            [got[pl.ds(which * per_row + part, parts, stride=pieces), :] for part in range(per_row)], axis=0
        )

    high, low = halves(jnp.concatenate([one(which) for which in range(3)], axis=1))
    coarse = matmul(first[...], jnp.concatenate([high, low, high], axis=0))
    turn_re, turn_im = twist[0], twist[1]

    def turned(real, imag):
        return real * turn_re - imag * turn_im, real * turn_im + imag * turn_re

    def mixed(values):
        high, low = halves(values)
        return matmul(high, mix_high[...]) + (matmul(low, mix_high[...]) + matmul(high, mix_low[...]))

    stacked = []
    for which in range(3):
        lanes = slice(which * side, (which + 1) * side)
        stacked.append(jnp.concatenate(turned(coarse[:rows, lanes], coarse[rows:, lanes]), axis=1))
    spectra = mixed(jnp.concatenate(stacked, axis=0))
    (gated_re, gated_im), (signal_re, signal_im), (taps_re, taps_im) = [
        (spectra[which * rows : (which + 1) * rows, :side], spectra[which * rows : (which + 1) * rows, side:])
        for which in range(3)
    ]
    conv = (taps_re * gated_re - taps_im * gated_im, -(taps_re * gated_im + taps_im * gated_re))
    corr = (taps_re * signal_re + taps_im * signal_im, taps_im * signal_re - taps_re * signal_im)
    cross = (gated_re * signal_re + gated_im * signal_im, gated_im * signal_re - gated_re * signal_im)
    products = mixed(jnp.concatenate([jnp.concatenate(pair, axis=1) for pair in (conv, corr, cross)], axis=0))
    turned_re, turned_im = [], []
    for which in range(3):
        block = products[which * rows : (which + 1) * rows]
        real, imag = turned(block[:, :side], block[:, side:])
        turned_re.append(real)
        turned_im.append(imag)
    high, low = halves(
        jnp.concatenate([jnp.concatenate(turned_re, axis=1), jnp.concatenate(turned_im, axis=1)], axis=0)
    )
    result = matmul(last_high[...], high) + (matmul(last_high[...], low) + matmul(last_low[...], high))
    for which in range(3):
        for part in range(per_row):
            sent[pl.ds(which * per_row + part, parts, stride=pieces), :] = result[
                part * parts : (part + 1) * parts, which * side : (which + 1) * side
            ]


def share_kernel(slots, groups, got, sent):
    per_row = sent.shape[0] // groups
    pieces = 3 * per_row
    for part in range(per_row):
        total = got[pl.ds(2 * per_row + part, groups, stride=pieces), :]
        for slot in range(1, slots):
            total += got[pl.ds(slot * pieces * groups + 2 * per_row + part, groups, stride=pieces), :]
        sent[pl.ds(part, groups, stride=per_row), :] = total


def grads_kernel(got, query, key_in, value, grad_out, skip, query_grad, key_grad, value_grad):
    slots, groups, length = query.shape
    per_row = length // LANES
    pieces = 3 * per_row
    shape = (groups, groups)
    diagonal = lax.broadcasted_iota(jnp.int32, shape, 0) == lax.broadcasted_iota(jnp.int32, shape, 1)
    for slot in range(slots):
        gains = jnp.broadcast_to(skip[slot : slot + 1, :], shape)
        gain = jnp.sum(jnp.where(diagonal, gains, 0.0), axis=1, keepdims=True)
        base = slot * pieces * groups
        for part in range(per_row):
            lanes = slice(part * LANES, (part + 1) * LANES)
            conv = got[pl.ds(base + part, groups, stride=pieces), :]
            corr = got[pl.ds(base + per_row + part, groups, stride=pieces), :]
            query_f = query[slot, :, lanes].astype(jnp.float32)
            key_f = key_in[slot, :, lanes].astype(jnp.float32)
            cotangent = grad_out[slot, :, lanes].astype(jnp.float32)
            out_field = conv + gain * (query_f * key_f)
            adjoint = corr + gain * (cotangent * value[slot, :, lanes].astype(jnp.float32))
            query_grad[slot, :, lanes] = (adjoint * key_f).astype(jnp.bfloat16)
            key_grad[slot, :, lanes] = (adjoint * query_f).astype(jnp.bfloat16)
            value_grad[slot, :, lanes] = (cotangent * out_field).astype(jnp.bfloat16)


def filter_kernel(scale, got, filter_grad):
    per_row = filter_grad.shape[1] // LANES
    senders = got.shape[0] // per_row
    for part in range(per_row):
        rows = got[pl.ds(part, senders, stride=per_row), :]
        filter_grad[:, part * LANES : (part + 1) * LANES] = scale * jnp.sum(rows, axis=0, keepdims=True)


def on_device(kernel, shapes, count):
    outs = jax.tree.map(lambda shape: VMEM, shapes)
    return pl.pallas_call(
        kernel,
        out_shape=shapes,
        in_specs=[VMEM] * count,
        out_specs=outs,
        compiler_params=pltpu.CompilerParams(vmem_limit_bytes=LIMIT),
    )


def exchange(rows, axis, count):
    blocks = rows.reshape(count, 1, rows.size // count)
    return lax.all_to_all(blocks, axis, 0, 0, tiled=True).reshape(rows.shape)


def local(query, key_in, value, grad_out, filters, skip):
    parts = lax.axis_size("seq")
    chans = lax.axis_size("chan")
    slots, groups, length = query.shape
    total = parts * length
    side = math.isqrt(2 * total)
    pieces = 3 * length // LANES
    packed = jax.ShapeDtypeStruct((parts * pieces, LANES), jnp.float32)
    sent = on_device(gate_kernel, packed, 5)(query, key_in, value, grad_out, filters)
    got = exchange(sent, "seq", parts)
    tables = fourier_tables(side, parts)
    spectral = functools.partial(spectral_kernel, side, parts)
    sent = on_device(spectral, packed, 1 + len(tables))(got, *tables)
    got = exchange(sent, "seq", parts)
    shared = jax.ShapeDtypeStruct((groups * length // LANES, LANES), jnp.float32)
    lagged = on_device(functools.partial(share_kernel, slots, groups), shared, 1)(got)
    lagged = exchange(lagged, "chan", chans)
    grad = jax.ShapeDtypeStruct(query.shape, jnp.bfloat16)
    grads = on_device(grads_kernel, (grad, grad, grad), 6)(got, query, key_in, value, grad_out, skip)
    scale = 1.0 / math.sqrt(slots * chans * total)
    row = jax.ShapeDtypeStruct((1, length), jnp.float32)
    filter_grad = on_device(functools.partial(filter_kernel, scale), row, 1)(lagged)
    return (*grads, filter_grad)


def solution(mesh):
    spread = P("chan", None, "seq")
    return jax.shard_map(
        local,
        mesh=mesh,
        in_specs=(spread, spread, spread, spread, P(None, "seq"), P("chan", None)),
        out_specs=(spread, spread, spread, P("chan", "seq")),
        check_vma=False,
    )
```

time: 537 us -> 73.9 us (0.14)
  the two profiles are of different devices: /device:TPU:24 before, /device:TPU:1 now
where the time goes in v1:
time: 73.9 us; the launch traced here: 73.2 us
  blocking collectives  52.1 us (71%)
  starting transfers between devices  7.34 us (10%)
  local copies, waits for them, and re-layouts  5.26 us (7%)
  waiting for transfers between devices  5.03 us (7%)
  Pallas kernels  2.82 us (4%)
    all_to_all x2, blocking collectives, exchange(): return lax.all_to_all(blocks, axis, 0, 0, tiled=True).reshape(rows.shape)  52.1 us
    all_to_all x1, starting transfers between devices, exchange(): return lax.all_to_all(blocks, axis, 0, 0, tiled=True).reshape(rows.shape)  7.34 us
    unnamed x32, local copies, waits for them, and re-layouts  5.26 us
    all_to_all x1, waiting for transfers between devices, exchange(): return lax.all_to_all(blocks, axis, 0, 0, tiled=True).reshape(rows.shape)  5.03 us
  transfers between devices with their start and end apart: 1, of which 1 were waited for; matrix products, arithmetic and copies ran while one was open for 0% of the time, Pallas kernels for 1%

profile of v1, /device:TPU:1, one launch (start us, length us, event | category | flops | bytes accessed | tf_op | source)
XLA Modules:
  0.0 73.2 jit_solution(7080322958307480247)
XLA Ops:
  0.6 0.0 copy-start.4
  0.6 0.7 copy-done.4
  1.4 0.0 copy-start.6
  1.4 0.7 copy-done.6
  2.1 0.0 copy-start.8
  2.1 0.7 copy-done.8
  2.8 0.0 copy-start.10
  2.8 0.7 copy-done.10
  3.5 0.0 copy-start.14
  3.5 0.7 copy-done.14
  4.2 0.0 copy-start.1
  4.2 0.0 copy-start.2
  4.2 0.0 copy-start
  4.3 0.0 copy-start.12
  4.3 32.8 %all_to_all.15 = f32[32,1,768]{2,1,0:T(1,128)S(1)} all-to-all(f32[32,1,768]{2,1,0:T(1,128)S(1)} %bitcast.8), channel_id=1, replica_groups=mesh['seq'=32,'chan'=16] {'seq'}, dimensions={0} | all-to-all | bytes 196608 | tf_op jit(solution)/shard_map/all_to_all | solution.py:188
  37.1 0.0 copy-done.1
  37.1 0.0 copy-done.2
  37.1 0.0 copy-done
  37.1 0.0 copy-done.12
  37.1 0.0 copy-start.3
  37.1 0.9 %copy-done.3 = bf16[144,192]{1,0:T(8,128)(2,1)S(1)} copy-done((bf16[144,192]{1,0:T(8,128)(2,1)S(1)}, bf16[144,192]{1,0:T(8,128)(2,1)}, u32[]{:S(2)}) %copy-start.3) | copy-done | bytes 55320
  38.0 0.0 copy-start.13
  38.0 0.8 %copy-done.13 = bf16[64,144]{1,0:T(8,128)(2,1)S(1)} copy-done((bf16[64,144]{1,0:T(8,128)(2,1)S(1)}, bf16[64,144]{1,0:T(8,128)(2,1)}, u32[]{:S(2)}) %copy-start.13) | copy-done | bytes 18456
  38.8 0.9 %shard_map.148 = f32[192,128]{1,0:T(8,128)S(1)} custom-call(f32[192,128]{1,0:T(8,128)S(1)} %bitcast.9, bf16[144,192]{1,0:T(8,128)(2,1)S(1)} %copy-done.3, f32[2,72,128]{2,1,0:T(8,128)S(1)} %copy-done.2, bf16[256,256]{1,0:T(8,128)(2,1)S(1)} %copy-done.1, bf16[256,256]{1,0:T(8,128)(2,1)S(1)} %copy-done, bf16[64,144]{1,0:T(8,128)(2,1)S(1)} %copy-done.13, ...), custom_call_target="tpu_custom_call" | custom-call | tf_op jit(solution)/shard_map/pallas_call | solution.py:203
  39.7 19.2 %all_to_all.16 = f32[32,1,768]{2,1,0:T(1,128)S(1)} all-to-all(f32[32,1,768]{2,1,0:T(1,128)S(1)} %bitcast.10), channel_id=1, replica_groups=mesh['seq'=32,'chan'=16] {'seq'}, dimensions={0} | all-to-all | bytes 196608 | tf_op jit(solution)/shard_map/all_to_all | solution.py:188
  58.9 0.0 copy-start.9
  58.9 0.0 copy-start.11
  58.9 0.0 copy-start.15
  58.9 0.6 shard_map.150
  59.5 0.0 copy-start.5
  59.5 0.0 copy-start.7
  59.5 7.3 %all-to-all-start.2 = ((f32[16,1,256]{2,1,0:T(1,128)}), f32[16,1,256]{2,1,0:T(1,128)S(1)}, u32[]{:S(2)}, u32[]{:S(2)}) async-start(f32[16,1,256]{2,1,0:T(1,128)} %bitcast.4), calls=%async_computation.2 | async-start | bytes 32768 | tf_op jit(solution)/shard_map/all_to_all | solution.py:188
  66.9 0.0 copy-done.9
  66.9 0.0 copy-done.11
  66.9 0.0 copy-done.15
  66.9 0.0 copy-done.5
  66.9 0.0 copy-done.7
  66.9 0.7 shard_map.149
  67.6 5.0 %all-to-all-done.2 = f32[16,1,256]{2,1,0:T(1,128)S(1)} async-done(((f32[16,1,256]{2,1,0:T(1,128)}), f32[16,1,256]{2,1,0:T(1,128)S(1)}, u32[]{:S(2)}, u32[]{:S(2)}) %all-to-all-start.2) | async-done | bytes 16416 | tf_op jit(solution)/shard_map/all_to_all | solution.py:188
  72.7 0.6 shard_map.151
  (1 shorter events, 0.0 us)
Async XLA Ops:
  0.6 0.7 copy-start.4
  1.4 0.7 copy-start.6
  2.1 0.7 copy-start.8
  2.8 0.7 copy-start.10
  3.5 0.7 copy-start.14
  4.2 32.9 %copy-start.1 = (bf16[256,256]{1,0:T(8,128)(2,1)S(1)}, bf16[256,256]{1,0:T(8,128)(2,1)}, u32[]{:S(2)}) copy-start(bf16[256,256]{1,0:T(8,128)(2,1)} %constant.14.clone.mix_high) | copy-start | bytes 393220
  4.2 32.9 %copy-start.2 = (f32[2,72,128]{2,1,0:T(8,128)S(1)}, f32[2,72,128]{2,1,0:T(8,128)}, u32[]{:S(2)}) copy-start(f32[2,72,128]{2,1,0:T(8,128)} %constant.13.clone.twist) | copy-start | bytes 221188
  4.2 32.9 %copy-start = (bf16[256,256]{1,0:T(8,128)(2,1)S(1)}, bf16[256,256]{1,0:T(8,128)(2,1)}, u32[]{:S(2)}) copy-start(bf16[256,256]{1,0:T(8,128)(2,1)} %constant.15.clone.mix_low) | copy-start | bytes 393220
  4.3 32.9 %copy-start.12 = (bf16[64,144]{1,0:T(8,128)(2,1)S(1)}, bf16[64,144]{1,0:T(8,128)(2,1)}, u32[]{:S(2)}) copy-start(bf16[64,144]{1,0:T(8,128)(2,1)} %constant.17.clone.last_low) | copy-start | bytes 55300
  37.1 0.9 %copy-start.3 = (bf16[144,192]{1,0:T(8,128)(2,1)S(1)}, bf16[144,192]{1,0:T(8,128)(2,1)}, u32[]{:S(2)}) copy-start(bf16[144,192]{1,0:T(8,128)(2,1)} %constant.12.clone.first) | copy-start | bytes 165892
  38.0 0.8 %copy-start.13 = (bf16[64,144]{1,0:T(8,128)(2,1)S(1)}, bf16[64,144]{1,0:T(8,128)(2,1)}, u32[]{:S(2)}) copy-start(bf16[64,144]{1,0:T(8,128)(2,1)} %constant.16.clone.last_high) | copy-start | bytes 55300
  58.9 8.0 %copy-start.9 = (bf16[2,16,256]{2,1,0:T(8,128)(2,1)S(1)}, bf16[2,16,256]{2,1,0:T(8,128)(2,1)}, u32[]{:S(2)}) copy-start(bf16[2,16,256]{2,1,0:T(8,128)(2,1)} %value.3) | copy-start | bytes 49156
  58.9 8.0 %copy-start.11 = (bf16[2,16,256]{2,1,0:T(8,128)(2,1)S(1)}, bf16[2,16,256]{2,1,0:T(8,128)(2,1)}, u32[]{:S(2)}) copy-start(bf16[2,16,256]{2,1,0:T(8,128)(2,1)} %grad_out.3) | copy-start | bytes 49156
  58.9 8.0 %copy-start.15 = (f32[2,16]{1,0:T(2,128)S(1)}, f32[2,16]{1,0:T(2,128)}, u32[]{:S(2)}) copy-start(f32[2,16]{1,0:T(2,128)} %skip.1) | copy-start | bytes 388
  59.5 7.4 %copy-start.5 = (bf16[2,16,256]{2,1,0:T(8,128)(2,1)S(1)}, bf16[2,16,256]{2,1,0:T(8,128)(2,1)}, u32[]{:S(2)}) copy-start(bf16[2,16,256]{2,1,0:T(8,128)(2,1)} %query.3) | copy-start | bytes 49156
  59.5 7.4 %copy-start.7 = (bf16[2,16,256]{2,1,0:T(8,128)(2,1)S(1)}, bf16[2,16,256]{2,1,0:T(8,128)(2,1)}, u32[]{:S(2)}) copy-start(bf16[2,16,256]{2,1,0:T(8,128)(2,1)} %key_in.3) | copy-start | bytes 49156
  59.5 13.1 %all-to-all-start.2 = ((f32[16,1,256]{2,1,0:T(1,128)}), f32[16,1,256]{2,1,0:T(1,128)S(1)}, u32[]{:S(2)}, u32[]{:S(2)}) async-start(f32[16,1,256]{2,1,0:T(1,128)} %bitcast.4), calls=%async_computation.2 | async-start | bytes 32768 | tf_op jit(solution)/shard_map/all_to_all | solution.py:188

commit v2 on v1

--- a/solution.py
+++ b/solution.py
@@ -12,7 +12,8 @@
 
 LANES = 128
 VMEM = pl.BlockSpec(memory_space=pltpu.VMEM)
-LIMIT = 24 * 1024 * 1024
+HBM = pl.BlockSpec(memory_space=pltpu.HBM)
+LIMIT = 16 * 1024 * 1024
 
 
 def split_table(table):
@@ -51,7 +52,20 @@
     mix = np.block([[fine_re, fine_im], [-fine_im, fine_re]])
     first_high, first_low = split_table(first)
     first = np.concatenate([first_high, first_high, first_low], axis=1)
-    return first, twist, *split_table(mix), *split_table(last)
+    blocks = [*split_table(mix), first, *split_table(last)]
+    wide = max(block.shape[1] for block in blocks)
+    stacked = [np.pad(block, ((0, 0), (0, wide - block.shape[1]))) for block in blocks]
+    return np.concatenate(stacked, axis=0), twist
+
+
+def table_slices(side):
+    rows = half_rows(side)
+    sizes = ((2 * side, 2 * side),) * 2 + ((2 * rows, 3 * side // 2),) + ((side // 2, 2 * rows),) * 2
+    starts = np.cumsum([0] + [size[0] for size in sizes])
+    return [
+        (slice(int(start), int(start) + height), slice(0, width))
+        for start, (height, width) in zip(starts, sizes)
+    ]
 
 
 def halves(values):
@@ -64,22 +78,33 @@
     return jnp.dot(left, right, preferred_element_type=jnp.float32)
 
 
-def gate_kernel(query, key_in, value, grad_out, filters, sent):
+def gate_kernel(
+    query, key_in, value, grad_out, filters, skip, tables, twist,
+    sent, inputs, gains, tables_held, twist_held, taps, sems,
+):
     slots, groups, length = query.shape
     per_row = length // LANES
     pieces = 3 * per_row
-    taps = filters[...]
+    pairs = [(source, inputs.at[place]) for place, source in enumerate((query, key_in, grad_out, value))]
+    pairs += [(filters, taps), (skip, gains), (tables, tables_held), (twist, twist_held)]
+    copies = [pltpu.make_async_copy(*pair, sems.at[place]) for place, pair in enumerate(pairs)]
+    for copy in copies:
+        copy.start()
+    for copy in copies[:5]:
+        copy.wait()
     for slot in range(slots):
-        gated = query[slot].astype(jnp.float32) * key_in[slot].astype(jnp.float32)
-        signal = grad_out[slot].astype(jnp.float32) * value[slot].astype(jnp.float32)
+        query_f, key_f, cotangent, value_f = [inputs[place, slot].astype(jnp.float32) for place in range(4)]
         base = pieces * groups * slot
-        for which, rows in enumerate((gated, signal, taps)):
+        for which, rows in enumerate((query_f * key_f, cotangent * value_f, taps[...])):
             for part in range(per_row):
                 place = pl.ds(base + which * per_row + part, groups, stride=pieces)
                 sent[place, :] = rows[:, part * LANES : (part + 1) * LANES]
-
-
-def spectral_kernel(side, parts, got, first, twist, mix_high, mix_low, last_high, last_low, sent):
+    for copy in copies[5:]:
+        copy.wait()
+
+
+def spectral_kernel(side, parts, got, tables, twist, sent):
+    mix_high, mix_low, first, last_high, last_low = [tables[place] for place in table_slices(side)]
     rows = half_rows(side)
     per_row = side // 2 // parts
     pieces = 3 * per_row
@@ -90,7 +115,7 @@
         )
 
     high, low = halves(jnp.concatenate([one(which) for which in range(3)], axis=1))
-    coarse = matmul(first[...], jnp.concatenate([high, low, high], axis=0))
+    coarse = matmul(first, jnp.concatenate([high, low, high], axis=0))
     turn_re, turn_im = twist[0], twist[1]
 
     def turned(real, imag):
@@ -98,7 +123,7 @@
 
     def mixed(values):
         high, low = halves(values)
-        return matmul(high, mix_high[...]) + (matmul(low, mix_high[...]) + matmul(high, mix_low[...]))
+        return matmul(high, mix_high) + (matmul(low, mix_high) + matmul(high, mix_low))
 
     stacked = []
     for which in range(3):
@@ -122,7 +147,7 @@
     high, low = halves(
         jnp.concatenate([jnp.concatenate(turned_re, axis=1), jnp.concatenate(turned_im, axis=1)], axis=0)
     )
-    result = matmul(last_high[...], high) + (matmul(last_high[...], low) + matmul(last_low[...], high))
+    result = matmul(last_high, high) + (matmul(last_high, low) + matmul(last_low, high))
     for which in range(3):
         for part in range(per_row):
             sent[pl.ds(which * per_row + part, parts, stride=pieces), :] = result[
@@ -140,8 +165,8 @@
         sent[pl.ds(part, groups, stride=per_row), :] = total
 
 
-def grads_kernel(got, query, key_in, value, grad_out, skip, query_grad, key_grad, value_grad):
-    slots, groups, length = query.shape
+def grads_kernel(got, inputs, skip, query_grad, key_grad, value_grad):
+    _, slots, groups, length = inputs.shape
     per_row = length // LANES
     pieces = 3 * per_row
     shape = (groups, groups)
@@ -154,11 +179,11 @@
             lanes = slice(part * LANES, (part + 1) * LANES)
             conv = got[pl.ds(base + part, groups, stride=pieces), :]
             corr = got[pl.ds(base + per_row + part, groups, stride=pieces), :]
-            query_f = query[slot, :, lanes].astype(jnp.float32)
-            key_f = key_in[slot, :, lanes].astype(jnp.float32)
-            cotangent = grad_out[slot, :, lanes].astype(jnp.float32)
+            query_f, key_f, cotangent, value_f = [
+                inputs[place, slot, :, lanes].astype(jnp.float32) for place in range(4)
+            ]
             out_field = conv + gain * (query_f * key_f)
-            adjoint = corr + gain * (cotangent * value[slot, :, lanes].astype(jnp.float32))
+            adjoint = corr + gain * (cotangent * value_f)
             query_grad[slot, :, lanes] = (adjoint * key_f).astype(jnp.bfloat16)
             key_grad[slot, :, lanes] = (adjoint * query_f).astype(jnp.bfloat16)
             value_grad[slot, :, lanes] = (cotangent * out_field).astype(jnp.bfloat16)
@@ -172,15 +197,20 @@
         filter_grad[:, part * LANES : (part + 1) * LANES] = scale * jnp.sum(rows, axis=0, keepdims=True)
 
 
-def on_device(kernel, shapes, count):
+def on_device(kernel, shapes, count, space=VMEM, scratch=()):
     outs = jax.tree.map(lambda shape: VMEM, shapes)
     return pl.pallas_call(
         kernel,
         out_shape=shapes,
-        in_specs=[VMEM] * count,
+        in_specs=[space] * count,
         out_specs=outs,
+        scratch_shapes=scratch,
         compiler_params=pltpu.CompilerParams(vmem_limit_bytes=LIMIT),
     )
+
+
+def in_hbm(array):
+    return pltpu.with_memory_space_constraint(jnp.asarray(array), pltpu.HBM)
 
 
 def exchange(rows, axis, count):
@@ -196,17 +226,25 @@
     side = math.isqrt(2 * total)
     pieces = 3 * length // LANES
     packed = jax.ShapeDtypeStruct((parts * pieces, LANES), jnp.float32)
-    sent = on_device(gate_kernel, packed, 5)(query, key_in, value, grad_out, filters)
+    tables, twist = fourier_tables(side, parts)
+    shapes = (
+        packed,
+        jax.ShapeDtypeStruct((4, *query.shape), query.dtype),
+        *[jax.ShapeDtypeStruct(array.shape, array.dtype) for array in (skip, tables, twist)],
+    )
+    scratch = [pltpu.VMEM(filters.shape, jnp.float32), pltpu.SemaphoreType.DMA((8,))]
+    sent, inputs, gains, tables, twist = on_device(gate_kernel, shapes, 8, HBM, scratch)(
+        *[in_hbm(array) for array in (query, key_in, value, grad_out, filters, skip, tables, twist)]
+    )
     got = exchange(sent, "seq", parts)
-    tables = fourier_tables(side, parts)
     spectral = functools.partial(spectral_kernel, side, parts)
-    sent = on_device(spectral, packed, 1 + len(tables))(got, *tables)
+    sent = on_device(spectral, packed, 3)(got, tables, twist)
     got = exchange(sent, "seq", parts)
     shared = jax.ShapeDtypeStruct((groups * length // LANES, LANES), jnp.float32)
     lagged = on_device(functools.partial(share_kernel, slots, groups), shared, 1)(got)
     lagged = exchange(lagged, "chan", chans)
     grad = jax.ShapeDtypeStruct(query.shape, jnp.bfloat16)
-    grads = on_device(grads_kernel, (grad, grad, grad), 6)(got, query, key_in, value, grad_out, skip)
+    grads = on_device(grads_kernel, (grad, grad, grad), 3)(got, inputs, gains)
     scale = 1.0 / math.sqrt(slots * chans * total)
     row = jax.ShapeDtypeStruct((1, length), jnp.float32)
     filter_grad = on_device(functools.partial(filter_kernel, scale), row, 1)(lagged)

time: 73.9 us -> 69.2 us (0.936)
  local copies, waits for them, and re-layouts: 5.26 us -> 0 us
  Pallas kernels: 2.82 us -> 3.98 us
    unnamed x32 -> x0, local copies, waits for them, and re-layouts: 5.26 us -> none
    pallas_call x3, Pallas kernels: 1.64 us -> 2.81 us  [the longest x1 1.18 us: local(): on_device(gate_kernel, shapes, 8, HBM, scratch)]
where the time goes in v2:
time: 69.2 us; the launch traced here: 68.8 us
  blocking collectives  51.9 us (75%)
  starting transfers between devices  7.26 us (10%)
  waiting for transfers between devices  5.08 us (7%)
  Pallas kernels  3.98 us (6%)
    all_to_all x2, blocking collectives, exchange(): return lax.all_to_all(blocks, axis, 0, 0, tiled=True).reshape(rows.shape)  51.9 us
    all_to_all x1, starting transfers between devices, exchange(): return lax.all_to_all(blocks, axis, 0, 0, tiled=True).reshape(rows.shape)  7.26 us
    all_to_all x1, waiting for transfers between devices, exchange(): return lax.all_to_all(blocks, axis, 0, 0, tiled=True).reshape(rows.shape)  5.08 us
  transfers between devices with their start and end apart: 1, of which 1 were waited for; matrix products, arithmetic and copies ran while one was open for 0% of the time, Pallas kernels for 1%

profile of v2, /device:TPU:1, one launch (start us, length us, event | category | flops | bytes accessed | tf_op | source)
XLA Modules:
  0.0 68.8 jit_solution(8375833677862443671)
XLA Ops:
  0.6 1.2 %shard_map.111 = (f32[192,128]{1,0:T(8,128)S(1)}, bf16[4,2,16,256]{3,2,1,0:T(8,128)(2,1)S(1)}, f32[2,16]{1,0:T(2,128)S(1)}, bf16[784,256]{1,0:T(8,128)(2,1)S(1)}, f32[2,72,128]{2,1,0:T(8,128)S(1)}) custom-call(bf16[2,16,256]{2,1,0:T(8,128)(2,1)} %query.1, bf16[2,16,256]{2,1,0:T(8,128)(2,1)} %key_in.1, bf16[2,16,256]{2,1,0:T(8,128)(2,1)} %value.1, ...), custom_call_target="tpu_custom_call" | custom-call | tf_op jit(solution)/shard_map/pallas_call | solution.py:236
  1.8 32.7 %all_to_all.15 = f32[32,1,768]{2,1,0:T(1,128)S(1)} all-to-all(f32[32,1,768]{2,1,0:T(1,128)S(1)} %bitcast.10), channel_id=1, replica_groups=mesh['seq'=32,'chan'=16] {'seq'}, dimensions={0} | all-to-all | bytes 196608 | tf_op jit(solution)/shard_map/all_to_all | solution.py:218
  34.5 0.9 %shard_map.112 = f32[192,128]{1,0:T(8,128)S(1)} custom-call(f32[192,128]{1,0:T(8,128)S(1)} %bitcast.8, bf16[784,256]{1,0:T(8,128)(2,1)S(1)} %get-tuple-element.13.tables, f32[2,72,128]{2,1,0:T(8,128)S(1)} %get-tuple-element.14.twist), custom_call_target="tpu_custom_call" | custom-call | tf_op jit(solution)/shard_map/pallas_call | solution.py:241
  35.5 19.2 %all_to_all.16 = f32[32,1,768]{2,1,0:T(1,128)S(1)} all-to-all(f32[32,1,768]{2,1,0:T(1,128)S(1)} %bitcast.9), channel_id=1, replica_groups=mesh['seq'=32,'chan'=16] {'seq'}, dimensions={0} | all-to-all | bytes 196608 | tf_op jit(solution)/shard_map/all_to_all | solution.py:218
  54.6 0.6 shard_map.114
  55.2 7.3 %all-to-all-start.2 = ((f32[16,1,256]{2,1,0:T(1,128)}), f32[16,1,256]{2,1,0:T(1,128)S(1)}, u32[]{:S(2)}, u32[]{:S(2)}) async-start(f32[16,1,256]{2,1,0:T(1,128)} %bitcast.4), calls=%async_computation.2 | async-start | bytes 32768 | tf_op jit(solution)/shard_map/all_to_all | solution.py:218
  62.5 0.7 %shard_map.113 = (bf16[2,16,256]{2,1,0:T(8,128)(2,1)}, bf16[2,16,256]{2,1,0:T(8,128)(2,1)}, bf16[2,16,256]{2,1,0:T(8,128)(2,1)}) custom-call(f32[192,128]{1,0:T(8,128)S(1)} %bitcast.7, bf16[4,2,16,256]{3,2,1,0:T(8,128)(2,1)S(1)} %get-tuple-element.15.inputs, f32[2,16]{1,0:T(2,128)S(1)} %get-tuple-element.16.skip), custom_call_target="tpu_custom_call" | custom-call | tf_op jit(solution)/shard_map/pallas_call | solution.py:247
  63.2 5.1 %all-to-all-done.2 = f32[16,1,256]{2,1,0:T(1,128)S(1)} async-done(((f32[16,1,256]{2,1,0:T(1,128)}), f32[16,1,256]{2,1,0:T(1,128)S(1)}, u32[]{:S(2)}, u32[]{:S(2)}) %all-to-all-start.2) | async-done | bytes 16416 | tf_op jit(solution)/shard_map/all_to_all | solution.py:218
  68.3 0.6 shard_map.115
Async XLA Ops:
  55.2 13.0 %all-to-all-start.2 = ((f32[16,1,256]{2,1,0:T(1,128)}), f32[16,1,256]{2,1,0:T(1,128)S(1)}, u32[]{:S(2)}, u32[]{:S(2)}) async-start(f32[16,1,256]{2,1,0:T(1,128)} %bitcast.4), calls=%async_computation.2 | async-start | bytes 32768 | tf_op jit(solution)/shard_map/all_to_all | solution.py:218

commit v3 on v2

--- a/solution.py
+++ b/solution.py
@@ -92,10 +92,14 @@
         copy.start()
     for copy in copies[:5]:
         copy.wait()
+    back = lax.rem(groups - lax.axis_index("chan"), groups)
+    taps_turned = pltpu.roll(taps[...], back, 0)
     for slot in range(slots):
         query_f, key_f, cotangent, value_f = [inputs[place, slot].astype(jnp.float32) for place in range(4)]
         base = pieces * groups * slot
-        for which, rows in enumerate((query_f * key_f, cotangent * value_f, taps[...])):
+        gated = pltpu.roll(query_f * key_f, back, 0)
+        signal = pltpu.roll(cotangent * value_f, back, 0)
+        for which, rows in enumerate((gated, signal, taps_turned)):
             for part in range(per_row):
                 place = pl.ds(base + which * per_row + part, groups, stride=pieces)
                 sent[place, :] = rows[:, part * LANES : (part + 1) * LANES]
@@ -103,7 +107,7 @@
         copy.wait()
 
 
-def spectral_kernel(side, parts, got, tables, twist, sent):
+def spectral_kernel(side, parts, signals, combine, got, tables, twist, sent):
     mix_high, mix_low, first, last_high, last_low = [tables[place] for place in table_slices(side)]
     rows = half_rows(side)
     per_row = side // 2 // parts
@@ -114,61 +118,58 @@
             [got[pl.ds(which * per_row + part, parts, stride=pieces), :] for part in range(per_row)], axis=0
         )
 
-    high, low = halves(jnp.concatenate([one(which) for which in range(3)], axis=1))
+    def turned(real, imag):
+        return real * twist[0] - imag * twist[1], real * twist[1] + imag * twist[0]
+
+    def mixed(pairs):
+        high, low = halves(jnp.concatenate([jnp.concatenate(pair, axis=1) for pair in pairs], axis=0))
+        values = matmul(high, mix_high) + (matmul(low, mix_high) + matmul(high, mix_low))
+        blocks = [values[place * rows : (place + 1) * rows] for place in range(len(pairs))]
+        return [(block[:, :side], block[:, side:]) for block in blocks]
+
+    high, low = halves(jnp.concatenate([one(which) for which in signals], axis=1))
     coarse = matmul(first, jnp.concatenate([high, low, high], axis=0))
-    turn_re, turn_im = twist[0], twist[1]
-
-    def turned(real, imag):
-        return real * turn_re - imag * turn_im, real * turn_im + imag * turn_re
-
-    def mixed(values):
-        high, low = halves(values)
-        return matmul(high, mix_high) + (matmul(low, mix_high) + matmul(high, mix_low))
-
-    stacked = []
-    for which in range(3):
-        lanes = slice(which * side, (which + 1) * side)
-        stacked.append(jnp.concatenate(turned(coarse[:rows, lanes], coarse[rows:, lanes]), axis=1))
-    spectra = mixed(jnp.concatenate(stacked, axis=0))
-    (gated_re, gated_im), (signal_re, signal_im), (taps_re, taps_im) = [
-        (spectra[which * rows : (which + 1) * rows, :side], spectra[which * rows : (which + 1) * rows, side:])
-        for which in range(3)
-    ]
+    lanes = [slice(place * side, (place + 1) * side) for place in range(len(signals))]
+    spectra = mixed([turned(coarse[:rows, lane], coarse[rows:, lane]) for lane in lanes])
+    products = [turned(*pair) for pair in mixed(combine(*spectra))]
+    high, low = halves(
+        jnp.concatenate([jnp.concatenate(parts_of, axis=1) for parts_of in zip(*products)], axis=0)
+    )
+    result = matmul(last_high, high) + (matmul(last_high, low) + matmul(last_low, high))
+    spread = sent.shape[0] > side // 2
+    for which in range(len(products)):
+        for part in range(per_row):
+            piece = result[part * parts : (part + 1) * parts, which * side : (which + 1) * side]
+            if spread:
+                sent[pl.ds(which * per_row + part, parts, stride=pieces), :] = piece
+            else:
+                sent[pl.ds(part * parts, parts), :] = piece
+
+
+def lag_product(gated, signal):
+    (gated_re, gated_im), (signal_re, signal_im) = gated, signal
+    return [(gated_re * signal_re + gated_im * signal_im, gated_im * signal_re - gated_re * signal_im)]
+
+
+def filtered(gated, signal, taps):
+    (gated_re, gated_im), (signal_re, signal_im), (taps_re, taps_im) = gated, signal, taps
     conv = (taps_re * gated_re - taps_im * gated_im, -(taps_re * gated_im + taps_im * gated_re))
     corr = (taps_re * signal_re + taps_im * signal_im, taps_im * signal_re - taps_re * signal_im)
-    cross = (gated_re * signal_re + gated_im * signal_im, gated_im * signal_re - gated_re * signal_im)
-    products = mixed(jnp.concatenate([jnp.concatenate(pair, axis=1) for pair in (conv, corr, cross)], axis=0))
-    turned_re, turned_im = [], []
-    for which in range(3):
-        block = products[which * rows : (which + 1) * rows]
-        real, imag = turned(block[:, :side], block[:, side:])
-        turned_re.append(real)
-        turned_im.append(imag)
-    high, low = halves(
-        jnp.concatenate([jnp.concatenate(turned_re, axis=1), jnp.concatenate(turned_im, axis=1)], axis=0)
-    )
-    result = matmul(last_high, high) + (matmul(last_high, low) + matmul(last_low, high))
-    for which in range(3):
-        for part in range(per_row):
-            sent[pl.ds(which * per_row + part, parts, stride=pieces), :] = result[
-                part * parts : (part + 1) * parts, which * side : (which + 1) * side
-            ]
-
-
-def share_kernel(slots, groups, got, sent):
-    per_row = sent.shape[0] // groups
-    pieces = 3 * per_row
+    return [conv, corr]
+
+
+def pack_kernel(parts, rows, lags, sent):
+    per_row = lags.shape[0] // parts
+    pieces = sent.shape[0] // parts
     for part in range(per_row):
-        total = got[pl.ds(2 * per_row + part, groups, stride=pieces), :]
-        for slot in range(1, slots):
-            total += got[pl.ds(slot * pieces * groups + 2 * per_row + part, groups, stride=pieces), :]
-        sent[pl.ds(part, groups, stride=per_row), :] = total
-
-
-def grads_kernel(got, inputs, skip, query_grad, key_grad, value_grad):
+        sent[pl.ds(2 * per_row + part, parts, stride=pieces), :] = lags[pl.ds(part * parts, parts), :]
+
+
+def grads_kernel(scale, got, inputs, skip, query_grad, key_grad, value_grad, filter_grad):
     _, slots, groups, length = inputs.shape
     per_row = length // LANES
     pieces = 3 * per_row
+    ahead = lax.axis_index("chan")
     shape = (groups, groups)
     diagonal = lax.broadcasted_iota(jnp.int32, shape, 0) == lax.broadcasted_iota(jnp.int32, shape, 1)
     for slot in range(slots):
@@ -177,8 +178,8 @@
         base = slot * pieces * groups
         for part in range(per_row):
             lanes = slice(part * LANES, (part + 1) * LANES)
-            conv = got[pl.ds(base + part, groups, stride=pieces), :]
-            corr = got[pl.ds(base + per_row + part, groups, stride=pieces), :]
+            conv = pltpu.roll(got[pl.ds(base + part, groups, stride=pieces), :], ahead, 0)
+            corr = pltpu.roll(got[pl.ds(base + per_row + part, groups, stride=pieces), :], ahead, 0)
             query_f, key_f, cotangent, value_f = [
                 inputs[place, slot, :, lanes].astype(jnp.float32) for place in range(4)
             ]
@@ -187,17 +188,12 @@
             query_grad[slot, :, lanes] = (adjoint * key_f).astype(jnp.bfloat16)
             key_grad[slot, :, lanes] = (adjoint * query_f).astype(jnp.bfloat16)
             value_grad[slot, :, lanes] = (cotangent * out_field).astype(jnp.bfloat16)
-
-
-def filter_kernel(scale, got, filter_grad):
-    per_row = filter_grad.shape[1] // LANES
-    senders = got.shape[0] // per_row
     for part in range(per_row):
-        rows = got[pl.ds(part, senders, stride=per_row), :]
-        filter_grad[:, part * LANES : (part + 1) * LANES] = scale * jnp.sum(rows, axis=0, keepdims=True)
-
-
-def on_device(kernel, shapes, count, space=VMEM, scratch=()):
+        lagged = got[pl.ds(2 * per_row + part, slots * groups, stride=pieces), :]
+        filter_grad[:, part * LANES : (part + 1) * LANES] = scale * jnp.sum(lagged, axis=0, keepdims=True)
+
+
+def on_device(kernel, shapes, count, space=VMEM, scratch=(), aliases=None):
     outs = jax.tree.map(lambda shape: VMEM, shapes)
     return pl.pallas_call(
         kernel,
@@ -205,6 +201,7 @@
         in_specs=[space] * count,
         out_specs=outs,
         scratch_shapes=scratch,
+        input_output_aliases=aliases or {},
         compiler_params=pltpu.CompilerParams(vmem_limit_bytes=LIMIT),
     )
 
@@ -237,18 +234,20 @@
         *[in_hbm(array) for array in (query, key_in, value, grad_out, filters, skip, tables, twist)]
     )
     got = exchange(sent, "seq", parts)
-    spectral = functools.partial(spectral_kernel, side, parts)
-    sent = on_device(spectral, packed, 3)(got, tables, twist)
+    lag_rows = jax.ShapeDtypeStruct((side // 2, LANES), jnp.float32)
+    lags = functools.partial(spectral_kernel, side, parts, (0, 1), lag_product)
+    lags = on_device(lags, lag_rows, 3)(got, tables, twist)
+    moves = [(s * chans + k, s * chans + (s + k) % chans) for s in range(parts) for k in range(chans)]
+    lags = lax.ppermute(lags, ("seq", "chan"), moves)
+    rows = functools.partial(spectral_kernel, side, parts, (0, 1, 2), filtered)
+    rows = on_device(rows, packed, 3)(got, tables, twist)
+    sent = on_device(functools.partial(pack_kernel, parts), packed, 2, aliases={0: 0})(rows, lags)
     got = exchange(sent, "seq", parts)
-    shared = jax.ShapeDtypeStruct((groups * length // LANES, LANES), jnp.float32)
-    lagged = on_device(functools.partial(share_kernel, slots, groups), shared, 1)(got)
-    lagged = exchange(lagged, "chan", chans)
     grad = jax.ShapeDtypeStruct(query.shape, jnp.bfloat16)
-    grads = on_device(grads_kernel, (grad, grad, grad), 3)(got, inputs, gains)
+    row = jax.ShapeDtypeStruct((1, length), jnp.float32)
     scale = 1.0 / math.sqrt(slots * chans * total)
-    row = jax.ShapeDtypeStruct((1, length), jnp.float32)
-    filter_grad = on_device(functools.partial(filter_kernel, scale), row, 1)(lagged)
-    return (*grads, filter_grad)
+    grads = functools.partial(grads_kernel, scale)
+    return on_device(grads, (grad, grad, grad, row), 3)(got, inputs, gains)
 
 
 def solution(mesh):

time: 69.2 us -> 64.7 us (0.935)
  the two profiles are of different devices: /device:TPU:1 before, /device:TPU:24 now
where the time goes in v3:
time: 64.7 us; the launch traced here: 64.4 us
  blocking collectives  59.5 us (92%)
  Pallas kernels  3.52 us (5%)
  between operations  0.68 us (1%)
  starting transfers between devices  0.66 us (1%)
    all_to_all x2, blocking collectives, exchange(): return lax.all_to_all(blocks, axis, 0, 0, tiled=True).reshape(rows.shape)  59.5 us
  transfers between devices with their start and end apart: 1, of which 0 were waited for; matrix products, arithmetic and copies ran while one was open for 0% of the time, Pallas kernels for 1%

profile of v3, /device:TPU:24, one launch (start us, length us, event | category | flops | bytes accessed | tf_op | source)
XLA Modules:
  0.0 64.4 jit_solution(7078201864632999219)
XLA Ops:
  0.6 1.2 %shard_map.111 = (f32[192,128]{1,0:T(8,128)S(1)}, bf16[4,2,16,256]{3,2,1,0:T(8,128)(2,1)S(1)}, f32[2,16]{1,0:T(2,128)S(1)}, bf16[784,256]{1,0:T(8,128)(2,1)S(1)}, f32[2,72,128]{2,1,0:T(8,128)S(1)}) custom-call(bf16[2,16,256]{2,1,0:T(8,128)(2,1)} %query.1, bf16[2,16,256]{2,1,0:T(8,128)(2,1)} %key_in.1, bf16[2,16,256]{2,1,0:T(8,128)(2,1)} %value.1, ...), custom_call_target="tpu_custom_call" | custom-call | tf_op jit(solution)/shard_map/pallas_call | solution.py:233
  1.8 34.1 %all_to_all.10 = f32[32,1,768]{2,1,0:T(1,128)S(1)} all-to-all(f32[32,1,768]{2,1,0:T(1,128)S(1)} %bitcast.8), channel_id=1, replica_groups=mesh['seq'=32,'chan'=16] {'seq'}, dimensions={0} | all-to-all | bytes 196608 | tf_op jit(solution)/shard_map/all_to_all | solution.py:215
  35.9 0.8 %shard_map.113 = f32[64,128]{1,0:T(8,128)S(1)} custom-call(f32[192,128]{1,0:T(8,128)S(1)} %bitcast.4, bf16[784,256]{1,0:T(8,128)(2,1)S(1)} %get-tuple-element.10.tables, f32[2,72,128]{2,1,0:T(8,128)S(1)} %get-tuple-element.11.twist), custom_call_target="tpu_custom_call" | custom-call | tf_op jit(solution)/shard_map/pallas_call | solution.py:239
  36.7 0.7 %collective-permute-start = (f32[64,128]{1,0:T(8,128)S(1)}, f32[64,128]{1,0:T(8,128)S(1)}, u32[]{:S(2)}, u32[]{:S(2)}) collective-permute-start(f32[64,128]{1,0:T(8,128)S(1)} %shard_map.113), channel_id=1, source_target_pairs={{0,0},{1,1},{2,2},{3,3},{4,4},{5,5},{6,6},{7,7},{8,8},{9,9},{10,10... | collective-permute-start | bytes 98312 | tf_op jit(solution)/shard_map/ppermute | solution.py:241
  37.4 0.9 %shard_map.112.rows = f32[192,128]{1,0:T(8,128)S(1)} custom-call(f32[192,128]{1,0:T(8,128)S(1)} %bitcast.5, bf16[784,256]{1,0:T(8,128)(2,1)S(1)} %get-tuple-element.10.tables, f32[2,72,128]{2,1,0:T(8,128)S(1)} %get-tuple-element.11.twist), custom_call_target="tpu_custom_call" | custom-call | tf_op jit(solution)/shard_map/pallas_call | solution.py:243
  38.2 0.0 collective-permute-done.lags
  38.3 25.4 %all_to_all.11 = f32[32,1,768]{2,1,0:T(1,128)S(1)} all-to-all(f32[32,1,768]{2,1,0:T(1,128)S(1)} %bitcast.6), channel_id=1, replica_groups=mesh['seq'=32,'chan'=16] {'seq'}, dimensions={0} | all-to-all | bytes 196608 | tf_op jit(solution)/shard_map/all_to_all | solution.py:215
  63.7 0.7 %shard_map.115 = (bf16[2,16,256]{2,1,0:T(8,128)(2,1)}, bf16[2,16,256]{2,1,0:T(8,128)(2,1)}, bf16[2,16,256]{2,1,0:T(8,128)(2,1)}, f32[1,256]{1,0:T(1,128)}) custom-call(f32[192,128]{1,0:T(8,128)S(1)} %bitcast.7, bf16[4,2,16,256]{3,2,1,0:T(8,128)(2,1)S(1)} %get-tuple-element.12.inputs, f32[2,16]{1,0:T(2,128)S(1)} %get-tuple-element.13.skip), custom_call_target="tpu_custom_call" | custom-call | tf_op jit(solution)/shard_map/pallas_call | solution.py:250
  (1 shorter events, 0.0 us)
Async XLA Ops:
  36.7 1.5 %collective-permute-start = (f32[64,128]{1,0:T(8,128)S(1)}, f32[64,128]{1,0:T(8,128)S(1)}, u32[]{:S(2)}, u32[]{:S(2)}) collective-permute-start(f32[64,128]{1,0:T(8,128)S(1)} %shard_map.113), channel_id=1, source_target_pairs={{0,0},{1,1},{2,2},{3,3},{4,4},{5,5},{6,6},{7,7},{8,8},{9,9},{10,10... | collective-permute-start | bytes 98312 | tf_op jit(solution)/shard_map/ppermute | solution.py:241

commit v4 on v3

--- a/solution.py
+++ b/solution.py
@@ -14,6 +14,7 @@
 VMEM = pl.BlockSpec(memory_space=pltpu.VMEM)
 HBM = pl.BlockSpec(memory_space=pltpu.HBM)
 LIMIT = 16 * 1024 * 1024
+COPIES = 2
 
 
 def split_table(table):
@@ -42,7 +43,8 @@
     last = np.zeros((side // 2, 2, rows))
     last[:, 0, :used] = (weight[:, None] * np.cos(angle)).T / side**2
     last[:, 1, :used] = (weight[:, None] * np.sin(angle)).T / side**2
-    last = last.reshape(side // 2, 2 * rows)
+    last = last.reshape(per_block, parts // COPIES, COPIES, 2 * rows)
+    last = last.transpose(2, 0, 1, 3).reshape(side // 2, 2 * rows)
     turn = 2.0 * math.pi / side**2 * (coarse[:, None] * np.arange(side)[None, :])
     twist = np.zeros((2, rows, side), np.float32)
     twist[0, :used] = np.cos(turn)
@@ -84,7 +86,6 @@
 ):
     slots, groups, length = query.shape
     per_row = length // LANES
-    pieces = 3 * per_row
     pairs = [(source, inputs.at[place]) for place, source in enumerate((query, key_in, grad_out, value))]
     pairs += [(filters, taps), (skip, gains), (tables, tables_held), (twist, twist_held)]
     copies = [pltpu.make_async_copy(*pair, sems.at[place]) for place, pair in enumerate(pairs)]
@@ -93,25 +94,33 @@
     for copy in copies[:5]:
         copy.wait()
     back = lax.rem(groups - lax.axis_index("chan"), groups)
-    taps_turned = pltpu.roll(taps[...], back, 0)
-    for slot in range(slots):
-        query_f, key_f, cotangent, value_f = [inputs[place, slot].astype(jnp.float32) for place in range(4)]
-        base = pieces * groups * slot
-        gated = pltpu.roll(query_f * key_f, back, 0)
-        signal = pltpu.roll(cotangent * value_f, back, 0)
-        for which, rows in enumerate((gated, signal, taps_turned)):
-            for part in range(per_row):
-                place = pl.ds(base + which * per_row + part, groups, stride=pieces)
+    products = []
+    for first, second in ((0, 1), (2, 3)):
+        for slot in range(slots):
+            products.append(inputs[first, slot].astype(jnp.float32) * inputs[second, slot].astype(jnp.float32))
+    pieces = (len(products) + 1) * per_row
+    for which, rows in enumerate((*products, taps[...])):
+        rows = pltpu.roll(rows, back, 0)
+        for part in range(per_row):
+            for twin in range(COPIES):
+                place = pl.ds(twin * pieces + which * per_row + part, groups, stride=COPIES * pieces)
                 sent[place, :] = rows[:, part * LANES : (part + 1) * LANES]
     for copy in copies[5:]:
         copy.wait()
 
 
 def spectral_kernel(side, parts, signals, combine, got, tables, twist, sent):
-    mix_high, mix_low, first, last_high, last_low = [tables[place] for place in table_slices(side)]
+    tables_at = table_slices(side)
+    mix_high, mix_low, first = [tables[place] for place in tables_at[:3]]
     rows = half_rows(side)
     per_row = side // 2 // parts
-    pieces = 3 * per_row
+    pieces = got.shape[0] // parts
+    count = parts // COPIES
+    mine = per_row * count
+    twin = lax.rem(lax.axis_index("seq"), COPIES)
+    last_high, last_low = [
+        tables[pl.ds(pl.multiple_of(place.start + twin * mine, mine), mine), lanes] for place, lanes in tables_at[3:]
+    ]
 
     def one(which):
         return jnp.concatenate(
@@ -127,59 +136,64 @@
         blocks = [values[place * rows : (place + 1) * rows] for place in range(len(pairs))]
         return [(block[:, :side], block[:, side:]) for block in blocks]
 
-    high, low = halves(jnp.concatenate([one(which) for which in signals], axis=1))
+    high, low = halves(jnp.concatenate([one(which) for which in range(signals)], axis=1))
     coarse = matmul(first, jnp.concatenate([high, low, high], axis=0))
-    lanes = [slice(place * side, (place + 1) * side) for place in range(len(signals))]
+    lanes = [slice(place * side, (place + 1) * side) for place in range(signals)]
     spectra = mixed([turned(coarse[:rows, lane], coarse[rows:, lane]) for lane in lanes])
     products = [turned(*pair) for pair in mixed(combine(*spectra))]
     high, low = halves(
         jnp.concatenate([jnp.concatenate(parts_of, axis=1) for parts_of in zip(*products)], axis=0)
     )
     result = matmul(last_high, high) + (matmul(last_high, low) + matmul(last_low, high))
-    spread = sent.shape[0] > side // 2
+    spread = sent.shape[0] > mine
     for which in range(len(products)):
         for part in range(per_row):
-            piece = result[part * parts : (part + 1) * parts, which * side : (which + 1) * side]
+            piece = result[part * count : (part + 1) * count, which * side : (which + 1) * side]
             if spread:
-                sent[pl.ds(which * per_row + part, parts, stride=pieces), :] = piece
+                sent[pl.ds(which * per_row + part, count, stride=pieces), :] = piece
             else:
-                sent[pl.ds(part * parts, parts), :] = piece
-
-
-def lag_product(gated, signal):
-    (gated_re, gated_im), (signal_re, signal_im) = gated, signal
-    return [(gated_re * signal_re + gated_im * signal_im, gated_im * signal_re - gated_re * signal_im)]
-
-
-def filtered(gated, signal, taps):
-    (gated_re, gated_im), (signal_re, signal_im), (taps_re, taps_im) = gated, signal, taps
-    conv = (taps_re * gated_re - taps_im * gated_im, -(taps_re * gated_im + taps_im * gated_re))
-    corr = (taps_re * signal_re + taps_im * signal_im, taps_im * signal_re - taps_re * signal_im)
-    return [conv, corr]
-
-
-def pack_kernel(parts, rows, lags, sent):
-    per_row = lags.shape[0] // parts
-    pieces = sent.shape[0] // parts
+                sent[pl.ds(part * count, count), :] = piece
+
+
+def lag_product(*spectra):
+    real = imag = 0.0
+    half = len(spectra) // 2
+    for (gated_re, gated_im), (signal_re, signal_im) in zip(spectra[:half], spectra[half:]):
+        real += gated_re * signal_re + gated_im * signal_im
+        imag += gated_im * signal_re - gated_re * signal_im
+    return [(real, imag)]
+
+
+def filtered(*spectra):
+    half = len(spectra) // 2
+    taps_re, taps_im = spectra[-1]
+    conv = [(taps_re * re - taps_im * im, -(taps_re * im + taps_im * re)) for re, im in spectra[:half]]
+    corr = [(taps_re * re + taps_im * im, taps_im * re - taps_re * im) for re, im in spectra[half:-1]]
+    return conv + corr
+
+
+def pack_kernel(count, rows, lags, sent):
+    per_row = lags.shape[0] // count
+    pieces = sent.shape[0] // count
     for part in range(per_row):
-        sent[pl.ds(2 * per_row + part, parts, stride=pieces), :] = lags[pl.ds(part * parts, parts), :]
+        sent[pl.ds(pieces - per_row + part, count, stride=pieces), :] = lags[pl.ds(part * count, count), :]
 
 
 def grads_kernel(scale, got, inputs, skip, query_grad, key_grad, value_grad, filter_grad):
     _, slots, groups, length = inputs.shape
     per_row = length // LANES
-    pieces = 3 * per_row
+    pieces = (2 * slots + 1) * per_row
     ahead = lax.axis_index("chan")
     shape = (groups, groups)
     diagonal = lax.broadcasted_iota(jnp.int32, shape, 0) == lax.broadcasted_iota(jnp.int32, shape, 1)
     for slot in range(slots):
         gains = jnp.broadcast_to(skip[slot : slot + 1, :], shape)
         gain = jnp.sum(jnp.where(diagonal, gains, 0.0), axis=1, keepdims=True)
-        base = slot * pieces * groups
         for part in range(per_row):
             lanes = slice(part * LANES, (part + 1) * LANES)
-            conv = pltpu.roll(got[pl.ds(base + part, groups, stride=pieces), :], ahead, 0)
-            corr = pltpu.roll(got[pl.ds(base + per_row + part, groups, stride=pieces), :], ahead, 0)
+            base = slot * per_row + part
+            conv = pltpu.roll(got[pl.ds(base, groups, stride=pieces), :], ahead, 0)
+            corr = pltpu.roll(got[pl.ds(base + slots * per_row, groups, stride=pieces), :], ahead, 0)
             query_f, key_f, cotangent, value_f = [
                 inputs[place, slot, :, lanes].astype(jnp.float32) for place in range(4)
             ]
@@ -189,7 +203,7 @@
             key_grad[slot, :, lanes] = (adjoint * query_f).astype(jnp.bfloat16)
             value_grad[slot, :, lanes] = (cotangent * out_field).astype(jnp.bfloat16)
     for part in range(per_row):
-        lagged = got[pl.ds(2 * per_row + part, slots * groups, stride=pieces), :]
+        lagged = got[pl.ds(2 * slots * per_row + part, groups, stride=pieces), :]
         filter_grad[:, part * LANES : (part + 1) * LANES] = scale * jnp.sum(lagged, axis=0, keepdims=True)
 
 
@@ -210,9 +224,9 @@
     return pltpu.with_memory_space_constraint(jnp.asarray(array), pltpu.HBM)
 
 
-def exchange(rows, axis, count):
+def exchange(rows, axis, count, among=None):
     blocks = rows.reshape(count, 1, rows.size // count)
-    return lax.all_to_all(blocks, axis, 0, 0, tiled=True).reshape(rows.shape)
+    return lax.all_to_all(blocks, axis, 0, 0, tiled=True, axis_index_groups=among).reshape(rows.shape)
 
 
 def local(query, key_in, value, grad_out, filters, skip):
@@ -221,7 +235,8 @@
     slots, groups, length = query.shape
     total = parts * length
     side = math.isqrt(2 * total)
-    pieces = 3 * length // LANES
+    pieces = (2 * slots + 1) * length // LANES
+    count = parts // COPIES
     packed = jax.ShapeDtypeStruct((parts * pieces, LANES), jnp.float32)
     tables, twist = fourier_tables(side, parts)
     shapes = (
@@ -234,15 +249,18 @@
         *[in_hbm(array) for array in (query, key_in, value, grad_out, filters, skip, tables, twist)]
     )
     got = exchange(sent, "seq", parts)
-    lag_rows = jax.ShapeDtypeStruct((side // 2, LANES), jnp.float32)
-    lags = functools.partial(spectral_kernel, side, parts, (0, 1), lag_product)
+    lag_rows = jax.ShapeDtypeStruct((side // 2 // COPIES, LANES), jnp.float32)
+    lags = functools.partial(spectral_kernel, side, parts, 2 * slots, lag_product)
     lags = on_device(lags, lag_rows, 3)(got, tables, twist)
-    moves = [(s * chans + k, s * chans + (s + k) % chans) for s in range(parts) for k in range(chans)]
+    moves = [
+        (s * chans + k, s * chans + (s // COPIES + k) % chans) for s in range(parts) for k in range(chans)
+    ]
     lags = lax.ppermute(lags, ("seq", "chan"), moves)
-    rows = functools.partial(spectral_kernel, side, parts, (0, 1, 2), filtered)
+    packed = jax.ShapeDtypeStruct((count * pieces, LANES), jnp.float32)
+    rows = functools.partial(spectral_kernel, side, parts, 2 * slots + 1, filtered)
     rows = on_device(rows, packed, 3)(got, tables, twist)
-    sent = on_device(functools.partial(pack_kernel, parts), packed, 2, aliases={0: 0})(rows, lags)
-    got = exchange(sent, "seq", parts)
+    sent = on_device(functools.partial(pack_kernel, count), packed, 2, aliases={0: 0})(rows, lags)
+    got = exchange(sent, "seq", count, [list(range(twin, parts, COPIES)) for twin in range(COPIES)])
     grad = jax.ShapeDtypeStruct(query.shape, jnp.bfloat16)
     row = jax.ShapeDtypeStruct((1, length), jnp.float32)
     scale = 1.0 / math.sqrt(slots * chans * total)

time: 64.7 us -> 64 us (0.989)
  blocking collectives: 59.5 us -> 57.8 us
    all_to_all x2, blocking collectives: 59.5 us -> 57.8 us  [exchange(): lax.all_to_all(blocks, axis, 0, 0, tiled=True, axis_index_groups=among)]
  transfers between devices with their start and end apart: 1 -> 1, of which waited for: 0 -> 0; matrix products, arithmetic and copies ran while one was open for 0% -> 0% of each run, Pallas kernels for 1% -> 2%
where the time goes in v4:
time: 64 us; the launch traced here: 63 us
  blocking collectives  57.8 us (90%)
  Pallas kernels  3.87 us (6%)
  starting transfers between devices  0.67 us (1%)
  between operations  0.67 us (1%)
    all_to_all x2, blocking collectives, exchange(): lax.all_to_all(blocks, axis, 0, 0, tiled=True, axis_index_groups=among)  57.8 us
  transfers between devices with their start and end apart: 1, of which 0 were waited for; matrix products, arithmetic and copies ran while one was open for 0% of the time, Pallas kernels for 2%

profile of v4, /device:TPU:24, one launch (start us, length us, event | category | flops | bytes accessed | tf_op | source)
XLA Modules:
  0.0 63.0 jit_solution(12445685298238650200)
XLA Ops:
  0.6 1.2 %shard_map.111 = (f32[320,128]{1,0:T(8,128)S(1)}, bf16[4,2,16,256]{3,2,1,0:T(8,128)(2,1)S(1)}, f32[2,16]{1,0:T(2,128)S(1)}, bf16[784,256]{1,0:T(8,128)(2,1)S(1)}, f32[2,72,128]{2,1,0:T(8,128)S(1)}) custom-call(bf16[2,16,256]{2,1,0:T(8,128)(2,1)} %query.1, bf16[2,16,256]{2,1,0:T(8,128)(2,1)} %key_in.1, bf16[2,16,256]{2,1,0:T(8,128)(2,1)} %value.1, ...), custom_call_target="tpu_custom_call" | custom-call | tf_op jit(solution)/shard_map/pallas_call | solution.py:248
  1.8 36.2 %all_to_all.10 = f32[32,1,1280]{2,1,0:T(1,128)S(1)} all-to-all(f32[32,1,1280]{2,1,0:T(1,128)S(1)} %bitcast.8), channel_id=1, replica_groups=mesh['seq'=32,'chan'=16] {'seq'}, dimensions={0} | all-to-all | bytes 327680 | tf_op jit(solution)/shard_map/all_to_all | solution.py:229
  38.0 0.9 %shard_map.113 = f32[32,128]{1,0:T(8,128)S(1)} custom-call(f32[320,128]{1,0:T(8,128)S(1)} %bitcast.4, bf16[784,256]{1,0:T(8,128)(2,1)S(1)} %get-tuple-element.10.tables, f32[2,72,128]{2,1,0:T(8,128)S(1)} %get-tuple-element.11.twist), custom_call_target="tpu_custom_call" | custom-call | tf_op jit(solution)/shard_map/pallas_call | solution.py:254
  38.9 0.7 %collective-permute-start = (f32[32,128]{1,0:T(8,128)S(1)}, f32[32,128]{1,0:T(8,128)S(1)}, u32[]{:S(2)}, u32[]{:S(2)}) collective-permute-start(f32[32,128]{1,0:T(8,128)S(1)} %shard_map.113), channel_id=1, source_target_pairs={{0,0},{1,1},{2,2},{3,3},{4,4},{5,5},{6,6},{7,7},{8,8},{9,9},{10,10... | collective-permute-start | bytes 49160 | tf_op jit(solution)/shard_map/ppermute | solution.py:258
  39.5 1.1 %shard_map.112.rows = f32[160,128]{1,0:T(8,128)S(1)} custom-call(f32[320,128]{1,0:T(8,128)S(1)} %bitcast.5, bf16[784,256]{1,0:T(8,128)(2,1)S(1)} %get-tuple-element.10.tables, f32[2,72,128]{2,1,0:T(8,128)S(1)} %get-tuple-element.11.twist), custom_call_target="tpu_custom_call" | custom-call | tf_op jit(solution)/shard_map/pallas_call | solution.py:261
  40.7 0.0 collective-permute-done.lags
  40.7 21.6 %all_to_all.11 = f32[16,1,1280]{2,1,0:T(1,128)S(1)} all-to-all(f32[16,1,1280]{2,1,0:T(1,128)S(1)} %bitcast.6), channel_id=1, replica_groups={{0,32,64,96,128,160,192,224,256,288,320,352,384,416,448,480},{16,48,80,..., dimensions={0} | all-to-all | bytes 163840 | tf_op jit(solution)/shard_map/all_to_all | solution.py:229
  62.3 0.7 %shard_map.115 = (bf16[2,16,256]{2,1,0:T(8,128)(2,1)}, bf16[2,16,256]{2,1,0:T(8,128)(2,1)}, bf16[2,16,256]{2,1,0:T(8,128)(2,1)}, f32[1,256]{1,0:T(1,128)}) custom-call(f32[160,128]{1,0:T(8,128)S(1)} %bitcast.7, bf16[4,2,16,256]{3,2,1,0:T(8,128)(2,1)S(1)} %get-tuple-element.12.inputs, f32[2,16]{1,0:T(2,128)S(1)} %get-tuple-element.13.skip), custom_call_target="tpu_custom_call" | custom-call | tf_op jit(solution)/shard_map/pallas_call | solution.py:268
  (1 shorter events, 0.0 us)
Async XLA Ops:
  38.9 1.8 %collective-permute-start = (f32[32,128]{1,0:T(8,128)S(1)}, f32[32,128]{1,0:T(8,128)S(1)}, u32[]{:S(2)}, u32[]{:S(2)}) collective-permute-start(f32[32,128]{1,0:T(8,128)S(1)} %shard_map.113), channel_id=1, source_target_pairs={{0,0},{1,1},{2,2},{3,3},{4,4},{5,5},{6,6},{7,7},{8,8},{9,9},{10,10... | collective-permute-start | bytes 49160 | tf_op jit(solution)/shard_map/ppermute | solution.py:258

commit v5 on v4

--- a/solution.py
+++ b/solution.py
@@ -46,24 +46,25 @@
     last = last.reshape(per_block, parts // COPIES, COPIES, 2 * rows)
     last = last.transpose(2, 0, 1, 3).reshape(side // 2, 2 * rows)
     turn = 2.0 * math.pi / side**2 * (coarse[:, None] * np.arange(side)[None, :])
-    twist = np.zeros((2, rows, side), np.float32)
+    twist = np.zeros((2, rows, side))
     twist[0, :used] = np.cos(turn)
     twist[1, :used] = -np.sin(turn)
     fine = 2.0 * math.pi / side * (np.arange(side)[:, None] * np.arange(side)[None, :] % side)
     fine_re, fine_im = np.cos(fine), -np.sin(fine)
-    mix = np.block([[fine_re, fine_im], [-fine_im, fine_re]])
+    fine = np.concatenate([fine_re, fine_im], axis=1)
+    twist = np.concatenate([twist[0], twist[1]], axis=1)
     first_high, first_low = split_table(first)
     first = np.concatenate([first_high, first_high, first_low], axis=1)
-    blocks = [*split_table(mix), first, *split_table(last)]
+    blocks = [*split_table(fine), first, *split_table(last), *split_table(twist)]
     wide = max(block.shape[1] for block in blocks)
-    stacked = [np.pad(block, ((0, 0), (0, wide - block.shape[1]))) for block in blocks]
-    return np.concatenate(stacked, axis=0), twist
+    stacked = [np.pad(block, ((0, -block.shape[0] % 16), (0, wide - block.shape[1]))) for block in blocks]
+    return np.concatenate(stacked, axis=0)
 
 
 def table_slices(side):
     rows = half_rows(side)
-    sizes = ((2 * side, 2 * side),) * 2 + ((2 * rows, 3 * side // 2),) + ((side // 2, 2 * rows),) * 2
-    starts = np.cumsum([0] + [size[0] for size in sizes])
+    sizes = ((side, 2 * side),) * 2 + ((2 * rows, 3 * side // 2),) + ((side // 2, 2 * rows),) * 2 + ((rows, 2 * side),) * 2
+    starts = np.cumsum([0] + [-(-size[0] // 16) * 16 for size in sizes])
     return [
         (slice(int(start), int(start) + height), slice(0, width))
         for start, (height, width) in zip(starts, sizes)
@@ -81,24 +82,25 @@
 
 
 def gate_kernel(
-    query, key_in, value, grad_out, filters, skip, tables, twist,
-    sent, inputs, gains, tables_held, twist_held, taps, sems,
+    query, key_in, value, grad_out, filters, tables,
+    sent, inputs, tables_held, taps, sems,
 ):
     slots, groups, length = query.shape
     per_row = length // LANES
     pairs = [(source, inputs.at[place]) for place, source in enumerate((query, key_in, grad_out, value))]
-    pairs += [(filters, taps), (skip, gains), (tables, tables_held), (twist, twist_held)]
+    pairs += [(filters, taps), (tables, tables_held)]
     copies = [pltpu.make_async_copy(*pair, sems.at[place]) for place, pair in enumerate(pairs)]
-    for copy in copies:
+    for copy in (copies[5], *copies[:5]):
         copy.start()
-    for copy in copies[:5]:
-        copy.wait()
     back = lax.rem(groups - lax.axis_index("chan"), groups)
     products = []
     for first, second in ((0, 1), (2, 3)):
+        copies[first].wait()
+        copies[second].wait()
         for slot in range(slots):
             products.append(inputs[first, slot].astype(jnp.float32) * inputs[second, slot].astype(jnp.float32))
     pieces = (len(products) + 1) * per_row
+    copies[4].wait()
     for which, rows in enumerate((*products, taps[...])):
         rows = pltpu.roll(rows, back, 0)
         for part in range(per_row):
@@ -109,9 +111,16 @@
         copy.wait()
 
 
-def spectral_kernel(side, parts, signals, combine, got, tables, twist, sent):
+def spectral_kernel(side, parts, signals, combine, got, tables, sent):
     tables_at = table_slices(side)
-    mix_high, mix_low, first = [tables[place] for place in tables_at[:3]]
+    fine_high, fine_low, first = [tables[place] for place in tables_at[:3]]
+    twist_high, twist_low = [tables[place].astype(jnp.float32) for place in tables_at[5:]]
+    twist = twist_high + twist_low
+    turn_re, turn_im = twist[:, :side], twist[:, side:]
+    mix_high, mix_low = [
+        jnp.concatenate([table, jnp.concatenate([-table[:, side:], table[:, :side]], axis=1)], axis=0)
+        for table in (fine_high, fine_low)
+    ]
     rows = half_rows(side)
     per_row = side // 2 // parts
     pieces = got.shape[0] // parts
@@ -119,7 +128,7 @@
     mine = per_row * count
     twin = lax.rem(lax.axis_index("seq"), COPIES)
     last_high, last_low = [
-        tables[pl.ds(pl.multiple_of(place.start + twin * mine, mine), mine), lanes] for place, lanes in tables_at[3:]
+        tables[pl.ds(pl.multiple_of(place.start + twin * mine, mine), mine), lanes] for place, lanes in tables_at[3:5]
     ]
 
     def one(which):
@@ -128,11 +137,14 @@
         )
 
     def turned(real, imag):
-        return real * twist[0] - imag * twist[1], real * twist[1] + imag * twist[0]
+        return real * turn_re - imag * turn_im, real * turn_im + imag * turn_re
 
     def mixed(pairs):
-        high, low = halves(jnp.concatenate([jnp.concatenate(pair, axis=1) for pair in pairs], axis=0))
-        values = matmul(high, mix_high) + (matmul(low, mix_high) + matmul(high, mix_low))
+        stack = jnp.concatenate([jnp.concatenate(pair, axis=1) for pair in pairs], axis=0)
+        high = stack.astype(jnp.bfloat16).astype(jnp.float32)
+        both = matmul(jnp.concatenate([high, stack - high], axis=0).astype(jnp.bfloat16), mix_high)
+        height = stack.shape[0]
+        values = both[:height] + (both[height:] + matmul(high.astype(jnp.bfloat16), mix_low))
         blocks = [values[place * rows : (place + 1) * rows] for place in range(len(pairs))]
         return [(block[:, :side], block[:, side:]) for block in blocks]
 
@@ -177,6 +189,13 @@
     pieces = sent.shape[0] // count
     for part in range(per_row):
         sent[pl.ds(pieces - per_row + part, count, stride=pieces), :] = lags[pl.ds(part * count, count), :]
+
+
+def filter_kernel(spectral, got, tables, skip, sent, gains, sem):
+    copy = pltpu.make_async_copy(skip, gains, sem)
+    copy.start()
+    spectral(got, tables, sent)
+    copy.wait()
 
 
 def grads_kernel(scale, got, inputs, skip, query_grad, key_grad, value_grad, filter_grad):
@@ -207,12 +226,12 @@
         filter_grad[:, part * LANES : (part + 1) * LANES] = scale * jnp.sum(lagged, axis=0, keepdims=True)
 
 
-def on_device(kernel, shapes, count, space=VMEM, scratch=(), aliases=None):
-    outs = jax.tree.map(lambda shape: VMEM, shapes)
+def on_device(kernel, shapes, spaces, scratch=(), aliases=None, out_space=VMEM):
+    outs = jax.tree.map(lambda shape: out_space, shapes)
     return pl.pallas_call(
         kernel,
         out_shape=shapes,
-        in_specs=[space] * count,
+        in_specs=spaces,
         out_specs=outs,
         scratch_shapes=scratch,
         input_output_aliases=aliases or {},
@@ -238,34 +257,38 @@
     pieces = (2 * slots + 1) * length // LANES
     count = parts // COPIES
     packed = jax.ShapeDtypeStruct((parts * pieces, LANES), jnp.float32)
-    tables, twist = fourier_tables(side, parts)
+    tables = fourier_tables(side, parts)
     shapes = (
         packed,
         jax.ShapeDtypeStruct((4, *query.shape), query.dtype),
-        *[jax.ShapeDtypeStruct(array.shape, array.dtype) for array in (skip, tables, twist)],
-    )
-    scratch = [pltpu.VMEM(filters.shape, jnp.float32), pltpu.SemaphoreType.DMA((8,))]
-    sent, inputs, gains, tables, twist = on_device(gate_kernel, shapes, 8, HBM, scratch)(
-        *[in_hbm(array) for array in (query, key_in, value, grad_out, filters, skip, tables, twist)]
+        jax.ShapeDtypeStruct(tables.shape, tables.dtype),
+    )
+    scratch = [pltpu.VMEM(filters.shape, jnp.float32), pltpu.SemaphoreType.DMA((6,))]
+    sent, inputs, tables = on_device(gate_kernel, shapes, [HBM] * 6, scratch)(
+        *[in_hbm(array) for array in (query, key_in, value, grad_out, filters, tables)]
     )
     got = exchange(sent, "seq", parts)
     lag_rows = jax.ShapeDtypeStruct((side // 2 // COPIES, LANES), jnp.float32)
     lags = functools.partial(spectral_kernel, side, parts, 2 * slots, lag_product)
-    lags = on_device(lags, lag_rows, 3)(got, tables, twist)
+    lags = on_device(lags, lag_rows, [VMEM] * 2)(got, tables)
     moves = [
         (s * chans + k, s * chans + (s // COPIES + k) % chans) for s in range(parts) for k in range(chans)
     ]
     lags = lax.ppermute(lags, ("seq", "chan"), moves)
     packed = jax.ShapeDtypeStruct((count * pieces, LANES), jnp.float32)
     rows = functools.partial(spectral_kernel, side, parts, 2 * slots + 1, filtered)
-    rows = on_device(rows, packed, 3)(got, tables, twist)
-    sent = on_device(functools.partial(pack_kernel, count), packed, 2, aliases={0: 0})(rows, lags)
+    held = jax.ShapeDtypeStruct(skip.shape, skip.dtype)
+    rows = functools.partial(filter_kernel, rows)
+    rows, gains = on_device(rows, (packed, held), [VMEM, VMEM, HBM], [pltpu.SemaphoreType.DMA])(
+        got, tables, in_hbm(skip)
+    )
+    sent = on_device(functools.partial(pack_kernel, count), packed, [VMEM] * 2, aliases={0: 0})(rows, lags)
     got = exchange(sent, "seq", count, [list(range(twin, parts, COPIES)) for twin in range(COPIES)])
     grad = jax.ShapeDtypeStruct(query.shape, jnp.bfloat16)
     row = jax.ShapeDtypeStruct((1, length), jnp.float32)
     scale = 1.0 / math.sqrt(slots * chans * total)
     grads = functools.partial(grads_kernel, scale)
-    return on_device(grads, (grad, grad, grad, row), 3)(got, inputs, gains)
+    return on_device(grads, (grad, grad, grad, row), [VMEM] * 3)(got, inputs, gains)
 
 
 def solution(mesh):

time: 64 us -> 63.8 us (level)
  no operation moved by 1% of the time
where the time goes in v5:
time: 63.8 us; the launch traced here: 62.8 us
  blocking collectives  57.8 us (91%)
  Pallas kernels  3.67 us (6%)
  starting transfers between devices  0.67 us (1%)
  between operations  0.67 us (1%)
    all_to_all x2, blocking collectives, exchange(): lax.all_to_all(blocks, axis, 0, 0, tiled=True, axis_index_groups=among)  57.8 us
  transfers between devices with their start and end apart: 1, of which 0 were waited for; matrix products, arithmetic and copies ran while one was open for 0% of the time, Pallas kernels for 2%

profile of v5, /device:TPU:24, one launch (start us, length us, event | category | flops | bytes accessed | tf_op | source)
XLA Modules:
  0.0 62.8 jit_solution(15055786607079862558)
XLA Ops:
  0.6 1.0 %shard_map.102 = (f32[320,128]{1,0:T(8,128)S(1)}, bf16[4,2,16,256]{3,2,1,0:T(8,128)(2,1)S(1)}, bf16[688,256]{1,0:T(8,128)(2,1)S(1)}) custom-call(bf16[2,16,256]{2,1,0:T(8,128)(2,1)} %query.1, bf16[2,16,256]{2,1,0:T(8,128)(2,1)} %key_in.1, bf16[2,16,256]{2,1,0:T(8,128)(2,1)} %value.1, bf16[2,16,256]{2,1,0:T(8,128)(2,1)} %grad_out.1, f32[16,256]{1,0:T(8,128)} %filters.1, ...), custom_call_target="tpu_custom_call" | custom-call | tf_op jit(solution)/shard_map/pallas_call | solution.py:267
  1.7 36.2 %all_to_all.10 = f32[32,1,1280]{2,1,0:T(1,128)S(1)} all-to-all(f32[32,1,1280]{2,1,0:T(1,128)S(1)} %bitcast.8), channel_id=1, replica_groups=mesh['seq'=32,'chan'=16] {'seq'}, dimensions={0} | all-to-all | bytes 327680 | tf_op jit(solution)/shard_map/all_to_all | solution.py:248
  37.9 0.8 %shard_map.104 = f32[32,128]{1,0:T(8,128)S(1)} custom-call(f32[320,128]{1,0:T(8,128)S(1)} %bitcast.4, bf16[688,256]{1,0:T(8,128)(2,1)S(1)} %get-tuple-element.10.tables), custom_call_target="tpu_custom_call" | custom-call | tf_op jit(solution)/shard_map/pallas_call | solution.py:273
  38.7 0.7 %collective-permute-start = (f32[32,128]{1,0:T(8,128)S(1)}, f32[32,128]{1,0:T(8,128)S(1)}, u32[]{:S(2)}, u32[]{:S(2)}) collective-permute-start(f32[32,128]{1,0:T(8,128)S(1)} %shard_map.104), channel_id=1, source_target_pairs={{0,0},{1,1},{2,2},{3,3},{4,4},{5,5},{6,6},{7,7},{8,8},{9,9},{10,10... | collective-permute-start | bytes 49160 | tf_op jit(solution)/shard_map/ppermute | solution.py:277
  39.4 1.1 %shard_map.103 = (f32[160,128]{1,0:T(8,128)S(1)}, f32[2,16]{1,0:T(2,128)S(1)}) custom-call(f32[320,128]{1,0:T(8,128)S(1)} %bitcast.5, bf16[688,256]{1,0:T(8,128)(2,1)S(1)} %get-tuple-element.10.tables, f32[2,16]{1,0:T(2,128)} %skip.1), custom_call_target="tpu_custom_call" | custom-call | tf_op jit(solution)/shard_map/pallas_call | solution.py:282
  40.5 0.0 collective-permute-done.lags
  40.5 21.6 %all_to_all.11 = f32[16,1,1280]{2,1,0:T(1,128)S(1)} all-to-all(f32[16,1,1280]{2,1,0:T(1,128)S(1)} %bitcast.6), channel_id=1, replica_groups={{0,32,64,96,128,160,192,224,256,288,320,352,384,416,448,480},{16,48,80,..., dimensions={0} | all-to-all | bytes 163840 | tf_op jit(solution)/shard_map/all_to_all | solution.py:248
  62.1 0.7 %shard_map.106 = (bf16[2,16,256]{2,1,0:T(8,128)(2,1)}, bf16[2,16,256]{2,1,0:T(8,128)(2,1)}, bf16[2,16,256]{2,1,0:T(8,128)(2,1)}, f32[1,256]{1,0:T(1,128)}) custom-call(f32[160,128]{1,0:T(8,128)S(1)} %bitcast.7, bf16[4,2,16,256]{3,2,1,0:T(8,128)(2,1)S(1)} %get-tuple-element.12.inputs, f32[2,16]{1,0:T(2,128)S(1)} %get-tuple-element.13.skip), custom_call_target="tpu_custom_call" | custom-call | tf_op jit(solution)/shard_map/pallas_call | solution.py:291
  (1 shorter events, 0.0 us)
Async XLA Ops:
  38.7 1.8 %collective-permute-start = (f32[32,128]{1,0:T(8,128)S(1)}, f32[32,128]{1,0:T(8,128)S(1)}, u32[]{:S(2)}, u32[]{:S(2)}) collective-permute-start(f32[32,128]{1,0:T(8,128)S(1)} %shard_map.104), channel_id=1, source_target_pairs={{0,0},{1,1},{2,2},{3,3},{4,4},{5,5},{6,6},{7,7},{8,8},{9,9},{10,10... | collective-permute-start | bytes 49160 | tf_op jit(solution)/shard_map/ppermute | solution.py:277

commit v6 on v5

--- a/solution.py
+++ b/solution.py
@@ -92,7 +92,7 @@
     copies = [pltpu.make_async_copy(*pair, sems.at[place]) for place, pair in enumerate(pairs)]
     for copy in (copies[5], *copies[:5]):
         copy.start()
-    back = lax.rem(groups - lax.axis_index("chan"), groups)
+    ahead = lax.axis_index("chan")
     products = []
     for first, second in ((0, 1), (2, 3)):
         copies[first].wait()
@@ -102,7 +102,7 @@
     pieces = (len(products) + 1) * per_row
     copies[4].wait()
     for which, rows in enumerate((*products, taps[...])):
-        rows = pltpu.roll(rows, back, 0)
+        rows = pltpu.roll(rows, ahead, 0)
         for part in range(per_row):
             for twin in range(COPIES):
                 place = pl.ds(twin * pieces + which * per_row + part, groups, stride=COPIES * pieces)
@@ -202,7 +202,7 @@
     _, slots, groups, length = inputs.shape
     per_row = length // LANES
     pieces = (2 * slots + 1) * per_row
-    ahead = lax.axis_index("chan")
+    back = lax.rem(groups - lax.axis_index("chan"), groups)
     shape = (groups, groups)
     diagonal = lax.broadcasted_iota(jnp.int32, shape, 0) == lax.broadcasted_iota(jnp.int32, shape, 1)
     for slot in range(slots):
@@ -211,8 +211,8 @@
         for part in range(per_row):
             lanes = slice(part * LANES, (part + 1) * LANES)
             base = slot * per_row + part
-            conv = pltpu.roll(got[pl.ds(base, groups, stride=pieces), :], ahead, 0)
-            corr = pltpu.roll(got[pl.ds(base + slots * per_row, groups, stride=pieces), :], ahead, 0)
+            conv = pltpu.roll(got[pl.ds(base, groups, stride=pieces), :], back, 0)
+            corr = pltpu.roll(got[pl.ds(base + slots * per_row, groups, stride=pieces), :], back, 0)
             query_f, key_f, cotangent, value_f = [
                 inputs[place, slot, :, lanes].astype(jnp.float32) for place in range(4)
             ]
@@ -272,7 +272,7 @@
     lags = functools.partial(spectral_kernel, side, parts, 2 * slots, lag_product)
     lags = on_device(lags, lag_rows, [VMEM] * 2)(got, tables)
     moves = [
-        (s * chans + k, s * chans + (s // COPIES + k) % chans) for s in range(parts) for k in range(chans)
+        (s * chans + k, s * chans + (s // COPIES - k) % chans) for s in range(parts) for k in range(chans)
     ]
     lags = lax.ppermute(lags, ("seq", "chan"), moves)
     packed = jax.ShapeDtypeStruct((count * pieces, LANES), jnp.float32)

time: 63.8 us -> 63.3 us (level)
  blocking collectives: 57.8 us -> 51.6 us
  waiting for transfers between devices: 0.01 us -> 3.74 us
  starting transfers between devices: 0.67 us -> 3.18 us
    all_to_all x2, blocking collectives: 57.8 us -> 51.6 us  [exchange(): lax.all_to_all(blocks, axis, 0, 0, tiled=True, axis_index_groups=among)]
    ppermute x1, waiting for transfers between devices: 0.01 us -> 3.74 us  [local(): lags = lax.ppermute(lags, ('seq', 'chan'), moves)]
    ppermute x1, starting transfers between devices: 0.67 us -> 3.18 us  [local(): lags = lax.ppermute(lags, ('seq', 'chan'), moves)]
  transfers between devices with their start and end apart: 1 -> 1, of which waited for: 0 -> 1; matrix products, arithmetic and copies ran while one was open for 0% -> 0% of each run, Pallas kernels for 2% -> 2%
where the time goes in v6:
time: 63.3 us; the launch traced here: 62.9 us
  blocking collectives  51.6 us (82%)
  waiting for transfers between devices  3.74 us (6%)
  Pallas kernels  3.67 us (6%)
  starting transfers between devices  3.18 us (5%)
  between operations  0.66 us (1%)
    all_to_all x2, blocking collectives, exchange(): lax.all_to_all(blocks, axis, 0, 0, tiled=True, axis_index_groups=among)  51.6 us
    ppermute x1, waiting for transfers between devices, local(): lags = lax.ppermute(lags, ('seq', 'chan'), moves)  3.74 us
    ppermute x1, starting transfers between devices, local(): lags = lax.ppermute(lags, ('seq', 'chan'), moves)  3.18 us
  transfers between devices with their start and end apart: 1, of which 1 were waited for; matrix products, arithmetic and copies ran while one was open for 0% of the time, Pallas kernels for 2%

profile of v6, /device:TPU:24, one launch (start us, length us, event | category | flops | bytes accessed | tf_op | source)
XLA Modules:
  0.0 62.9 jit_solution(1489090016575253765)
XLA Ops:
  0.6 1.0 %shard_map.102 = (f32[320,128]{1,0:T(8,128)S(1)}, bf16[4,2,16,256]{3,2,1,0:T(8,128)(2,1)S(1)}, bf16[688,256]{1,0:T(8,128)(2,1)S(1)}) custom-call(bf16[2,16,256]{2,1,0:T(8,128)(2,1)} %query.1, bf16[2,16,256]{2,1,0:T(8,128)(2,1)} %key_in.1, bf16[2,16,256]{2,1,0:T(8,128)(2,1)} %value.1, bf16[2,16,256]{2,1,0:T(8,128)(2,1)} %grad_out.1, f32[16,256]{1,0:T(8,128)} %filters.1, ...), custom_call_target="tpu_custom_call" | custom-call | tf_op jit(solution)/shard_map/pallas_call | solution.py:267
  1.7 36.2 %all_to_all.10 = f32[32,1,1280]{2,1,0:T(1,128)S(1)} all-to-all(f32[32,1,1280]{2,1,0:T(1,128)S(1)} %bitcast.8), channel_id=1, replica_groups=mesh['seq'=32,'chan'=16] {'seq'}, dimensions={0} | all-to-all | bytes 327680 | tf_op jit(solution)/shard_map/all_to_all | solution.py:248
  37.9 0.8 %shard_map.104 = f32[32,128]{1,0:T(8,128)S(1)} custom-call(f32[320,128]{1,0:T(8,128)S(1)} %bitcast.4, bf16[688,256]{1,0:T(8,128)(2,1)S(1)} %get-tuple-element.10.tables), custom_call_target="tpu_custom_call" | custom-call | tf_op jit(solution)/shard_map/pallas_call | solution.py:273
  38.7 3.2 %collective-permute-start = (f32[32,128]{1,0:T(8,128)S(1)}, f32[32,128]{1,0:T(8,128)S(1)}, u32[]{:S(2)}, u32[]{:S(2)}) collective-permute-start(f32[32,128]{1,0:T(8,128)S(1)} %shard_map.104), channel_id=1, source_target_pairs={{0,0},{1,15},{2,14},{3,13},{4,12},{5,11},{6,10},{7,9},{8,8},{9,7},... | collective-permute-start | bytes 49160 | tf_op jit(solution)/shard_map/ppermute | solution.py:277
  41.9 1.1 %shard_map.103 = (f32[160,128]{1,0:T(8,128)S(1)}, f32[2,16]{1,0:T(2,128)S(1)}) custom-call(f32[320,128]{1,0:T(8,128)S(1)} %bitcast.5, bf16[688,256]{1,0:T(8,128)(2,1)S(1)} %get-tuple-element.10.tables, f32[2,16]{1,0:T(2,128)} %skip.1), custom_call_target="tpu_custom_call" | custom-call | tf_op jit(solution)/shard_map/pallas_call | solution.py:282
  43.0 3.7 %collective-permute-done.lags = f32[32,128]{1,0:T(8,128)S(1)} collective-permute-done((f32[32,128]{1,0:T(8,128)S(1)}, f32[32,128]{1,0:T(8,128)S(1)}, u32[]{:S(2)}, u32[]{:S(2)}) %collective-permute-start) | collective-permute-done | bytes 16416 | tf_op jit(solution)/shard_map/ppermute | solution.py:277
  46.7 15.4 %all_to_all.11 = f32[16,1,1280]{2,1,0:T(1,128)S(1)} all-to-all(f32[16,1,1280]{2,1,0:T(1,128)S(1)} %bitcast.6), channel_id=1, replica_groups={{0,32,64,96,128,160,192,224,256,288,320,352,384,416,448,480},{16,48,80,..., dimensions={0} | all-to-all | bytes 163840 | tf_op jit(solution)/shard_map/all_to_all | solution.py:248
  62.2 0.7 %shard_map.106 = (bf16[2,16,256]{2,1,0:T(8,128)(2,1)}, bf16[2,16,256]{2,1,0:T(8,128)(2,1)}, bf16[2,16,256]{2,1,0:T(8,128)(2,1)}, f32[1,256]{1,0:T(1,128)}) custom-call(f32[160,128]{1,0:T(8,128)S(1)} %bitcast.7, bf16[4,2,16,256]{3,2,1,0:T(8,128)(2,1)S(1)} %get-tuple-element.12.inputs, f32[2,16]{1,0:T(2,128)S(1)} %get-tuple-element.13.skip), custom_call_target="tpu_custom_call" | custom-call | tf_op jit(solution)/shard_map/pallas_call | solution.py:291
  (1 shorter events, 0.0 us)
Async XLA Ops:
  38.7 8.0 %collective-permute-start = (f32[32,128]{1,0:T(8,128)S(1)}, f32[32,128]{1,0:T(8,128)S(1)}, u32[]{:S(2)}, u32[]{:S(2)}) collective-permute-start(f32[32,128]{1,0:T(8,128)S(1)} %shard_map.104), channel_id=1, source_target_pairs={{0,0},{1,15},{2,14},{3,13},{4,12},{5,11},{6,10},{7,9},{8,8},{9,7},... | collective-permute-start | bytes 49160 | tf_op jit(solution)/shard_map/ppermute | solution.py:277

commit v7 on v6

--- a/solution.py
+++ b/solution.py
@@ -128,7 +128,7 @@
     mine = per_row * count
     twin = lax.rem(lax.axis_index("seq"), COPIES)
     last_high, last_low = [
-        tables[pl.ds(pl.multiple_of(place.start + twin * mine, mine), mine), lanes] for place, lanes in tables_at[3:5]
+        tables[pl.ds(pl.multiple_of(place.start + twin * mine, 16), mine), lanes] for place, lanes in tables_at[3:5]
     ]
 
     def one(which):
@@ -140,23 +140,28 @@
         return real * turn_re - imag * turn_im, real * turn_im + imag * turn_re
 
     def mixed(pairs):
-        stack = jnp.concatenate([jnp.concatenate(pair, axis=1) for pair in pairs], axis=0)
-        high = stack.astype(jnp.bfloat16).astype(jnp.float32)
-        both = matmul(jnp.concatenate([high, stack - high], axis=0).astype(jnp.bfloat16), mix_high)
-        height = stack.shape[0]
-        values = both[:height] + (both[height:] + matmul(high.astype(jnp.bfloat16), mix_low))
-        blocks = [values[place * rows : (place + 1) * rows] for place in range(len(pairs))]
-        return [(block[:, :side], block[:, side:]) for block in blocks]
-
-    high, low = halves(jnp.concatenate([one(which) for which in range(signals)], axis=1))
-    coarse = matmul(first, jnp.concatenate([high, low, high], axis=0))
-    lanes = [slice(place * side, (place + 1) * side) for place in range(signals)]
-    spectra = mixed([turned(coarse[:rows, lane], coarse[rows:, lane]) for lane in lanes])
+        out = []
+        for pair in pairs:
+            stack = jnp.concatenate(pair, axis=1)
+            high = stack.astype(jnp.bfloat16).astype(jnp.float32)
+            both = matmul(jnp.concatenate([high, stack - high], axis=0).astype(jnp.bfloat16), mix_high)
+            values = both[:rows] + (both[rows:] + matmul(high.astype(jnp.bfloat16), mix_low))
+            out.append((values[:, :side], values[:, side:]))
+        return out
+
+    def coarse(which):
+        high, low = halves(one(which))
+        values = matmul(first, jnp.concatenate([high, low, high], axis=0))
+        return turned(values[:rows], values[rows:])
+
+    spectra = mixed([coarse(which) for which in range(signals)])
     products = [turned(*pair) for pair in mixed(combine(*spectra))]
     high, low = halves(
         jnp.concatenate([jnp.concatenate(parts_of, axis=1) for parts_of in zip(*products)], axis=0)
     )
-    result = matmul(last_high, high) + (matmul(last_high, low) + matmul(last_low, high))
+    tall = jnp.concatenate([last_high, last_low], axis=0)
+    both = matmul(tall, high)
+    result = both[:mine] + (both[mine:] + matmul(last_high, low))
     spread = sent.shape[0] > mine
     for which in range(len(products)):
         for part in range(per_row):

time: 63.3 us -> 63.3 us (level)
  no operation moved by 1% of the time
where the time goes in v7:
time: 63.3 us; the launch traced here: 62.8 us
  blocking collectives  51.6 us (82%)
  waiting for transfers between devices  3.88 us (6%)
  Pallas kernels  3.47 us (5%)
  starting transfers between devices  3.19 us (5%)
  between operations  0.66 us (1%)
    all_to_all x2, blocking collectives, exchange(): lax.all_to_all(blocks, axis, 0, 0, tiled=True, axis_index_groups=among)  51.6 us
    ppermute x1, waiting for transfers between devices, local(): lags = lax.ppermute(lags, ('seq', 'chan'), moves)  3.88 us
    ppermute x1, starting transfers between devices, local(): lags = lax.ppermute(lags, ('seq', 'chan'), moves)  3.19 us
  transfers between devices with their start and end apart: 1, of which 1 were waited for; matrix products, arithmetic and copies ran while one was open for 0% of the time, Pallas kernels for 2%

profile of v7, /device:TPU:24, one launch (start us, length us, event | category | flops | bytes accessed | tf_op | source)
XLA Modules:
  0.0 62.8 jit_solution(566653355682204893)
XLA Ops:
  0.6 1.0 %shard_map.102 = (f32[320,128]{1,0:T(8,128)S(1)}, bf16[4,2,16,256]{3,2,1,0:T(8,128)(2,1)S(1)}, bf16[688,256]{1,0:T(8,128)(2,1)S(1)}) custom-call(bf16[2,16,256]{2,1,0:T(8,128)(2,1)} %query.1, bf16[2,16,256]{2,1,0:T(8,128)(2,1)} %key_in.1, bf16[2,16,256]{2,1,0:T(8,128)(2,1)} %value.1, bf16[2,16,256]{2,1,0:T(8,128)(2,1)} %grad_out.1, f32[16,256]{1,0:T(8,128)} %filters.1, ...), custom_call_target="tpu_custom_call" | custom-call | tf_op jit(solution)/shard_map/pallas_call | solution.py:272
  1.7 36.2 %all_to_all.10 = f32[32,1,1280]{2,1,0:T(1,128)S(1)} all-to-all(f32[32,1,1280]{2,1,0:T(1,128)S(1)} %bitcast.8), channel_id=1, replica_groups=mesh['seq'=32,'chan'=16] {'seq'}, dimensions={0} | all-to-all | bytes 327680 | tf_op jit(solution)/shard_map/all_to_all | solution.py:253
  37.9 0.8 %shard_map.104 = f32[32,128]{1,0:T(8,128)S(1)} custom-call(f32[320,128]{1,0:T(8,128)S(1)} %bitcast.4, bf16[688,256]{1,0:T(8,128)(2,1)S(1)} %get-tuple-element.10.tables), custom_call_target="tpu_custom_call" | custom-call | tf_op jit(solution)/shard_map/pallas_call | solution.py:278
  38.6 3.2 %collective-permute-start = (f32[32,128]{1,0:T(8,128)S(1)}, f32[32,128]{1,0:T(8,128)S(1)}, u32[]{:S(2)}, u32[]{:S(2)}) collective-permute-start(f32[32,128]{1,0:T(8,128)S(1)} %shard_map.104), channel_id=1, source_target_pairs={{0,0},{1,15},{2,14},{3,13},{4,12},{5,11},{6,10},{7,9},{8,8},{9,7},... | collective-permute-start | bytes 49160 | tf_op jit(solution)/shard_map/ppermute | solution.py:282
  41.8 1.0 %shard_map.103 = (f32[160,128]{1,0:T(8,128)S(1)}, f32[2,16]{1,0:T(2,128)S(1)}) custom-call(f32[320,128]{1,0:T(8,128)S(1)} %bitcast.5, bf16[688,256]{1,0:T(8,128)(2,1)S(1)} %get-tuple-element.10.tables, f32[2,16]{1,0:T(2,128)} %skip.1), custom_call_target="tpu_custom_call" | custom-call | tf_op jit(solution)/shard_map/pallas_call | solution.py:287
  42.8 3.9 %collective-permute-done.lags = f32[32,128]{1,0:T(8,128)S(1)} collective-permute-done((f32[32,128]{1,0:T(8,128)S(1)}, f32[32,128]{1,0:T(8,128)S(1)}, u32[]{:S(2)}, u32[]{:S(2)}) %collective-permute-start) | collective-permute-done | bytes 16416 | tf_op jit(solution)/shard_map/ppermute | solution.py:282
  46.7 15.4 %all_to_all.11 = f32[16,1,1280]{2,1,0:T(1,128)S(1)} all-to-all(f32[16,1,1280]{2,1,0:T(1,128)S(1)} %bitcast.6), channel_id=1, replica_groups={{0,32,64,96,128,160,192,224,256,288,320,352,384,416,448,480},{16,48,80,..., dimensions={0} | all-to-all | bytes 163840 | tf_op jit(solution)/shard_map/all_to_all | solution.py:253
  62.1 0.7 %shard_map.106 = (bf16[2,16,256]{2,1,0:T(8,128)(2,1)}, bf16[2,16,256]{2,1,0:T(8,128)(2,1)}, bf16[2,16,256]{2,1,0:T(8,128)(2,1)}, f32[1,256]{1,0:T(1,128)}) custom-call(f32[160,128]{1,0:T(8,128)S(1)} %bitcast.7, bf16[4,2,16,256]{3,2,1,0:T(8,128)(2,1)S(1)} %get-tuple-element.12.inputs, f32[2,16]{1,0:T(2,128)S(1)} %get-tuple-element.13.skip), custom_call_target="tpu_custom_call" | custom-call | tf_op jit(solution)/shard_map/pallas_call | solution.py:296
  (1 shorter events, 0.0 us)
Async XLA Ops:
  38.6 8.0 %collective-permute-start = (f32[32,128]{1,0:T(8,128)S(1)}, f32[32,128]{1,0:T(8,128)S(1)}, u32[]{:S(2)}, u32[]{:S(2)}) collective-permute-start(f32[32,128]{1,0:T(8,128)S(1)} %shard_map.104), channel_id=1, source_target_pairs={{0,0},{1,15},{2,14},{3,13},{4,12},{5,11},{6,10},{7,9},{8,8},{9,7},... | collective-permute-start | bytes 49160 | tf_op jit(solution)/shard_map/ppermute | solution.py:282

commit v8 on v7

--- a/solution.py
+++ b/solution.py
@@ -196,23 +196,27 @@
         sent[pl.ds(pieces - per_row + part, count, stride=pieces), :] = lags[pl.ds(part * count, count), :]
 
 
-def filter_kernel(spectral, got, tables, skip, sent, gains, sem):
-    copy = pltpu.make_async_copy(skip, gains, sem)
+def filter_kernel(spectral, got, tables, skip, sent, gains, fetched, sem):
+    copy = pltpu.make_async_copy(skip, fetched, sem)
     copy.start()
     spectral(got, tables, sent)
     copy.wait()
-
-
-def grads_kernel(scale, got, inputs, skip, query_grad, key_grad, value_grad, filter_grad):
+    slots, groups, _ = gains.shape
+    shape = (groups, groups)
+    diagonal = lax.broadcasted_iota(jnp.int32, shape, 0) == lax.broadcasted_iota(jnp.int32, shape, 1)
+    for slot in range(slots):
+        spread = jnp.broadcast_to(fetched[slot : slot + 1, :], shape)
+        gain = jnp.sum(jnp.where(diagonal, spread, 0.0), axis=1, keepdims=True)
+        gains[slot] = jnp.broadcast_to(gain, gains.shape[1:])
+
+
+def grads_kernel(scale, got, inputs, gains, query_grad, key_grad, value_grad, filter_grad):
     _, slots, groups, length = inputs.shape
     per_row = length // LANES
     pieces = (2 * slots + 1) * per_row
     back = lax.rem(groups - lax.axis_index("chan"), groups)
-    shape = (groups, groups)
-    diagonal = lax.broadcasted_iota(jnp.int32, shape, 0) == lax.broadcasted_iota(jnp.int32, shape, 1)
     for slot in range(slots):
-        gains = jnp.broadcast_to(skip[slot : slot + 1, :], shape)
-        gain = jnp.sum(jnp.where(diagonal, gains, 0.0), axis=1, keepdims=True)
+        gain = gains[slot]
         for part in range(per_row):
             lanes = slice(part * LANES, (part + 1) * LANES)
             base = slot * per_row + part
@@ -282,9 +286,10 @@
     lags = lax.ppermute(lags, ("seq", "chan"), moves)
     packed = jax.ShapeDtypeStruct((count * pieces, LANES), jnp.float32)
     rows = functools.partial(spectral_kernel, side, parts, 2 * slots + 1, filtered)
-    held = jax.ShapeDtypeStruct(skip.shape, skip.dtype)
+    held = jax.ShapeDtypeStruct((*skip.shape, LANES), jnp.float32)
+    scratch = [pltpu.VMEM(skip.shape, jnp.float32), pltpu.SemaphoreType.DMA]
     rows = functools.partial(filter_kernel, rows)
-    rows, gains = on_device(rows, (packed, held), [VMEM, VMEM, HBM], [pltpu.SemaphoreType.DMA])(
+    rows, gains = on_device(rows, (packed, held), [VMEM, VMEM, HBM], scratch)(
         got, tables, in_hbm(skip)
     )
     sent = on_device(functools.partial(pack_kernel, count), packed, [VMEM] * 2, aliases={0: 0})(rows, lags)

time: 63.3 us -> 63.2 us (level)
  no operation moved by 1% of the time
where the time goes in v8:
time: 63.2 us; the launch traced here: 62.7 us
  blocking collectives  51.6 us (82%)
  waiting for transfers between devices  3.8 us (6%)
  Pallas kernels  3.48 us (6%)
  starting transfers between devices  3.19 us (5%)
  between operations  0.66 us (1%)
    all_to_all x2, blocking collectives, exchange(): lax.all_to_all(blocks, axis, 0, 0, tiled=True, axis_index_groups=among)  51.6 us
    ppermute x1, waiting for transfers between devices, local(): lags = lax.ppermute(lags, ('seq', 'chan'), moves)  3.8 us
    ppermute x1, starting transfers between devices, local(): lags = lax.ppermute(lags, ('seq', 'chan'), moves)  3.19 us
  transfers between devices with their start and end apart: 1, of which 1 were waited for; matrix products, arithmetic and copies ran while one was open for 0% of the time, Pallas kernels for 2%

profile of v8, /device:TPU:24, one launch (start us, length us, event | category | flops | bytes accessed | tf_op | source)
XLA Modules:
  0.0 62.7 jit_solution(10897266088059246550)
XLA Ops:
  0.6 1.0 %shard_map.102 = (f32[320,128]{1,0:T(8,128)S(1)}, bf16[4,2,16,256]{3,2,1,0:T(8,128)(2,1)S(1)}, bf16[688,256]{1,0:T(8,128)(2,1)S(1)}) custom-call(bf16[2,16,256]{2,1,0:T(8,128)(2,1)} %query.1, bf16[2,16,256]{2,1,0:T(8,128)(2,1)} %key_in.1, bf16[2,16,256]{2,1,0:T(8,128)(2,1)} %value.1, bf16[2,16,256]{2,1,0:T(8,128)(2,1)} %grad_out.1, f32[16,256]{1,0:T(8,128)} %filters.1, ...), custom_call_target="tpu_custom_call" | custom-call | tf_op jit(solution)/shard_map/pallas_call | solution.py:276
  1.7 36.2 %all_to_all.10 = f32[32,1,1280]{2,1,0:T(1,128)S(1)} all-to-all(f32[32,1,1280]{2,1,0:T(1,128)S(1)} %bitcast.8), channel_id=1, replica_groups=mesh['seq'=32,'chan'=16] {'seq'}, dimensions={0} | all-to-all | bytes 327680 | tf_op jit(solution)/shard_map/all_to_all | solution.py:257
  37.9 0.8 %shard_map.104 = f32[32,128]{1,0:T(8,128)S(1)} custom-call(f32[320,128]{1,0:T(8,128)S(1)} %bitcast.4, bf16[688,256]{1,0:T(8,128)(2,1)S(1)} %get-tuple-element.10.tables), custom_call_target="tpu_custom_call" | custom-call | tf_op jit(solution)/shard_map/pallas_call | solution.py:282
  38.6 3.2 %collective-permute-start = (f32[32,128]{1,0:T(8,128)S(1)}, f32[32,128]{1,0:T(8,128)S(1)}, u32[]{:S(2)}, u32[]{:S(2)}) collective-permute-start(f32[32,128]{1,0:T(8,128)S(1)} %shard_map.104), channel_id=1, source_target_pairs={{0,0},{1,15},{2,14},{3,13},{4,12},{5,11},{6,10},{7,9},{8,8},{9,7},... | collective-permute-start | bytes 49160 | tf_op jit(solution)/shard_map/ppermute | solution.py:286
  41.8 1.0 %shard_map.103 = (f32[160,128]{1,0:T(8,128)S(1)}, f32[2,16,128]{2,1,0:T(8,128)S(1)}) custom-call(f32[320,128]{1,0:T(8,128)S(1)} %bitcast.5, bf16[688,256]{1,0:T(8,128)(2,1)S(1)} %get-tuple-element.10.tables, f32[2,16]{1,0:T(2,128)} %skip.1), custom_call_target="tpu_custom_call" | custom-call | tf_op jit(solution)/shard_map/pallas_call | solution.py:292
  42.9 3.8 %collective-permute-done.lags = f32[32,128]{1,0:T(8,128)S(1)} collective-permute-done((f32[32,128]{1,0:T(8,128)S(1)}, f32[32,128]{1,0:T(8,128)S(1)}, u32[]{:S(2)}, u32[]{:S(2)}) %collective-permute-start) | collective-permute-done | bytes 16416 | tf_op jit(solution)/shard_map/ppermute | solution.py:286
  46.7 15.4 %all_to_all.11 = f32[16,1,1280]{2,1,0:T(1,128)S(1)} all-to-all(f32[16,1,1280]{2,1,0:T(1,128)S(1)} %bitcast.6), channel_id=1, replica_groups={{0,32,64,96,128,160,192,224,256,288,320,352,384,416,448,480},{16,48,80,..., dimensions={0} | all-to-all | bytes 163840 | tf_op jit(solution)/shard_map/all_to_all | solution.py:257
  62.1 0.6 %shard_map.106 = (bf16[2,16,256]{2,1,0:T(8,128)(2,1)}, bf16[2,16,256]{2,1,0:T(8,128)(2,1)}, bf16[2,16,256]{2,1,0:T(8,128)(2,1)}, f32[1,256]{1,0:T(1,128)}) custom-call(f32[160,128]{1,0:T(8,128)S(1)} %bitcast.7, bf16[4,2,16,256]{3,2,1,0:T(8,128)(2,1)S(1)} %get-tuple-element.12.inputs, f32[2,16,128]{2,1,0:T(8,128)S(1)} %get-tuple-element.13.gains), custom_call_target="tpu_custom_call" | custom-call | tf_op jit(solution)/shard_map/pallas_call | solution.py:301
  (1 shorter events, 0.0 us)
Async XLA Ops:
  38.6 8.0 %collective-permute-start = (f32[32,128]{1,0:T(8,128)S(1)}, f32[32,128]{1,0:T(8,128)S(1)}, u32[]{:S(2)}, u32[]{:S(2)}) collective-permute-start(f32[32,128]{1,0:T(8,128)S(1)} %shard_map.104), channel_id=1, source_target_pairs={{0,0},{1,15},{2,14},{3,13},{4,12},{5,11},{6,10},{7,9},{8,8},{9,7},... | collective-permute-start | bytes 49160 | tf_op jit(solution)/shard_map/ppermute | solution.py:286

commit v9 on v8

--- a/solution.py
+++ b/solution.py
@@ -55,20 +55,8 @@
     twist = np.concatenate([twist[0], twist[1]], axis=1)
     first_high, first_low = split_table(first)
     first = np.concatenate([first_high, first_high, first_low], axis=1)
-    blocks = [*split_table(fine), first, *split_table(last), *split_table(twist)]
-    wide = max(block.shape[1] for block in blocks)
-    stacked = [np.pad(block, ((0, -block.shape[0] % 16), (0, wide - block.shape[1]))) for block in blocks]
-    return np.concatenate(stacked, axis=0)
-
-
-def table_slices(side):
-    rows = half_rows(side)
-    sizes = ((side, 2 * side),) * 2 + ((2 * rows, 3 * side // 2),) + ((side // 2, 2 * rows),) * 2 + ((rows, 2 * side),) * 2
-    starts = np.cumsum([0] + [-(-size[0] // 16) * 16 for size in sizes])
-    return [
-        (slice(int(start), int(start) + height), slice(0, width))
-        for start, (height, width) in zip(starts, sizes)
-    ]
+    fine, last, twist = [np.concatenate(split_table(table), axis=0) for table in (fine, last, twist)]
+    return fine, first, last, twist
 
 
 def halves(values):
@@ -82,15 +70,15 @@
 
 
 def gate_kernel(
-    query, key_in, value, grad_out, filters, tables,
-    sent, inputs, tables_held, taps, sems,
+    query, key_in, value, grad_out, filters,
+    sent, inputs, taps, sems,
 ):
     slots, groups, length = query.shape
     per_row = length // LANES
     pairs = [(source, inputs.at[place]) for place, source in enumerate((query, key_in, grad_out, value))]
-    pairs += [(filters, taps), (tables, tables_held)]
+    pairs += [(filters, taps)]
     copies = [pltpu.make_async_copy(*pair, sems.at[place]) for place, pair in enumerate(pairs)]
-    for copy in (copies[5], *copies[:5]):
+    for copy in copies:
         copy.start()
     ahead = lax.axis_index("chan")
     products = []
@@ -107,15 +95,14 @@
             for twin in range(COPIES):
                 place = pl.ds(twin * pieces + which * per_row + part, groups, stride=COPIES * pieces)
                 sent[place, :] = rows[:, part * LANES : (part + 1) * LANES]
-    for copy in copies[5:]:
-        copy.wait()
-
-
-def spectral_kernel(side, parts, signals, combine, got, tables, sent):
-    tables_at = table_slices(side)
-    fine_high, fine_low, first = [tables[place] for place in tables_at[:3]]
-    twist_high, twist_low = [tables[place].astype(jnp.float32) for place in tables_at[5:]]
-    twist = twist_high + twist_low
+
+
+def spectral_kernel(side, parts, signals, combine, got, fine, first, last, twist, sent):
+    fine_high, fine_low = fine[:side], fine[side:]
+    first = first[...]
+    rows = half_rows(side)
+    twist = twist[...].astype(jnp.float32)
+    twist = twist[:rows] + twist[rows:]
     turn_re, turn_im = twist[:, :side], twist[:, side:]
     mix_high, mix_low = [
         jnp.concatenate([table, jnp.concatenate([-table[:, side:], table[:, :side]], axis=1)], axis=0)
@@ -127,9 +114,8 @@
     count = parts // COPIES
     mine = per_row * count
     twin = lax.rem(lax.axis_index("seq"), COPIES)
-    last_high, last_low = [
-        tables[pl.ds(pl.multiple_of(place.start + twin * mine, 16), mine), lanes] for place, lanes in tables_at[3:5]
-    ]
+    start = pl.multiple_of(twin * mine, 16)
+    last_high, last_low = last[pl.ds(start, mine), :], last[pl.ds(side // 2 + start, mine), :]
 
     def one(which):
         return jnp.concatenate(
@@ -196,10 +182,10 @@
         sent[pl.ds(pieces - per_row + part, count, stride=pieces), :] = lags[pl.ds(part * count, count), :]
 
 
-def filter_kernel(spectral, got, tables, skip, sent, gains, fetched, sem):
+def filter_kernel(spectral, got, fine, first, last, twist, skip, sent, gains, fetched, sem):
     copy = pltpu.make_async_copy(skip, fetched, sem)
     copy.start()
-    spectral(got, tables, sent)
+    spectral(got, fine, first, last, twist, sent)
     copy.wait()
     slots, groups, _ = gains.shape
     shape = (groups, groups)
@@ -270,16 +256,15 @@
     shapes = (
         packed,
         jax.ShapeDtypeStruct((4, *query.shape), query.dtype),
-        jax.ShapeDtypeStruct(tables.shape, tables.dtype),
-    )
-    scratch = [pltpu.VMEM(filters.shape, jnp.float32), pltpu.SemaphoreType.DMA((6,))]
-    sent, inputs, tables = on_device(gate_kernel, shapes, [HBM] * 6, scratch)(
-        *[in_hbm(array) for array in (query, key_in, value, grad_out, filters, tables)]
+    )
+    scratch = [pltpu.VMEM(filters.shape, jnp.float32), pltpu.SemaphoreType.DMA((5,))]
+    sent, inputs = on_device(gate_kernel, shapes, [HBM] * 5, scratch)(
+        *[in_hbm(array) for array in (query, key_in, value, grad_out, filters)]
     )
     got = exchange(sent, "seq", parts)
     lag_rows = jax.ShapeDtypeStruct((side // 2 // COPIES, LANES), jnp.float32)
     lags = functools.partial(spectral_kernel, side, parts, 2 * slots, lag_product)
-    lags = on_device(lags, lag_rows, [VMEM] * 2)(got, tables)
+    lags = on_device(lags, lag_rows, [VMEM] * 5)(got, *tables)
     moves = [
         (s * chans + k, s * chans + (s // COPIES - k) % chans) for s in range(parts) for k in range(chans)
     ]
@@ -289,8 +274,8 @@
     held = jax.ShapeDtypeStruct((*skip.shape, LANES), jnp.float32)
     scratch = [pltpu.VMEM(skip.shape, jnp.float32), pltpu.SemaphoreType.DMA]
     rows = functools.partial(filter_kernel, rows)
-    rows, gains = on_device(rows, (packed, held), [VMEM, VMEM, HBM], scratch)(
-        got, tables, in_hbm(skip)
+    rows, gains = on_device(rows, (packed, held), [*[VMEM] * 5, HBM], scratch)(
+        got, *tables, in_hbm(skip)
     )
     sent = on_device(functools.partial(pack_kernel, count), packed, [VMEM] * 2, aliases={0: 0})(rows, lags)
     got = exchange(sent, "seq", count, [list(range(twin, parts, COPIES)) for twin in range(COPIES)])

time: 63.2 us -> 63.3 us (level)
  no operation moved by 1% of the time
where the time goes in v9:
time: 63.3 us; the launch traced here: 62.8 us
  blocking collectives  51.8 us (82%)
  waiting for transfers between devices  3.8 us (6%)
  Pallas kernels  3.32 us (5%)
  starting transfers between devices  3.19 us (5%)
  between operations  0.7 us (1%)
    all_to_all x2, blocking collectives, exchange(): lax.all_to_all(blocks, axis, 0, 0, tiled=True, axis_index_groups=among)  51.8 us
    ppermute x1, waiting for transfers between devices, local(): lags = lax.ppermute(lags, ('seq', 'chan'), moves)  3.8 us
    ppermute x1, starting transfers between devices, local(): lags = lax.ppermute(lags, ('seq', 'chan'), moves)  3.19 us
  transfers between devices with their start and end apart: 1, of which 1 were waited for; matrix products, arithmetic and copies ran while one was open for 0% of the time, Pallas kernels for 2%

profile of v9, /device:TPU:24, one launch (start us, length us, event | category | flops | bytes accessed | tf_op | source)
XLA Modules:
  0.0 62.8 jit_solution(8464729553093161235)
XLA Ops:
  0.6 0.0 copy-start.3
  0.6 0.9 %shard_map.129 = (f32[320,128]{1,0:T(8,128)S(1)}, bf16[4,2,16,256]{3,2,1,0:T(8,128)(2,1)S(1)}) custom-call(bf16[2,16,256]{2,1,0:T(8,128)(2,1)} %query.1, bf16[2,16,256]{2,1,0:T(8,128)(2,1)} %key_in.1, bf16[2,16,256]{2,1,0:T(8,128)(2,1)} %value.1, bf16[2,16,256]{2,1,0:T(8,128)(2,1)} %grad_out.1, f32[16,256]{1,0:T(8,128)} %filters.1), custom_call_target="tpu_custom_call" | custom-call | tf_op jit(solution)/shard_map/pallas_call | solution.py:261
  1.5 0.0 copy-start
  1.5 0.0 copy-start.1
  1.6 0.0 copy-start.2
  1.6 36.3 %all_to_all.10 = f32[32,1,1280]{2,1,0:T(1,128)S(1)} all-to-all(f32[32,1,1280]{2,1,0:T(1,128)S(1)} %bitcast.8), channel_id=1, replica_groups=mesh['seq'=32,'chan'=16] {'seq'}, dimensions={0} | all-to-all | bytes 327680 | tf_op jit(solution)/shard_map/all_to_all | solution.py:243
  37.9 0.0 copy-done.3
  37.9 0.0 copy-done
  37.9 0.0 copy-done.1
  37.9 0.0 copy-done.2
  37.9 0.8 %shard_map.131 = f32[32,128]{1,0:T(8,128)S(1)} custom-call(f32[320,128]{1,0:T(8,128)S(1)} %bitcast.4, bf16[256,256]{1,0:T(8,128)(2,1)S(1)} %copy-done, bf16[144,192]{1,0:T(8,128)(2,1)S(1)} %copy-done.2, bf16[128,144]{1,0:T(8,128)(2,1)S(1)} %copy-done.3, bf16[144,256]{1,0:T(8,128)(2,1)S(1)} %copy-done.1), custom_call_target="tpu_custom_call" | custom-call | tf_op jit(solution)/shard_map/pallas_call | solution.py:267
  38.7 3.2 %collective-permute-start = (f32[32,128]{1,0:T(8,128)S(1)}, f32[32,128]{1,0:T(8,128)S(1)}, u32[]{:S(2)}, u32[]{:S(2)}) collective-permute-start(f32[32,128]{1,0:T(8,128)S(1)} %shard_map.131), channel_id=1, source_target_pairs={{0,0},{1,15},{2,14},{3,13},{4,12},{5,11},{6,10},{7,9},{8,8},{9,7},... | collective-permute-start | bytes 49160 | tf_op jit(solution)/shard_map/ppermute | solution.py:271
  41.9 1.0 %shard_map.130 = (f32[160,128]{1,0:T(8,128)S(1)}, f32[2,16,128]{2,1,0:T(8,128)S(1)}) custom-call(f32[320,128]{1,0:T(8,128)S(1)} %bitcast.5, bf16[256,256]{1,0:T(8,128)(2,1)S(1)} %copy-done, bf16[144,192]{1,0:T(8,128)(2,1)S(1)} %copy-done.2, bf16[128,144]{1,0:T(8,128)(2,1)S(1)} %copy-done.3, bf16[144,256]{1,0:T(8,128)(2,1)S(1)} %copy-done.1, f32[2,16]{1,0:T(2,128)} %skip.1), custom_call_target="tpu_custom_call" | custom-call | tf_op jit(solution)/shard_map/pallas_call | solution.py:277
  42.9 3.8 %collective-permute-done.lags = f32[32,128]{1,0:T(8,128)S(1)} collective-permute-done((f32[32,128]{1,0:T(8,128)S(1)}, f32[32,128]{1,0:T(8,128)S(1)}, u32[]{:S(2)}, u32[]{:S(2)}) %collective-permute-start) | collective-permute-done | bytes 16416 | tf_op jit(solution)/shard_map/ppermute | solution.py:271
  46.7 15.4 %all_to_all.11 = f32[16,1,1280]{2,1,0:T(1,128)S(1)} all-to-all(f32[16,1,1280]{2,1,0:T(1,128)S(1)} %bitcast.6), channel_id=1, replica_groups={{0,32,64,96,128,160,192,224,256,288,320,352,384,416,448,480},{16,48,80,..., dimensions={0} | all-to-all | bytes 163840 | tf_op jit(solution)/shard_map/all_to_all | solution.py:243
  62.1 0.6 %shard_map.133 = (bf16[2,16,256]{2,1,0:T(8,128)(2,1)}, bf16[2,16,256]{2,1,0:T(8,128)(2,1)}, bf16[2,16,256]{2,1,0:T(8,128)(2,1)}, f32[1,256]{1,0:T(1,128)}) custom-call(f32[160,128]{1,0:T(8,128)S(1)} %bitcast.7, bf16[4,2,16,256]{3,2,1,0:T(8,128)(2,1)S(1)} %get-tuple-element.10.inputs, f32[2,16,128]{2,1,0:T(8,128)S(1)} %get-tuple-element.11.gains), custom_call_target="tpu_custom_call" | custom-call | tf_op jit(solution)/shard_map/pallas_call | solution.py:286
  (1 shorter events, 0.0 us)
Async XLA Ops:
  0.6 37.3 %copy-start.3 = (bf16[128,144]{1,0:T(8,128)(2,1)S(1)}, bf16[128,144]{1,0:T(8,128)(2,1)}, u32[]{:S(2)}) copy-start(bf16[128,144]{1,0:T(8,128)(2,1)} %constant.10.clone.last) | copy-start | bytes 110596
  1.5 36.4 %copy-start = (bf16[256,256]{1,0:T(8,128)(2,1)S(1)}, bf16[256,256]{1,0:T(8,128)(2,1)}, u32[]{:S(2)}) copy-start(bf16[256,256]{1,0:T(8,128)(2,1)} %constant.8.clone.fine) | copy-start | bytes 393220
  1.5 36.4 %copy-start.1 = (bf16[144,256]{1,0:T(8,128)(2,1)S(1)}, bf16[144,256]{1,0:T(8,128)(2,1)}, u32[]{:S(2)}) copy-start(bf16[144,256]{1,0:T(8,128)(2,1)} %constant.11.clone.twist) | copy-start | bytes 221188
  1.6 36.3 %copy-start.2 = (bf16[144,192]{1,0:T(8,128)(2,1)S(1)}, bf16[144,192]{1,0:T(8,128)(2,1)}, u32[]{:S(2)}) copy-start(bf16[144,192]{1,0:T(8,128)(2,1)} %constant.9.clone.first) | copy-start | bytes 165892
  38.7 8.0 %collective-permute-start = (f32[32,128]{1,0:T(8,128)S(1)}, f32[32,128]{1,0:T(8,128)S(1)}, u32[]{:S(2)}, u32[]{:S(2)}) collective-permute-start(f32[32,128]{1,0:T(8,128)S(1)} %shard_map.131), channel_id=1, source_target_pairs={{0,0},{1,15},{2,14},{3,13},{4,12},{5,11},{6,10},{7,9},{8,8},{9,7},... | collective-permute-start | bytes 49160 | tf_op jit(solution)/shard_map/ppermute | solution.py:271

commit v10 on v9

--- a/solution.py
+++ b/solution.py
@@ -182,27 +182,23 @@
         sent[pl.ds(pieces - per_row + part, count, stride=pieces), :] = lags[pl.ds(part * count, count), :]
 
 
-def filter_kernel(spectral, got, fine, first, last, twist, skip, sent, gains, fetched, sem):
-    copy = pltpu.make_async_copy(skip, fetched, sem)
+def filter_kernel(spectral, got, fine, first, last, twist, skip, sent, gains, sem):
+    copy = pltpu.make_async_copy(skip, gains, sem)
     copy.start()
     spectral(got, fine, first, last, twist, sent)
     copy.wait()
-    slots, groups, _ = gains.shape
-    shape = (groups, groups)
-    diagonal = lax.broadcasted_iota(jnp.int32, shape, 0) == lax.broadcasted_iota(jnp.int32, shape, 1)
-    for slot in range(slots):
-        spread = jnp.broadcast_to(fetched[slot : slot + 1, :], shape)
-        gain = jnp.sum(jnp.where(diagonal, spread, 0.0), axis=1, keepdims=True)
-        gains[slot] = jnp.broadcast_to(gain, gains.shape[1:])
-
-
-def grads_kernel(scale, got, inputs, gains, query_grad, key_grad, value_grad, filter_grad):
+
+
+def grads_kernel(scale, got, inputs, skip, query_grad, key_grad, value_grad, filter_grad):
     _, slots, groups, length = inputs.shape
     per_row = length // LANES
     pieces = (2 * slots + 1) * per_row
     back = lax.rem(groups - lax.axis_index("chan"), groups)
+    shape = (groups, groups)
+    diagonal = lax.broadcasted_iota(jnp.int32, shape, 0) == lax.broadcasted_iota(jnp.int32, shape, 1)
     for slot in range(slots):
-        gain = gains[slot]
+        gains = jnp.broadcast_to(skip[slot : slot + 1, :], shape)
+        gain = jnp.sum(jnp.where(diagonal, gains, 0.0), axis=1, keepdims=True)
         for part in range(per_row):
             lanes = slice(part * LANES, (part + 1) * LANES)
             base = slot * per_row + part
@@ -271,10 +267,9 @@
     lags = lax.ppermute(lags, ("seq", "chan"), moves)
     packed = jax.ShapeDtypeStruct((count * pieces, LANES), jnp.float32)
     rows = functools.partial(spectral_kernel, side, parts, 2 * slots + 1, filtered)
-    held = jax.ShapeDtypeStruct((*skip.shape, LANES), jnp.float32)
-    scratch = [pltpu.VMEM(skip.shape, jnp.float32), pltpu.SemaphoreType.DMA]
+    held = jax.ShapeDtypeStruct(skip.shape, skip.dtype)
     rows = functools.partial(filter_kernel, rows)
-    rows, gains = on_device(rows, (packed, held), [*[VMEM] * 5, HBM], scratch)(
+    rows, gains = on_device(rows, (packed, held), [*[VMEM] * 5, HBM], [pltpu.SemaphoreType.DMA])(
         got, *tables, in_hbm(skip)
     )
     sent = on_device(functools.partial(pack_kernel, count), packed, [VMEM] * 2, aliases={0: 0})(rows, lags)

time: 63.3 us -> 63.3 us (level)
  no operation moved by 1% of the time
where the time goes in v10:
time: 63.3 us; the launch traced here: 62.9 us
  blocking collectives  51.8 us (82%)
  waiting for transfers between devices  3.88 us (6%)
  Pallas kernels  3.31 us (5%)
  starting transfers between devices  3.19 us (5%)
  between operations  0.7 us (1%)
    all_to_all x2, blocking collectives, exchange(): lax.all_to_all(blocks, axis, 0, 0, tiled=True, axis_index_groups=among)  51.8 us
    ppermute x1, waiting for transfers between devices, local(): lags = lax.ppermute(lags, ('seq', 'chan'), moves)  3.88 us
    ppermute x1, starting transfers between devices, local(): lags = lax.ppermute(lags, ('seq', 'chan'), moves)  3.19 us
  transfers between devices with their start and end apart: 1, of which 1 were waited for; matrix products, arithmetic and copies ran while one was open for 0% of the time, Pallas kernels for 2%

profile of v10, /device:TPU:24, one launch (start us, length us, event | category | flops | bytes accessed | tf_op | source)
XLA Modules:
  0.0 62.9 jit_solution(7593952542157362233)
XLA Ops:
  0.6 0.0 copy-start.3
  0.6 0.9 %shard_map.129 = (f32[320,128]{1,0:T(8,128)S(1)}, bf16[4,2,16,256]{3,2,1,0:T(8,128)(2,1)S(1)}) custom-call(bf16[2,16,256]{2,1,0:T(8,128)(2,1)} %query.1, bf16[2,16,256]{2,1,0:T(8,128)(2,1)} %key_in.1, bf16[2,16,256]{2,1,0:T(8,128)(2,1)} %value.1, bf16[2,16,256]{2,1,0:T(8,128)(2,1)} %grad_out.1, f32[16,256]{1,0:T(8,128)} %filters.1), custom_call_target="tpu_custom_call" | custom-call | tf_op jit(solution)/shard_map/pallas_call | solution.py:257
  1.5 0.0 copy-start
  1.5 0.0 copy-start.1
  1.6 0.0 copy-start.2
  1.6 36.3 %all_to_all.10 = f32[32,1,1280]{2,1,0:T(1,128)S(1)} all-to-all(f32[32,1,1280]{2,1,0:T(1,128)S(1)} %bitcast.8), channel_id=1, replica_groups=mesh['seq'=32,'chan'=16] {'seq'}, dimensions={0} | all-to-all | bytes 327680 | tf_op jit(solution)/shard_map/all_to_all | solution.py:239
  37.9 0.0 copy-done.3
  37.9 0.0 copy-done
  37.9 0.0 copy-done.1
  37.9 0.0 copy-done.2
  37.9 0.8 %shard_map.131 = f32[32,128]{1,0:T(8,128)S(1)} custom-call(f32[320,128]{1,0:T(8,128)S(1)} %bitcast.4, bf16[256,256]{1,0:T(8,128)(2,1)S(1)} %copy-done, bf16[144,192]{1,0:T(8,128)(2,1)S(1)} %copy-done.2, bf16[128,144]{1,0:T(8,128)(2,1)S(1)} %copy-done.3, bf16[144,256]{1,0:T(8,128)(2,1)S(1)} %copy-done.1), custom_call_target="tpu_custom_call" | custom-call | tf_op jit(solution)/shard_map/pallas_call | solution.py:263
  38.7 3.2 %collective-permute-start = (f32[32,128]{1,0:T(8,128)S(1)}, f32[32,128]{1,0:T(8,128)S(1)}, u32[]{:S(2)}, u32[]{:S(2)}) collective-permute-start(f32[32,128]{1,0:T(8,128)S(1)} %shard_map.131), channel_id=1, source_target_pairs={{0,0},{1,15},{2,14},{3,13},{4,12},{5,11},{6,10},{7,9},{8,8},{9,7},... | collective-permute-start | bytes 49160 | tf_op jit(solution)/shard_map/ppermute | solution.py:267
  41.9 1.0 %shard_map.130 = (f32[160,128]{1,0:T(8,128)S(1)}, f32[2,16]{1,0:T(2,128)S(1)}) custom-call(f32[320,128]{1,0:T(8,128)S(1)} %bitcast.5, bf16[256,256]{1,0:T(8,128)(2,1)S(1)} %copy-done, bf16[144,192]{1,0:T(8,128)(2,1)S(1)} %copy-done.2, bf16[128,144]{1,0:T(8,128)(2,1)S(1)} %copy-done.3, bf16[144,256]{1,0:T(8,128)(2,1)S(1)} %copy-done.1, f32[2,16]{1,0:T(2,128)} %skip.1), custom_call_target="tpu_custom_call" | custom-call | tf_op jit(solution)/shard_map/pallas_call | solution.py:272
  42.8 3.9 %collective-permute-done.lags = f32[32,128]{1,0:T(8,128)S(1)} collective-permute-done((f32[32,128]{1,0:T(8,128)S(1)}, f32[32,128]{1,0:T(8,128)S(1)}, u32[]{:S(2)}, u32[]{:S(2)}) %collective-permute-start) | collective-permute-done | bytes 16416 | tf_op jit(solution)/shard_map/ppermute | solution.py:267
  46.7 15.4 %all_to_all.11 = f32[16,1,1280]{2,1,0:T(1,128)S(1)} all-to-all(f32[16,1,1280]{2,1,0:T(1,128)S(1)} %bitcast.6), channel_id=1, replica_groups={{0,32,64,96,128,160,192,224,256,288,320,352,384,416,448,480},{16,48,80,..., dimensions={0} | all-to-all | bytes 163840 | tf_op jit(solution)/shard_map/all_to_all | solution.py:239
  62.1 0.7 %shard_map.133 = (bf16[2,16,256]{2,1,0:T(8,128)(2,1)}, bf16[2,16,256]{2,1,0:T(8,128)(2,1)}, bf16[2,16,256]{2,1,0:T(8,128)(2,1)}, f32[1,256]{1,0:T(1,128)}) custom-call(f32[160,128]{1,0:T(8,128)S(1)} %bitcast.7, bf16[4,2,16,256]{3,2,1,0:T(8,128)(2,1)S(1)} %get-tuple-element.10.inputs, f32[2,16]{1,0:T(2,128)S(1)} %get-tuple-element.11.skip), custom_call_target="tpu_custom_call" | custom-call | tf_op jit(solution)/shard_map/pallas_call | solution.py:281
  (1 shorter events, 0.0 us)
Async XLA Ops:
  0.6 37.3 %copy-start.3 = (bf16[128,144]{1,0:T(8,128)(2,1)S(1)}, bf16[128,144]{1,0:T(8,128)(2,1)}, u32[]{:S(2)}) copy-start(bf16[128,144]{1,0:T(8,128)(2,1)} %constant.10.clone.last) | copy-start | bytes 110596
  1.5 36.4 %copy-start = (bf16[256,256]{1,0:T(8,128)(2,1)S(1)}, bf16[256,256]{1,0:T(8,128)(2,1)}, u32[]{:S(2)}) copy-start(bf16[256,256]{1,0:T(8,128)(2,1)} %constant.8.clone.fine) | copy-start | bytes 393220
  1.5 36.4 %copy-start.1 = (bf16[144,256]{1,0:T(8,128)(2,1)S(1)}, bf16[144,256]{1,0:T(8,128)(2,1)}, u32[]{:S(2)}) copy-start(bf16[144,256]{1,0:T(8,128)(2,1)} %constant.11.clone.twist) | copy-start | bytes 221188
  1.6 36.3 %copy-start.2 = (bf16[144,192]{1,0:T(8,128)(2,1)S(1)}, bf16[144,192]{1,0:T(8,128)(2,1)}, u32[]{:S(2)}) copy-start(bf16[144,192]{1,0:T(8,128)(2,1)} %constant.9.clone.first) | copy-start | bytes 165892
  38.7 8.0 %collective-permute-start = (f32[32,128]{1,0:T(8,128)S(1)}, f32[32,128]{1,0:T(8,128)S(1)}, u32[]{:S(2)}, u32[]{:S(2)}) collective-permute-start(f32[32,128]{1,0:T(8,128)S(1)} %shard_map.131), channel_id=1, source_target_pairs={{0,0},{1,15},{2,14},{3,13},{4,12},{5,11},{6,10},{7,9},{8,8},{9,7},... | collective-permute-start | bytes 49160 | tf_op jit(solution)/shard_map/ppermute | solution.py:267

commit v11 on v7

--- a/solution.py
+++ b/solution.py
@@ -15,6 +15,15 @@
 HBM = pl.BlockSpec(memory_space=pltpu.HBM)
 LIMIT = 16 * 1024 * 1024
 COPIES = 2
+OFFSETS = (12, 4, 5, 15, 7, 11, 8, 9, 0, 1, 3, 2, 10, 6, 14, 13)
+
+
+def plane_order():
+    return sorted(range(len(OFFSETS)), key=OFFSETS.__getitem__)
+
+
+def block_order():
+    return [plane * COPIES + twin for plane in plane_order() for twin in range(COPIES)]
 
 
 def split_table(table):
@@ -31,7 +40,7 @@
     used = side // 2 + 1
     rows = half_rows(side)
     per_block = side // 2 // parts
-    order = np.arange(side // 2).reshape(parts, per_block).T.reshape(-1)
+    order = np.arange(side // 2).reshape(parts, per_block)[block_order()].T.reshape(-1)
     coarse = np.arange(used)
     angle = 2.0 * math.pi / side * (coarse[:, None] * order[None, :] % side)
     first = np.zeros((2, rows, side // 2))
@@ -81,6 +90,19 @@
     return jnp.dot(left, right, preferred_element_type=jnp.float32)
 
 
+def xor_rows(values, offset):
+    count = values.shape[0]
+    row = lax.broadcasted_iota(jnp.int32, values.shape, 0)
+    bit = 1
+    while bit < count:
+        swapped = pltpu.roll(values, bit, 0)
+        if 2 * bit < count:
+            swapped = jnp.where((row & bit) == 0, pltpu.roll(values, count - bit, 0), swapped)
+        values = jnp.where((offset & bit) == 0, values, swapped)
+        bit *= 2
+    return values
+
+
 def gate_kernel(
     query, key_in, value, grad_out, filters, tables,
     sent, inputs, tables_held, taps, sems,
@@ -92,7 +114,7 @@
     copies = [pltpu.make_async_copy(*pair, sems.at[place]) for place, pair in enumerate(pairs)]
     for copy in (copies[5], *copies[:5]):
         copy.start()
-    ahead = lax.axis_index("chan")
+    chan = lax.axis_index("chan")
     products = []
     for first, second in ((0, 1), (2, 3)):
         copies[first].wait()
@@ -102,7 +124,7 @@
     pieces = (len(products) + 1) * per_row
     copies[4].wait()
     for which, rows in enumerate((*products, taps[...])):
-        rows = pltpu.roll(rows, ahead, 0)
+        rows = xor_rows(rows, chan)
         for part in range(per_row):
             for twin in range(COPIES):
                 place = pl.ds(twin * pieces + which * per_row + part, groups, stride=COPIES * pieces)
@@ -207,7 +229,7 @@
     _, slots, groups, length = inputs.shape
     per_row = length // LANES
     pieces = (2 * slots + 1) * per_row
-    back = lax.rem(groups - lax.axis_index("chan"), groups)
+    chan = lax.axis_index("chan")
     shape = (groups, groups)
     diagonal = lax.broadcasted_iota(jnp.int32, shape, 0) == lax.broadcasted_iota(jnp.int32, shape, 1)
     for slot in range(slots):
@@ -216,8 +238,8 @@
         for part in range(per_row):
             lanes = slice(part * LANES, (part + 1) * LANES)
             base = slot * per_row + part
-            conv = pltpu.roll(got[pl.ds(base, groups, stride=pieces), :], back, 0)
-            corr = pltpu.roll(got[pl.ds(base + slots * per_row, groups, stride=pieces), :], back, 0)
+            conv = xor_rows(got[pl.ds(base, groups, stride=pieces), :], chan)
+            corr = xor_rows(got[pl.ds(base + slots * per_row, groups, stride=pieces), :], chan)
             query_f, key_f, cotangent, value_f = [
                 inputs[place, slot, :, lanes].astype(jnp.float32) for place in range(4)
             ]
@@ -272,12 +294,12 @@
     sent, inputs, tables = on_device(gate_kernel, shapes, [HBM] * 6, scratch)(
         *[in_hbm(array) for array in (query, key_in, value, grad_out, filters, tables)]
     )
-    got = exchange(sent, "seq", parts)
+    got = exchange(sent, "seq", parts, [block_order()])
     lag_rows = jax.ShapeDtypeStruct((side // 2 // COPIES, LANES), jnp.float32)
     lags = functools.partial(spectral_kernel, side, parts, 2 * slots, lag_product)
     lags = on_device(lags, lag_rows, [VMEM] * 2)(got, tables)
     moves = [
-        (s * chans + k, s * chans + (s // COPIES - k) % chans) for s in range(parts) for k in range(chans)
+        (s * chans + k, s * chans + (OFFSETS[s // COPIES] ^ k)) for s in range(parts) for k in range(chans)
     ]
     lags = lax.ppermute(lags, ("seq", "chan"), moves)
     packed = jax.ShapeDtypeStruct((count * pieces, LANES), jnp.float32)
@@ -288,7 +310,7 @@
         got, tables, in_hbm(skip)
     )
     sent = on_device(functools.partial(pack_kernel, count), packed, [VMEM] * 2, aliases={0: 0})(rows, lags)
-    got = exchange(sent, "seq", count, [list(range(twin, parts, COPIES)) for twin in range(COPIES)])
+    got = exchange(sent, "seq", count, [block_order()[twin::COPIES] for twin in range(COPIES)])
     grad = jax.ShapeDtypeStruct(query.shape, jnp.bfloat16)
     row = jax.ShapeDtypeStruct((1, length), jnp.float32)
     scale = 1.0 / math.sqrt(slots * chans * total)

time: 63.3 us -> 58.6 us (0.926)
  blocking collectives: 51.6 us -> 47.1 us
    all_to_all x2, blocking collectives: 51.6 us -> 47.1 us  [exchange(): lax.all_to_all(blocks, axis, 0, 0, tiled=True, axis_index_groups=among)]
where the time goes in v11:
time: 58.6 us; the launch traced here: 58.3 us
  blocking collectives  47.1 us (80%)
  waiting for transfers between devices  3.88 us (7%)
  Pallas kernels  3.47 us (6%)
  starting transfers between devices  3.19 us (5%)
  between operations  0.66 us (1%)
    all_to_all x2, blocking collectives, exchange(): lax.all_to_all(blocks, axis, 0, 0, tiled=True, axis_index_groups=among)  47.1 us
    ppermute x1, waiting for transfers between devices, local(): lags = lax.ppermute(lags, ('seq', 'chan'), moves)  3.88 us
    ppermute x1, starting transfers between devices, local(): lags = lax.ppermute(lags, ('seq', 'chan'), moves)  3.19 us
  transfers between devices with their start and end apart: 1, of which 1 were waited for; matrix products, arithmetic and copies ran while one was open for 0% of the time, Pallas kernels for 2%

profile of v11, /device:TPU:24, one launch (start us, length us, event | category | flops | bytes accessed | tf_op | source)
XLA Modules:
  0.0 58.3 jit_solution(9968439041404493709)
XLA Ops:
  0.6 1.0 %shard_map.102 = (f32[320,128]{1,0:T(8,128)S(1)}, bf16[4,2,16,256]{3,2,1,0:T(8,128)(2,1)S(1)}, bf16[688,256]{1,0:T(8,128)(2,1)S(1)}) custom-call(bf16[2,16,256]{2,1,0:T(8,128)(2,1)} %query.1, bf16[2,16,256]{2,1,0:T(8,128)(2,1)} %key_in.1, bf16[2,16,256]{2,1,0:T(8,128)(2,1)} %value.1, bf16[2,16,256]{2,1,0:T(8,128)(2,1)} %grad_out.1, f32[16,256]{1,0:T(8,128)} %filters.1, ...), custom_call_target="tpu_custom_call" | custom-call | tf_op jit(solution)/shard_map/pallas_call | solution.py:294
  1.7 31.4 %all_to_all.10 = f32[32,1,1280]{2,1,0:T(1,128)S(1)} all-to-all(f32[32,1,1280]{2,1,0:T(1,128)S(1)} %bitcast.8), channel_id=1, replica_groups={{256,272,288,304,352,368,320,336,32,48,64,80,416,432,128,144,192,208,22..., dimensions={0} | all-to-all | bytes 327680 | tf_op jit(solution)/shard_map/all_to_all | solution.py:275
  33.0 0.8 %shard_map.104 = f32[32,128]{1,0:T(8,128)S(1)} custom-call(f32[320,128]{1,0:T(8,128)S(1)} %bitcast.4, bf16[688,256]{1,0:T(8,128)(2,1)S(1)} %get-tuple-element.10.tables), custom_call_target="tpu_custom_call" | custom-call | tf_op jit(solution)/shard_map/pallas_call | solution.py:300
  33.8 3.2 %collective-permute-start = (f32[32,128]{1,0:T(8,128)S(1)}, f32[32,128]{1,0:T(8,128)S(1)}, u32[]{:S(2)}, u32[]{:S(2)}) collective-permute-start(f32[32,128]{1,0:T(8,128)S(1)} %shard_map.104), channel_id=1, source_target_pairs={{0,12},{1,13},{2,14},{3,15},{4,8},{5,9},{6,10},{7,11},{8,4},{9,5},... | collective-permute-start | bytes 49160 | tf_op jit(solution)/shard_map/ppermute | solution.py:304
  37.0 1.0 %shard_map.103 = (f32[160,128]{1,0:T(8,128)S(1)}, f32[2,16]{1,0:T(2,128)S(1)}) custom-call(f32[320,128]{1,0:T(8,128)S(1)} %bitcast.5, bf16[688,256]{1,0:T(8,128)(2,1)S(1)} %get-tuple-element.10.tables, f32[2,16]{1,0:T(2,128)} %skip.1), custom_call_target="tpu_custom_call" | custom-call | tf_op jit(solution)/shard_map/pallas_call | solution.py:309
  38.0 3.9 %collective-permute-done.lags = f32[32,128]{1,0:T(8,128)S(1)} collective-permute-done((f32[32,128]{1,0:T(8,128)S(1)}, f32[32,128]{1,0:T(8,128)S(1)}, u32[]{:S(2)}, u32[]{:S(2)}) %collective-permute-start) | collective-permute-done | bytes 16416 | tf_op jit(solution)/shard_map/ppermute | solution.py:304
  41.8 15.8 %all_to_all.11 = f32[16,1,1280]{2,1,0:T(1,128)S(1)} all-to-all(f32[16,1,1280]{2,1,0:T(1,128)S(1)} %bitcast.6), channel_id=1, replica_groups={{256,288,352,320,32,64,416,128,192,224,384,160,0,480,448,96},{272,304,3..., dimensions={0} | all-to-all | bytes 163840 | tf_op jit(solution)/shard_map/all_to_all | solution.py:275
  57.6 0.7 %shard_map.106 = (bf16[2,16,256]{2,1,0:T(8,128)(2,1)}, bf16[2,16,256]{2,1,0:T(8,128)(2,1)}, bf16[2,16,256]{2,1,0:T(8,128)(2,1)}, f32[1,256]{1,0:T(1,128)}) custom-call(f32[160,128]{1,0:T(8,128)S(1)} %bitcast.7, bf16[4,2,16,256]{3,2,1,0:T(8,128)(2,1)S(1)} %get-tuple-element.12.inputs, f32[2,16]{1,0:T(2,128)S(1)} %get-tuple-element.13.skip), custom_call_target="tpu_custom_call" | custom-call | tf_op jit(solution)/shard_map/pallas_call | solution.py:318
  (1 shorter events, 0.0 us)
Async XLA Ops:
  33.8 8.0 %collective-permute-start = (f32[32,128]{1,0:T(8,128)S(1)}, f32[32,128]{1,0:T(8,128)S(1)}, u32[]{:S(2)}, u32[]{:S(2)}) collective-permute-start(f32[32,128]{1,0:T(8,128)S(1)} %shard_map.104), channel_id=1, source_target_pairs={{0,12},{1,13},{2,14},{3,15},{4,8},{5,9},{6,10},{7,11},{8,4},{9,5},... | collective-permute-start | bytes 49160 | tf_op jit(solution)/shard_map/ppermute | solution.py:304

commit v12 on v11

--- a/solution.py
+++ b/solution.py
@@ -23,7 +23,7 @@
 
 
 def block_order():
-    return [plane * COPIES + twin for plane in plane_order() for twin in range(COPIES)]
+    return [plane * COPIES + twin for plane in plane_order() for twin in reversed(range(COPIES))]
 
 
 def split_table(table):
@@ -148,7 +148,7 @@
     pieces = got.shape[0] // parts
     count = parts // COPIES
     mine = per_row * count
-    twin = lax.rem(lax.axis_index("seq"), COPIES)
+    twin = COPIES - 1 - lax.rem(lax.axis_index("seq"), COPIES)
     last_high, last_low = [
         tables[pl.ds(pl.multiple_of(place.start + twin * mine, 16), mine), lanes] for place, lanes in tables_at[3:5]
     ]

time: 58.6 us -> 57 us (0.973); the launches traced: 58.3 us -> 55.9 us
  blocking collectives: 47.1 us -> 44.7 us
  waiting for transfers between devices: 3.88 us -> 3.04 us
  starting transfers between devices: 3.19 us -> 4.02 us
    all_to_all x2, blocking collectives: 47.1 us -> 44.7 us  [exchange(): lax.all_to_all(blocks, axis, 0, 0, tiled=True, axis_index_groups=among)]
    ppermute x1, waiting for transfers between devices: 3.88 us -> 3.04 us  [local(): lags = lax.ppermute(lags, ('seq', 'chan'), moves)]
    ppermute x1, starting transfers between devices: 3.19 us -> 4.02 us  [local(): lags = lax.ppermute(lags, ('seq', 'chan'), moves)]
where the time goes in v12:
time: 57 us; the launch traced here: 55.9 us
  blocking collectives  44.7 us (78%)
  starting transfers between devices  4.02 us (7%)
  Pallas kernels  3.47 us (6%)
  waiting for transfers between devices  3.04 us (5%)
  between operations  0.66 us (1%)
    all_to_all x2, blocking collectives, exchange(): lax.all_to_all(blocks, axis, 0, 0, tiled=True, axis_index_groups=among)  44.7 us
    ppermute x1, starting transfers between devices, local(): lags = lax.ppermute(lags, ('seq', 'chan'), moves)  4.02 us
    ppermute x1, waiting for transfers between devices, local(): lags = lax.ppermute(lags, ('seq', 'chan'), moves)  3.04 us
  transfers between devices with their start and end apart: 1, of which 1 were waited for; matrix products, arithmetic and copies ran while one was open for 0% of the time, Pallas kernels for 2%

profile of v12, /device:TPU:24, one launch (start us, length us, event | category | flops | bytes accessed | tf_op | source)
XLA Modules:
  0.0 55.9 jit_solution(1853186904936821566)
XLA Ops:
  0.6 1.0 %shard_map.102 = (f32[320,128]{1,0:T(8,128)S(1)}, bf16[4,2,16,256]{3,2,1,0:T(8,128)(2,1)S(1)}, bf16[688,256]{1,0:T(8,128)(2,1)S(1)}) custom-call(bf16[2,16,256]{2,1,0:T(8,128)(2,1)} %query.1, bf16[2,16,256]{2,1,0:T(8,128)(2,1)} %key_in.1, bf16[2,16,256]{2,1,0:T(8,128)(2,1)} %value.1, bf16[2,16,256]{2,1,0:T(8,128)(2,1)} %grad_out.1, f32[16,256]{1,0:T(8,128)} %filters.1, ...), custom_call_target="tpu_custom_call" | custom-call | tf_op jit(solution)/shard_map/pallas_call | solution.py:294
  1.7 29.0 %all_to_all.10 = f32[32,1,1280]{2,1,0:T(1,128)S(1)} all-to-all(f32[32,1,1280]{2,1,0:T(1,128)S(1)} %bitcast.8), channel_id=1, replica_groups={{272,256,304,288,368,352,336,320,48,32,80,64,432,416,144,128,208,192,24..., dimensions={0} | all-to-all | bytes 327680 | tf_op jit(solution)/shard_map/all_to_all | solution.py:275
  30.7 0.8 %shard_map.104 = f32[32,128]{1,0:T(8,128)S(1)} custom-call(f32[320,128]{1,0:T(8,128)S(1)} %bitcast.4, bf16[688,256]{1,0:T(8,128)(2,1)S(1)} %get-tuple-element.10.tables), custom_call_target="tpu_custom_call" | custom-call | tf_op jit(solution)/shard_map/pallas_call | solution.py:300
  31.4 4.0 %collective-permute-start = (f32[32,128]{1,0:T(8,128)S(1)}, f32[32,128]{1,0:T(8,128)S(1)}, u32[]{:S(2)}, u32[]{:S(2)}) collective-permute-start(f32[32,128]{1,0:T(8,128)S(1)} %shard_map.104), channel_id=1, source_target_pairs={{0,12},{1,13},{2,14},{3,15},{4,8},{5,9},{6,10},{7,11},{8,4},{9,5},... | collective-permute-start | bytes 49160 | tf_op jit(solution)/shard_map/ppermute | solution.py:304
  35.4 1.0 %shard_map.103 = (f32[160,128]{1,0:T(8,128)S(1)}, f32[2,16]{1,0:T(2,128)S(1)}) custom-call(f32[320,128]{1,0:T(8,128)S(1)} %bitcast.5, bf16[688,256]{1,0:T(8,128)(2,1)S(1)} %get-tuple-element.10.tables, f32[2,16]{1,0:T(2,128)} %skip.1), custom_call_target="tpu_custom_call" | custom-call | tf_op jit(solution)/shard_map/pallas_call | solution.py:309
  36.4 3.0 %collective-permute-done.lags = f32[32,128]{1,0:T(8,128)S(1)} collective-permute-done((f32[32,128]{1,0:T(8,128)S(1)}, f32[32,128]{1,0:T(8,128)S(1)}, u32[]{:S(2)}, u32[]{:S(2)}) %collective-permute-start) | collective-permute-done | bytes 16416 | tf_op jit(solution)/shard_map/ppermute | solution.py:304
  39.5 15.8 %all_to_all.11 = f32[16,1,1280]{2,1,0:T(1,128)S(1)} all-to-all(f32[16,1,1280]{2,1,0:T(1,128)S(1)} %bitcast.6), channel_id=1, replica_groups={{272,304,368,336,48,80,432,144,208,240,400,176,16,496,464,112},{256,288..., dimensions={0} | all-to-all | bytes 163840 | tf_op jit(solution)/shard_map/all_to_all | solution.py:275
  55.2 0.7 %shard_map.106 = (bf16[2,16,256]{2,1,0:T(8,128)(2,1)}, bf16[2,16,256]{2,1,0:T(8,128)(2,1)}, bf16[2,16,256]{2,1,0:T(8,128)(2,1)}, f32[1,256]{1,0:T(1,128)}) custom-call(f32[160,128]{1,0:T(8,128)S(1)} %bitcast.7, bf16[4,2,16,256]{3,2,1,0:T(8,128)(2,1)S(1)} %get-tuple-element.12.inputs, f32[2,16]{1,0:T(2,128)S(1)} %get-tuple-element.13.skip), custom_call_target="tpu_custom_call" | custom-call | tf_op jit(solution)/shard_map/pallas_call | solution.py:318
  (1 shorter events, 0.0 us)
Async XLA Ops:
  31.4 8.0 %collective-permute-start = (f32[32,128]{1,0:T(8,128)S(1)}, f32[32,128]{1,0:T(8,128)S(1)}, u32[]{:S(2)}, u32[]{:S(2)}) collective-permute-start(f32[32,128]{1,0:T(8,128)S(1)} %shard_map.104), channel_id=1, source_target_pairs={{0,12},{1,13},{2,14},{3,15},{4,8},{5,9},{6,10},{7,11},{8,4},{9,5},... | collective-permute-start | bytes 49160 | tf_op jit(solution)/shard_map/ppermute | solution.py:304

commit v13 on v12

--- a/solution.py
+++ b/solution.py
@@ -15,7 +15,7 @@
 HBM = pl.BlockSpec(memory_space=pltpu.HBM)
 LIMIT = 16 * 1024 * 1024
 COPIES = 2
-OFFSETS = (12, 4, 5, 15, 7, 11, 8, 9, 0, 1, 3, 2, 10, 6, 14, 13)
+OFFSETS = (13, 15, 14, 12, 10, 8, 6, 4, 1, 0, 2, 3, 5, 7, 9, 11)
 
 
 def plane_order():

time: 57 us -> 57 us (level)
  starting transfers between devices: 4.02 us -> 2.47 us
  waiting for transfers between devices: 3.04 us -> 4.02 us
  blocking collectives: 44.7 us -> 45.3 us
    ppermute x1, starting transfers between devices: 4.02 us -> 2.47 us  [local(): lags = lax.ppermute(lags, ('seq', 'chan'), moves)]
    ppermute x1, waiting for transfers between devices: 3.04 us -> 4.02 us  [local(): lags = lax.ppermute(lags, ('seq', 'chan'), moves)]
    all_to_all x2, blocking collectives: 44.7 us -> 45.3 us  [exchange(): lax.all_to_all(blocks, axis, 0, 0, tiled=True, axis_index_groups=among)]
where the time goes in v13:
time: 57 us; the launch traced here: 56 us
  blocking collectives  45.3 us (79%)
  waiting for transfers between devices  4.02 us (7%)
  Pallas kernels  3.48 us (6%)
  starting transfers between devices  2.47 us (4%)
  between operations  0.66 us (1%)
    all_to_all x2, blocking collectives, exchange(): lax.all_to_all(blocks, axis, 0, 0, tiled=True, axis_index_groups=among)  45.3 us
    ppermute x1, waiting for transfers between devices, local(): lags = lax.ppermute(lags, ('seq', 'chan'), moves)  4.02 us
    ppermute x1, starting transfers between devices, local(): lags = lax.ppermute(lags, ('seq', 'chan'), moves)  2.47 us
  transfers between devices with their start and end apart: 1, of which 1 were waited for; matrix products, arithmetic and copies ran while one was open for 0% of the time, Pallas kernels for 2%

profile of v13, /device:TPU:24, one launch (start us, length us, event | category | flops | bytes accessed | tf_op | source)
XLA Modules:
  0.0 56.0 jit_solution(7341880883627544205)
XLA Ops:
  0.6 1.0 %shard_map.102 = (f32[320,128]{1,0:T(8,128)S(1)}, bf16[4,2,16,256]{3,2,1,0:T(8,128)(2,1)S(1)}, bf16[688,256]{1,0:T(8,128)(2,1)S(1)}) custom-call(bf16[2,16,256]{2,1,0:T(8,128)(2,1)} %query.1, bf16[2,16,256]{2,1,0:T(8,128)(2,1)} %key_in.1, bf16[2,16,256]{2,1,0:T(8,128)(2,1)} %value.1, bf16[2,16,256]{2,1,0:T(8,128)(2,1)} %grad_out.1, f32[16,256]{1,0:T(8,128)} %filters.1, ...), custom_call_target="tpu_custom_call" | custom-call | tf_op jit(solution)/shard_map/pallas_call | solution.py:294
  1.7 29.0 %all_to_all.10 = f32[32,1,1280]{2,1,0:T(1,128)S(1)} all-to-all(f32[32,1,1280]{2,1,0:T(1,128)S(1)} %bitcast.8), channel_id=1, replica_groups={{304,288,272,256,336,320,368,352,240,224,400,384,208,192,432,416,176,16..., dimensions={0} | all-to-all | bytes 327680 | tf_op jit(solution)/shard_map/all_to_all | solution.py:275
  30.7 0.8 %shard_map.104 = f32[32,128]{1,0:T(8,128)S(1)} custom-call(f32[320,128]{1,0:T(8,128)S(1)} %bitcast.4, bf16[688,256]{1,0:T(8,128)(2,1)S(1)} %get-tuple-element.10.tables), custom_call_target="tpu_custom_call" | custom-call | tf_op jit(solution)/shard_map/pallas_call | solution.py:300
  31.4 2.5 %collective-permute-start = (f32[32,128]{1,0:T(8,128)S(1)}, f32[32,128]{1,0:T(8,128)S(1)}, u32[]{:S(2)}, u32[]{:S(2)}) collective-permute-start(f32[32,128]{1,0:T(8,128)S(1)} %shard_map.104), channel_id=1, source_target_pairs={{0,13},{1,12},{2,15},{3,14},{4,9},{5,8},{6,11},{7,10},{8,5},{9,4},... | collective-permute-start | bytes 49160 | tf_op jit(solution)/shard_map/ppermute | solution.py:304
  33.9 1.0 %shard_map.103 = (f32[160,128]{1,0:T(8,128)S(1)}, f32[2,16]{1,0:T(2,128)S(1)}) custom-call(f32[320,128]{1,0:T(8,128)S(1)} %bitcast.5, bf16[688,256]{1,0:T(8,128)(2,1)S(1)} %get-tuple-element.10.tables, f32[2,16]{1,0:T(2,128)} %skip.1), custom_call_target="tpu_custom_call" | custom-call | tf_op jit(solution)/shard_map/pallas_call | solution.py:309
  34.9 4.0 %collective-permute-done.lags = f32[32,128]{1,0:T(8,128)S(1)} collective-permute-done((f32[32,128]{1,0:T(8,128)S(1)}, f32[32,128]{1,0:T(8,128)S(1)}, u32[]{:S(2)}, u32[]{:S(2)}) %collective-permute-start) | collective-permute-done | bytes 16416 | tf_op jit(solution)/shard_map/ppermute | solution.py:304
  38.9 16.3 %all_to_all.11 = f32[16,1,1280]{2,1,0:T(1,128)S(1)} all-to-all(f32[16,1,1280]{2,1,0:T(1,128)S(1)} %bitcast.6), channel_id=1, replica_groups={{304,272,336,368,240,400,208,432,176,464,144,496,112,16,80,48},{288,256..., dimensions={0} | all-to-all | bytes 163840 | tf_op jit(solution)/shard_map/all_to_all | solution.py:275
  55.3 0.7 %shard_map.106 = (bf16[2,16,256]{2,1,0:T(8,128)(2,1)}, bf16[2,16,256]{2,1,0:T(8,128)(2,1)}, bf16[2,16,256]{2,1,0:T(8,128)(2,1)}, f32[1,256]{1,0:T(1,128)}) custom-call(f32[160,128]{1,0:T(8,128)S(1)} %bitcast.7, bf16[4,2,16,256]{3,2,1,0:T(8,128)(2,1)S(1)} %get-tuple-element.12.inputs, f32[2,16]{1,0:T(2,128)S(1)} %get-tuple-element.13.skip), custom_call_target="tpu_custom_call" | custom-call | tf_op jit(solution)/shard_map/pallas_call | solution.py:318
  (1 shorter events, 0.0 us)
Async XLA Ops:
  31.4 7.5 %collective-permute-start = (f32[32,128]{1,0:T(8,128)S(1)}, f32[32,128]{1,0:T(8,128)S(1)}, u32[]{:S(2)}, u32[]{:S(2)}) collective-permute-start(f32[32,128]{1,0:T(8,128)S(1)} %shard_map.104), channel_id=1, source_target_pairs={{0,13},{1,12},{2,15},{3,14},{4,9},{5,8},{6,11},{7,10},{8,5},{9,4},... | collective-permute-start | bytes 49160 | tf_op jit(solution)/shard_map/ppermute | solution.py:304
